TPU v7x, 512 devices: a whole 4x4x16 slice. The times are simulated.
512 devices in a mesh: rows: 2 (over y_lo), hidden: 8 (over y_hi, x), latents: 32 (over z, core).
Axes of the slice: x: 4, y: 4 (y_hi: 2, y_lo: 2; y = y_hi * 2 + y_lo), z: 16, core: 2. Of those that a mesh axis runs over, the one named last changes fastest.
Arguments:
- inputs: bfloat16 [256, 3584], P('rows', ('hidden', 'latents')), may hold values from -6 to 6
- gate_weight: bfloat16 [3584, 14336], P(None, ('hidden', 'latents')), may hold values from -0.09375 to 0.09375
- up_weight: bfloat16 [3584, 14336], P(None, ('hidden', 'latents')), may hold values from -0.09375 to 0.09375
- down_weight: bfloat16 [14336, 3584], P(('hidden', 'latents')), may hold values from -0.046875 to 0.046875
- encoder: bfloat16 [3584, 65536], P('hidden', ('rows', 'latents')), may hold values from -0.09375 to 0.09375
- decoder: bfloat16 [65536, 3584], P(('rows', 'latents'), 'hidden'), may hold values from -0.09375 to 0.09375
- enc_bias: float32 [65536], P(('rows', 'latents')), may hold values from -3 to 3
- dec_bias: float32 [3584], P('hidden'), may hold values from -3 to 3
- shuffle_order: int32 [256], replicated, may hold values from 0 to 255, each once
Outputs:
- recon_out: bfloat16 [256, 3584], P(('rows', 'latents'), 'hidden')
- grad_enc: bfloat16 [3584, 65536], P('hidden', ('rows', 'latents'))
- grad_dec: bfloat16 [65536, 3584], P(('rows', 'latents'), 'hidden')
Inputs may be any that keep to these rules, and one draw needn't show every extreme that they name: shuffle_order names every token index 0 to 255 exactly once.
All inputs are finite; a program needn't handle non-finite values.
Results may differ from a plain program's by a relative error of at most 0.038.
Values may be sent and summed in bfloat16 or wider, within the bound.
No kernel may reach another device: no remote copies, remote signals or barrier semaphores. Data moves between devices by JAX's collectives and lax.ppermute only.
A program may use at most 64 MiB of HBM per device.

v0:
```python
import math

import jax
import jax.numpy as jnp
from jax import lax
from jax.sharding import Mesh
from jax.sharding import PartitionSpec as P

HIDDEN_LATENTS = ("hidden_0", "hidden_1", "latents_0", "latents_1")
HIDDEN = ("hidden_0", "hidden_1")
LATENTS = ("latents_0", "latents_1")
ROWS_LATENTS = ("rows", "latents_0", "latents_1")


smooth_scale = 0.1
sparsity_weight = 0.5


def sent_to_all(x, axis):
    copies = jnp.broadcast_to(x, (lax.axis_size(axis), *x.shape))
    return lax.all_to_all(copies, axis, split_axis=0, concat_axis=0, tiled=True)


def laid_out(blocks, dim):
    blocks = jnp.moveaxis(blocks, 0, dim)
    lengths = blocks.shape
    return blocks.reshape(*lengths[:dim], lengths[dim] * lengths[dim + 1], *lengths[dim + 2 :])


def whole_of(x, axes, dim):
    far, near = axes
    blocks = sent_to_all(sent_to_all(x, far), near)
    return laid_out(blocks.swapaxes(0, 1).reshape(-1, *x.shape), dim)


def collect(x, axis, dim):
    return laid_out(sent_to_all(x, axis), dim)


def rows_for(lines, peers):
    spare = -len(lines) % peers
    return jnp.pad(lines, [(0, spare)] + [(0, 0)] * (lines.ndim - 1))


def cut_along(x, dim, peers):
    lengths = x.shape
    blocks = x.reshape(*lengths[:dim], peers, lengths[dim] // peers, *lengths[dim + 1 :])
    return jnp.moveaxis(blocks, dim, 0)


def sent_and_summed(x, axis, dim):
    peers = lax.axis_size(axis)
    blocks = lax.all_to_all(cut_along(x, dim, peers), axis, 0, 0, tiled=True)
    return jnp.sum(blocks.astype(jnp.float32), axis=0)


def nested_sum(x, axes):
    lines = x.reshape(-1, x.shape[-1])
    padded = rows_for(lines, lax.axis_size(axes))
    whole = collect(sent_and_summed(padded, axes, 0).astype(jnp.bfloat16), axes, 0)
    return lax.slice_in_dim(whole, 0, len(lines)).reshape(x.shape).astype(jnp.float32)


def taken_together(x, axis):
    everything = sent_to_all(x, axis)
    return jnp.sum(everything.astype(jnp.float32), axis=0)


def summed_on_arrival(x, axis, dim):
    peers = lax.axis_size(axis)
    blocks = lax.all_to_all(cut_along(x, dim, peers), axis, 0, 0, tiled=True)
    return jnp.sum(blocks, axis=0)


def sum_in_two_steps(x, axes, dim):
    far, near = axes
    own = summed_on_arrival(cut_along(x, dim, lax.axis_size(far)), near, dim + 1)
    return jnp.sum(lax.all_to_all(own, far, 0, 0, tiled=True), axis=0)


def sum_by_parts(x, axes):
    lines = x.reshape(-1, x.shape[-1])
    own = sum_in_two_steps(
        rows_for(lines, lax.axis_size(axes[0]) * lax.axis_size(axes[1])), axes, 0
    )
    whole = whole_of(own, axes, 0)
    return whole[: len(lines)].reshape(x.shape)


def shards(
    inputs, gate_weight, up_weight, down_weight, encoder, decoder, enc_bias, dec_bias, shuffle_order
):
    gathered = whole_of(inputs, (("hidden_0", "hidden_1"), ("latents_0", "latents_1")), 1)
    gate_act = jnp.dot(gathered, gate_weight, preferred_element_type=jnp.float32)
    up_act = jnp.dot(gathered, up_weight, preferred_element_type=jnp.float32)
    hidden = (jax.nn.gelu(gate_act, approximate=True) * up_act).astype(jnp.bfloat16)
    units = collect(hidden, HIDDEN, 1)
    block_rows = lax.all_to_all(down_weight, HIDDEN, split_axis=1, concat_axis=0, tiled=True)
    block_part = jnp.dot(units, block_rows, preferred_element_type=jnp.float32)
    width_rows = nested_sum(block_part.astype(jnp.bfloat16), LATENTS).astype(jnp.bfloat16)
    every_row = collect(width_rows, "rows", 0)
    shuffled = jnp.take(every_row, shuffle_order, axis=0)
    pre_local = jnp.dot(shuffled, encoder, preferred_element_type=jnp.float32)
    pre_act = (
        taken_together(pre_local.astype(jnp.bfloat16), HIDDEN).astype(jnp.float32)
        + enc_bias[None, :]
    )
    latent_act = (smooth_scale * jax.nn.softplus(pre_act / smooth_scale)).astype(jnp.bfloat16)
    recon_local = jnp.dot(latent_act, decoder, preferred_element_type=jnp.float32)
    recon = sum_by_parts(recon_local, (("rows", "latents_0"), "latents_1")) + dec_bias[None, :]
    recon_full = recon.astype(jnp.bfloat16)
    scale = 1.0 / math.sqrt(shuffle_order.shape[0])
    d_err = (scale * (recon - shuffled.astype(jnp.float32))).astype(jnp.bfloat16)
    back_local = lax.dot_general(
        d_err, decoder, (((1,), (1,)), ((), ())), preferred_element_type=jnp.float32
    )
    grad_dec = lax.dot_general(
        latent_act, d_err, (((0,), (0,)), ((), ())), preferred_element_type=jnp.float32
    ).astype(jnp.bfloat16)
    d_latent = taken_together(back_local.astype(jnp.bfloat16), HIDDEN).astype(jnp.float32)
    d_pre = ((d_latent + sparsity_weight * scale) * jax.nn.sigmoid(pre_act / smooth_scale)).astype(
        jnp.bfloat16
    )
    grad_enc = lax.dot_general(
        shuffled, d_pre, (((0,), (0,)), ((), ())), preferred_element_type=jnp.float32
    ).astype(jnp.bfloat16)
    row_count = recon_full.shape[0] // lax.axis_size(ROWS_LATENTS)
    first_row = lax.axis_index(ROWS_LATENTS) * row_count
    recon_out = lax.dynamic_slice_in_dim(recon_full, first_row, row_count, 0)
    return (recon_out, grad_enc, grad_dec)


def solution(mesh):
    finer = Mesh(
        mesh.devices.reshape(mesh.shape["rows"], 2, 4, 16, 2),
        ("rows", "hidden_0", "hidden_1", "latents_0", "latents_1"),
    )
    return jax.shard_map(
        shards,
        mesh=finer,
        in_specs=(
            P("rows", HIDDEN_LATENTS),
            P(None, HIDDEN_LATENTS),
            P(None, HIDDEN_LATENTS),
            P(HIDDEN_LATENTS, None),
            P(HIDDEN, ROWS_LATENTS),
            P(ROWS_LATENTS, HIDDEN),
            P(ROWS_LATENTS),
            P(HIDDEN),
            P(),
        ),
        out_specs=(P(ROWS_LATENTS, HIDDEN), P(HIDDEN, ROWS_LATENTS), P(ROWS_LATENTS, HIDDEN)),
        check_vma=False,
    )
```

profile of v0, /device:TPU:6, one launch (start us, length us, event | category | flops | bytes accessed | tf_op | source)
XLA Modules:
  0.0 351.8 jit_solution(13278466627374858800)
XLA Ops:
  0.6 0.0 copy-start
  0.6 0.8 broadcast_in_dim.42
  1.4 13.9 %all_to_all.76 = bf16[8,128,14]{1,2,0:T(8,128)(2,1)S(1)} all-to-all(bf16[8,128,14]{1,2,0:T(8,128)(2,1)S(1)} %broadcast_in_dim.42), channel_id=1, replica_groups=mesh['rows'=2,'hidden_0'=2,'hidden_1'=4,'latents_0'=16,'latents_1'=2] {'..., dimensions={0} | all-to-all | bytes 57344 | tf_op jit(solution)/shard_map/all_to_all | solution.py:21
  15.4 1.0 broadcast_in_dim.43
  16.4 14.5 %all-to-all-start.1 = ((bf16[32,8,128,14]{2,1,3,0:T(8,128)(2,1)}), bf16[32,8,128,14]{2,1,3,0:T(8,128)(2,1)S(1)}, u32[]{:S(2)}, u32[]{:S(2)}) async-start(bf16[32,8,128,14]{2,1,3,0:T(8,128)(2,1)} %broadcast_in_dim.43), calls=%async_computation.1 | async-start | bytes 1835008 | tf_op jit(solution)/shard_map/all_to_all | solution.py:21
  30.9 1.5 all_to_all.51
  32.4 0.9 copy.40
  33.4 48.0 %all-to-all-done.1 = bf16[32,8,128,14]{2,1,3,0:T(8,128)(2,1)S(1)} async-done(((bf16[32,8,128,14]{2,1,3,0:T(8,128)(2,1)}), bf16[32,8,128,14]{2,1,3,0:T(8,128)(2,1)S(1)}, u32[]{:S(2)}, u32[]{:S(2)}) %all-to-all-start.1) | async-done | bytes 917536 | tf_op jit(solution)/shard_map/all_to_all | solution.py:21
  81.4 5.4 %all-to-all-start.3 = ((bf16[56,8,448]{2,0,1:T(8,128)(2,1)}), bf16[56,8,448]{2,0,1:T(8,128)(2,1)S(1)}, u32[]{:S(2)}, u32[]{:S(2)}) async-start(bf16[56,8,448]{2,0,1:T(8,128)(2,1)} %copy.40), calls=%async_computation.3 | async-start | bytes 917504 | tf_op jit(solution)/shard_map/all_to_all | solution.py:98
  86.8 0.2 copy.38
  87.0 0.0 copy-start.2
  87.0 0.6 copy.39
  87.6 0.3 reshape.33
  87.9 1.3 fusion.19
  89.2 0.0 copy-start.3
  89.2 1.4 fusion.1
  90.5 5.2 %all-to-all-done.3 = bf16[56,8,448]{2,0,1:T(8,128)(2,1)S(1)} async-done(((bf16[56,8,448]{2,0,1:T(8,128)(2,1)}), bf16[56,8,448]{2,0,1:T(8,128)(2,1)S(1)}, u32[]{:S(2)}, u32[]{:S(2)}) %all-to-all-start.3) | async-done | bytes 401440 | tf_op jit(solution)/shard_map/all_to_all | solution.py:98
  95.8 10.9 %all_to_all.77 = bf16[8,128,56]{1,2,0:T(8,128)(2,1)S(1)} all-to-all(bf16[8,128,56]{1,2,0:T(8,128)(2,1)S(1)} %broadcast_in_dim.44), channel_id=1, replica_groups=mesh['rows'=2,'hidden_0'=2,'hidden_1'=4,'latents_0'=16,'latents_1'=2] {'..., dimensions={0} | all-to-all | bytes 229376 | tf_op jit(solution)/shard_map/all_to_all | solution.py:21
  106.7 0.3 fusion
  107.1 0.1 copy.41
  107.3 20.2 %all_to_all.78 = bf16[32,4,448]{2,1,0:T(4,128)(2,1)S(1)} all-to-all(bf16[32,4,448]{2,1,0:T(4,128)(2,1)S(1)} %reshape.34), channel_id=1, replica_groups=mesh['rows'=2,'hidden_0'=2,'hidden_1'=4,'latents_0'=16,'latents_1'=2] {'..., dimensions={0} | all-to-all | bytes 229376 | tf_op jit(solution)/shard_map/all_to_all | solution.py:53
  127.4 0.1 reduce_sum.48
  127.5 0.7 broadcast_in_dim.45
  128.2 3.9 %all-to-all-start.5 = ((bf16[32,4,448]{2,1,0:T(4,128)(2,1)}), bf16[32,4,448]{2,1,0:T(4,128)(2,1)S(1)}, u32[]{:S(2)}, u32[]{:S(2)}) async-start(bf16[32,4,448]{2,1,0:T(4,128)(2,1)} %broadcast_in_dim.45), calls=%async_computation.5 | async-start | bytes 262144 | tf_op jit(solution)/shard_map/all_to_all | solution.py:21
  132.1 0.0 copy-done.2
  132.1 17.2 %all-to-all-done.5 = bf16[32,4,448]{2,1,0:T(4,128)(2,1)S(1)} async-done(((bf16[32,4,448]{2,1,0:T(4,128)(2,1)}), bf16[32,4,448]{2,1,0:T(4,128)(2,1)S(1)}, u32[]{:S(2)}, u32[]{:S(2)}) %all-to-all-start.5) | async-done | bytes 114720 | tf_op jit(solution)/shard_map/all_to_all | solution.py:21
  149.2 0.1 reshape.35
  149.3 0.1 copy.42
  149.4 0.7 broadcast_in_dim.46
  150.1 3.4 all-to-all-start.6
  153.6 5.0 %all-to-all-done.6 = bf16[2,128,448]{1,2,0:T(8,128)(2,1)S(1)} async-done(((bf16[2,128,448]{1,2,0:T(8,128)(2,1)}), bf16[2,128,448]{1,2,0:T(8,128)(2,1)S(1)}, u32[]{:S(2)}, u32[]{:S(2)}) %all-to-all-start.6) | async-done | bytes 229408 | tf_op jit(solution)/shard_map/all_to_all | solution.py:21
  158.6 0.1 copy.43
  158.7 1.2 gather_fusion
  159.9 0.0 copy-done.3
  159.9 0.5 convolution_convert_fusion.3
  160.4 0.5 broadcast_in_dim.49
  160.9 51.7 %all_to_all.79 = bf16[8,256,1024]{2,1,0:T(8,128)(2,1)S(1)} all-to-all(bf16[8,256,1024]{2,1,0:T(8,128)(2,1)S(1)} %broadcast_in_dim.49), channel_id=1, replica_groups=mesh['rows'=2,'hidden_0'=2,'hidden_1'=4,'latents_0'=16,'latents_1'=2] {'..., dimensions={0} | all-to-all | bytes 8388608 | tf_op jit(solution)/shard_map/all_to_all | solution.py:21
  212.6 0.0 copy-start.4
  212.6 0.8 convert_reduce_fusion.1
  213.4 0.0 copy-done
  213.4 0.0 copy-done.4
  213.4 0.8 fusion.17
  214.3 0.2 reshape_reshape.6
  214.5 0.0 copy-start.1
  214.5 4.2 %all_to_all.80 = f32[2,32,4,448]{3,2,1,0:T(4,128)S(1)} all-to-all(f32[2,32,4,448]{3,2,1,0:T(4,128)S(1)} %copy.45), channel_id=1, replica_groups=mesh['rows'=2,'hidden_0'=2,'hidden_1'=4,'latents_0'=16,'latents_1'=2] {'..., dimensions={0} | all-to-all | bytes 917504 | tf_op jit(solution)/shard_map/all_to_all | solution.py:71
  218.7 0.2 reduce_sum.50
  218.9 26.6 %all_to_all.81 = f32[32,4,448]{2,1,0:T(4,128)S(1)} all-to-all(f32[32,4,448]{2,1,0:T(4,128)S(1)} %reduce_sum.50), channel_id=1, replica_groups=mesh['rows'=2,'hidden_0'=2,'hidden_1'=4,'latents_0'=16,'latents_1'=2] {'..., dimensions={0} | all-to-all | bytes 458752 | tf_op jit(solution)/shard_map/all_to_all | solution.py:78
  245.4 0.1 reduce_sum.51
  245.5 25.0 %all_to_all.82 = f32[32,4,448]{2,1,0:T(4,128)S(1)} all-to-all(f32[32,4,448]{2,1,0:T(4,128)S(1)} %broadcast_in_dim.50), channel_id=1, replica_groups=mesh['rows'=2,'hidden_0'=2,'hidden_1'=4,'latents_0'=16,'latents_1'=2] {'..., dimensions={0} | all-to-all | bytes 458752 | tf_op jit(solution)/shard_map/all_to_all | solution.py:21
  270.6 0.1 broadcast_in_dim.51
  270.6 4.2 %all_to_all.83 = f32[2,32,4,448]{3,2,1,0:T(4,128)S(1)} all-to-all(f32[2,32,4,448]{3,2,1,0:T(4,128)S(1)} %broadcast_in_dim.51), channel_id=1, replica_groups=mesh['rows'=2,'hidden_0'=2,'hidden_1'=4,'latents_0'=16,'latents_1'=2] {'..., dimensions={0} | all-to-all | bytes 917504 | tf_op jit(solution)/shard_map/all_to_all | solution.py:21
  274.8 0.2 reshape_reshape.7
  275.0 0.0 copy-done.1
  275.1 0.2 multiply_convert_fusion.1
  275.2 0.4 convolution_convert_fusion.2
  275.7 2.5 broadcast_in_dim.52
  278.2 6.4 %all-to-all-start.12 = ((bf16[8,256,1024]{2,1,0:T(8,128)(2,1)}), bf16[8,256,1024]{2,1,0:T(8,128)(2,1)}, u32[]{:S(2)}, u32[]{:S(2)}) async-start(bf16[8,256,1024]{2,1,0:T(8,128)(2,1)} %broadcast_in_dim.52), calls=%async_computation.12 | async-start | bytes 8388608 | tf_op jit(solution)/shard_map/all_to_all | solution.py:21
  284.6 0.6 dynamic-slice_convert_fusion
  285.2 1.9 convolution_convert_fusion
  287.1 59.9 %all-to-all-done.12 = bf16[8,256,1024]{2,1,0:T(8,128)(2,1)} async-done(((bf16[8,256,1024]{2,1,0:T(8,128)(2,1)}), bf16[8,256,1024]{2,1,0:T(8,128)(2,1)}, u32[]{:S(2)}, u32[]{:S(2)}) %all-to-all-start.12) | async-done | bytes 4194336 | tf_op jit(solution)/shard_map/all_to_all | solution.py:21
  347.1 3.2 convert_reduce_fusion
  350.2 1.6 convolution_convert_fusion.1
  (9 shorter events, 0.2 us)
Async XLA Ops:
  0.6 212.8 %copy-start = (bf16[1024,448]{0,1:T(8,128)(2,1)S(1)}, bf16[1024,448]{0,1:T(8,128)(2,1)}, u32[]{:S(2)}) copy-start(bf16[1024,448]{0,1:T(8,128)(2,1)} %param.14) | copy-start | bytes 2752516
  16.4 64.9 %all-to-all-start.1 = ((bf16[32,8,128,14]{2,1,3,0:T(8,128)(2,1)}), bf16[32,8,128,14]{2,1,3,0:T(8,128)(2,1)S(1)}, u32[]{:S(2)}, u32[]{:S(2)}) async-start(bf16[32,8,128,14]{2,1,3,0:T(8,128)(2,1)} %broadcast_in_dim.43), calls=%async_computation.1 | async-start | bytes 1835008 | tf_op jit(solution)/shard_map/all_to_all | solution.py:21
  81.4 14.4 %all-to-all-start.3 = ((bf16[56,8,448]{2,0,1:T(8,128)(2,1)}), bf16[56,8,448]{2,0,1:T(8,128)(2,1)S(1)}, u32[]{:S(2)}, u32[]{:S(2)}) async-start(bf16[56,8,448]{2,0,1:T(8,128)(2,1)} %copy.40), calls=%async_computation.3 | async-start | bytes 917504 | tf_op jit(solution)/shard_map/all_to_all | solution.py:98
  87.0 45.0 %copy-start.2 = (s32[256]{0:T(256)S(1)}, s32[256]{0:T(256)}, u32[]{:S(2)}) copy-start(s32[256]{0:T(256)} %param.17) | copy-start | bytes 3076
  89.2 70.7 %copy-start.3 = (bf16[448,1024]{1,0:T(8,128)(2,1)S(1)}, bf16[448,1024]{1,0:T(8,128)(2,1)}, u32[]{:S(2)}) copy-start(bf16[448,1024]{1,0:T(8,128)(2,1)} %param.13) | copy-start | bytes 2752516
  128.2 21.0 %all-to-all-start.5 = ((bf16[32,4,448]{2,1,0:T(4,128)(2,1)}), bf16[32,4,448]{2,1,0:T(4,128)(2,1)S(1)}, u32[]{:S(2)}, u32[]{:S(2)}) async-start(bf16[32,4,448]{2,1,0:T(4,128)(2,1)} %broadcast_in_dim.45), calls=%async_computation.5 | async-start | bytes 262144 | tf_op jit(solution)/shard_map/all_to_all | solution.py:21
  150.1 8.4 %all-to-all-start.6 = ((bf16[2,128,448]{1,2,0:T(8,128)(2,1)}), bf16[2,128,448]{1,2,0:T(8,128)(2,1)S(1)}, u32[]{:S(2)}, u32[]{:S(2)}) async-start(bf16[2,128,448]{1,2,0:T(8,128)(2,1)} %broadcast_in_dim.46), calls=%async_computation.6 | async-start | bytes 458752 | tf_op jit(solution)/shard_map/all_to_all | solution.py:21
  212.6 0.9 copy-start.4
  214.5 60.6 %copy-start.1 = (f32[448]{0:T(512)S(1)}, f32[448]{0:T(512)}, u32[]{:S(2)}) copy-start(f32[448]{0:T(512)} %param.16) | copy-start | bytes 5380
  278.2 68.9 %all-to-all-start.12 = ((bf16[8,256,1024]{2,1,0:T(8,128)(2,1)}), bf16[8,256,1024]{2,1,0:T(8,128)(2,1)}, u32[]{:S(2)}, u32[]{:S(2)}) async-start(bf16[8,256,1024]{2,1,0:T(8,128)(2,1)} %broadcast_in_dim.52), calls=%async_computation.12 | async-start | bytes 8388608 | tf_op jit(solution)/shard_map/all_to_all | solution.py:21
where the time goes:
time: 353 us; the launch traced here: 352 us
  blocking collectives  157 us (44%)
  waiting for transfers between devices  135 us (38%)
  starting transfers between devices  33.6 us (10%)
  local copies, waits for them, and re-layouts  12.7 us (4%)
  matrix products  8.26 us (2%)
  other arithmetic  4.5 us (1%)
    all_to_all x4, waiting for transfers between devices, sent_to_all(): return lax.all_to_all(copies, axis, split_axis=0, concat_axis=0, tiled=True)  130 us
    all_to_all x5, blocking collectives, sent_to_all(): return lax.all_to_all(copies, axis, split_axis=0, concat_axis=0, tiled=True)  106 us
    all_to_all x4, starting transfers between devices, sent_to_all(): return lax.all_to_all(copies, axis, split_axis=0, concat_axis=0, tiled=True)  28.2 us
    all_to_all x1, blocking collectives, sum_in_two_steps(): return jnp.sum(lax.all_to_all(own, far, 0, 0, tiled=True), axis=0)  26.6 us
    all_to_all x1, blocking collectives, sent_and_summed(): blocks = lax.all_to_all(cut_along(x, dim, peers), axis, 0, 0, tiled=True)  20.2 us
  transfers between devices with their start and end apart: 5, of which 5 were waited for; matrix products, arithmetic and copies ran while one was open for 2% of the time, Pallas kernels for 0%

commit v1 on v0

v1 whole, which is shorter than its diff:
```python
import math

import jax
import jax.numpy as jnp
from jax import lax
from jax.sharding import Mesh
from jax.sharding import PartitionSpec as P

R, Y, X, Z, C = "rows", "hidden_0", "hidden_1", "latents_0", "latents_1"
HIDDEN = (Y, X)
LATENTS = (Z, C)
HIDDEN_LATENTS = (Y, X, Z, C)
ROWS_LATENTS = (R, Z, C)
ROWS_Z = (R, Z)

smooth_scale = 0.1
sparsity_weight = 0.5
F32 = jnp.float32
BF16 = jnp.bfloat16


def exchange(blocks, axes):
    return lax.all_to_all(blocks, axes, 0, 0, tiled=True)


def sent_to_all(x, axes):
    return exchange(jnp.broadcast_to(x, (lax.axis_size(axes), *x.shape)), axes)


def both_cores(x):
    return lax.all_gather(x, C, axis=0, tiled=False)


def total(blocks):
    return jnp.sum(blocks.astype(F32), axis=0)


def own(x, index, dim):
    return lax.dynamic_index_in_dim(x, index, dim, keepdims=False)


def shards(
    inputs, gate_weight, up_weight, down_weight, encoder, decoder, enc_bias, dec_bias, shuffle_order
):
    tokens = shuffle_order.shape[0]
    n_hidden = lax.axis_size(HIDDEN)
    n_z = lax.axis_size(Z)
    n_rows_z = lax.axis_size(ROWS_Z)
    core = lax.axis_index(C)
    width = decoder.shape[1]
    half = width // 2
    latents = encoder.shape[1]
    units = gate_weight.shape[1]

    few = sent_to_all(inputs.T, Z)
    more = sent_to_all(few, HIDDEN)
    every = both_cores(more)
    gathered = every.transpose(1, 2, 0, 3, 4).reshape(-1, inputs.shape[0])
    both_weights = jnp.concatenate([gate_weight, up_weight], axis=1)
    acts = lax.dot_general(
        both_weights, gathered, (((0,), (0,)), ((), ())), preferred_element_type=F32
    )
    hidden = (jax.nn.gelu(acts[:units], approximate=True) * acts[units:]).astype(BF16)
    part = lax.dot_general(
        down_weight, hidden, (((0,), (0,)), ((), ())), preferred_element_type=F32
    ).astype(BF16)

    pair = total(both_cores(part)).reshape(n_hidden, 2, half, -1)
    mine = own(pair, core, 1).astype(BF16)
    summed = total(exchange(mine, HIDDEN)).T.astype(BF16)
    rows_own = total(exchange(summed.reshape(n_z, -1, half), Z)).astype(BF16)
    mlp_out = both_cores(sent_to_all(rows_own, ROWS_Z).reshape(tokens, half))

    order = shuffle_order.reshape(n_rows_z, 2, -1).transpose(1, 0, 2).reshape(-1)
    pick = (order[:, None] == jnp.arange(tokens)[None, :]).astype(BF16)
    shuffled = jnp.concatenate(
        [jnp.dot(pick, mlp_out[c], preferred_element_type=F32).astype(BF16) for c in range(2)],
        axis=1,
    )
    pre_local = jnp.dot(shuffled, encoder, preferred_element_type=F32).astype(BF16)
    pre_act = total(exchange(pre_local.reshape(n_hidden, -1, latents), HIDDEN)) + enc_bias[None, :]
    latent_own = (smooth_scale * jax.nn.softplus(pre_act / smooth_scale)).astype(BF16)
    latent_act = sent_to_all(latent_own, HIDDEN).reshape(tokens, latents)
    recon_local = jnp.dot(latent_act, decoder, preferred_element_type=F32)
    recon_pair = jnp.sum(both_cores(recon_local), axis=0)
    recon_mine = own(recon_pair.reshape(2, n_rows_z, -1, width), core, 0).astype(BF16)
    recon = total(exchange(recon_mine, ROWS_Z)) + dec_bias[None, :]
    recon_out = recon.astype(BF16)

    scale = 1.0 / math.sqrt(tokens)
    count = recon.shape[0]
    first = (core * n_rows_z + lax.axis_index(ROWS_Z)) * count
    target = lax.dynamic_slice_in_dim(shuffled, first, count, 0)
    err_own = (scale * (recon - target.astype(F32))).astype(BF16)
    d_err = both_cores(sent_to_all(err_own, ROWS_Z).reshape(-1, width)).reshape(tokens, width)

    back_local = lax.dot_general(
        d_err, decoder, (((1,), (1,)), ((), ())), preferred_element_type=F32
    ).astype(BF16)
    d_latent = total(exchange(back_local.reshape(n_hidden, -1, latents), HIDDEN))
    grad_dec = lax.dot_general(
        latent_act, d_err, (((0,), (0,)), ((), ())), preferred_element_type=F32
    ).astype(BF16)
    d_pre_own = (
        (d_latent + sparsity_weight * scale) * jax.nn.sigmoid(pre_act / smooth_scale)
    ).astype(BF16)
    d_pre = sent_to_all(d_pre_own, HIDDEN).reshape(tokens, latents)
    grad_enc = lax.dot_general(
        shuffled, d_pre, (((0,), (0,)), ((), ())), preferred_element_type=F32
    ).astype(BF16)
    return (recon_out, grad_enc, grad_dec)


def solution(mesh):
    finer = Mesh(
        mesh.devices.reshape(mesh.shape["rows"], 2, 4, 16, 2),
        (R, Y, X, Z, C),
    )
    return jax.shard_map(
        shards,
        mesh=finer,
        in_specs=(
            P(R, HIDDEN_LATENTS),
            P(None, HIDDEN_LATENTS),
            P(None, HIDDEN_LATENTS),
            P(HIDDEN_LATENTS, None),
            P(HIDDEN, ROWS_LATENTS),
            P(ROWS_LATENTS, HIDDEN),
            P(ROWS_LATENTS),
            P(HIDDEN),
            P(),
        ),
        out_specs=(P(ROWS_LATENTS, HIDDEN), P(HIDDEN, ROWS_LATENTS), P(ROWS_LATENTS, HIDDEN)),
        check_vma=False,
    )
```

time: 353 us -> 266 us (0.75)
  waiting for transfers between devices: 135 us -> 51.2 us
  starting transfers between devices: 33.6 us -> 13.3 us
  between operations: 0.9 us -> 14.4 us
  other arithmetic: 4.5 us -> 8.75 us
    all_to_all x5 -> x3, waiting for transfers between devices: 135 us -> 40.8 us  [exchange(): return lax.all_to_all(blocks, axes, 0, 0, tiled=True)]
    all_to_all x5 -> x3, starting transfers between devices: 33.6 us -> 13.3 us  [exchange(): return lax.all_to_all(blocks, axes, 0, 0, tiled=True)]
    all_gather x0 -> x1, waiting for transfers between devices: none -> 10.4 us  [both_cores(): return lax.all_gather(x, C, axis=0, tiled=False)]
    all_to_all x8, blocking collectives: 157 us -> 146 us  [exchange(): return lax.all_to_all(blocks, axes, 0, 0, tiled=True)]
    all_gather x0 -> x4, blocking collectives: none -> 9.03 us  [both_cores(): return lax.all_gather(x, C, axis=0, tiled=False)]
    convert_element_type x2 -> x4, local copies, waits for them, and re-layouts: 0.71 us -> 6.64 us  [the longest x1 5.79 us: total(): return jnp.sum(blocks.astype(F32), axis=0)]
    broadcast_in_dim x9 -> x6, local copies, waits for them, and re-layouts: 6.37 us -> 2.44 us  [sent_to_all(): return exchange(jnp.broadcast_to(x, (lax.axis_size(axes), *x.shape)), axes)]
    reduce_sum x5 -> x7, other arithmetic: 4.32 us -> 8 us  [the longest x6 6.81 us: total(): return jnp.sum(blocks.astype(F32), axis=0)]
  transfers between devices with their start and end apart: 5 -> 4, of which waited for: 5 -> 4; matrix products, arithmetic and copies ran while one was open for 2% -> 1% of each run, Pallas kernels for 0% -> 0%
where the time goes in v1:
time: 266 us; the launch traced here: 262 us
  blocking collectives  155 us (58%)
  waiting for transfers between devices  51.2 us (19%)
  between operations  14.4 us (5%)
  starting transfers between devices  13.3 us (5%)
  local copies, waits for them, and re-layouts  11.6 us (4%)
  other arithmetic  8.75 us (3%)
  matrix products  7.49 us (3%)
    all_to_all x8, blocking collectives, exchange(): return lax.all_to_all(blocks, axes, 0, 0, tiled=True)  146 us
    all_to_all x3, waiting for transfers between devices, exchange(): return lax.all_to_all(blocks, axes, 0, 0, tiled=True)  40.8 us
    all_to_all x3, starting transfers between devices, exchange(): return lax.all_to_all(blocks, axes, 0, 0, tiled=True)  13.3 us
    all_gather x1, waiting for transfers between devices, both_cores(): return lax.all_gather(x, C, axis=0, tiled=False)  10.4 us
    all_gather x4, blocking collectives, both_cores(): return lax.all_gather(x, C, axis=0, tiled=False)  9.03 us
    reduce_sum x6, other arithmetic, total(): return jnp.sum(blocks.astype(F32), axis=0)  6.81 us
    convert_element_type x1, local copies, waits for them, and re-layouts, total(): return jnp.sum(blocks.astype(F32), axis=0)  5.79 us
  transfers between devices with their start and end apart: 4, of which 4 were waited for; matrix products, arithmetic and copies ran while one was open for 1% of the time, Pallas kernels for 0%

profile of v1, /device:TPU:6, one launch (start us, length us, event | category | flops | bytes accessed | tf_op | source)
XLA Modules:
  0.0 262.3 jit_solution(6662293688486701225)
XLA Ops:
  7.2 0.0 copy-start
  7.2 0.0 all-gather.5.cloned.1.call-start
  7.2 0.8 broadcast_in_dim.21
  8.0 27.7 %all_to_all.55 = bf16[16,14,128]{2,1,0:T(8,128)(2,1)S(1)} all-to-all(bf16[16,14,128]{2,1,0:T(8,128)(2,1)S(1)} %broadcast_in_dim.21), channel_id=1, replica_groups=mesh['rows'=2,'hidden_0'=2,'hidden_1'=4,'latents_0'=16,'latents_1'=2] {'..., dimensions={0} | all-to-all | bytes 114688 | tf_op jit(solution)/shard_map/all_to_all | solution.py:23
  35.7 0.1 broadcast_in_dim.22
  35.8 15.0 %all_to_all.56 = bf16[8,16,14,128]{3,1,2,0:T(8,128)(2,1)S(1)} all-to-all(bf16[8,16,14,128]{3,1,2,0:T(8,128)(2,1)S(1)} %broadcast_in_dim.22), channel_id=1, replica_groups=mesh['rows'=2,'hidden_0'=2,'hidden_1'=4,'latents_0'=16,'latents_1'=2] {'..., dimensions={0} | all-to-all | bytes 917504 | tf_op jit(solution)/shard_map/all_to_all | solution.py:23
  50.8 2.5 all-gather
  53.3 0.3 copy.60
  53.5 0.0 copy-start.3
  53.6 0.3 reshape.42
  53.8 1.5 fusion.1
  55.3 1.4 fusion
  56.7 0.0 all-gather.5.cloned.1.call-update
  56.7 10.4 %all-gather.5.cloned.1.call-done = bf16[7168,128]{0,1:T(8,128)(2,1)} async-done(((bf16[3584,128]{0,1:T(8,128)(2,1)}), bf16[7168,128]{0,1:T(8,128)(2,1)}) %all-gather.5.cloned.1.call-update) | async-done | bytes 1835024 | tf_op jit(solution)/shard_map/all_gather | solution.py:31
  67.2 5.8 %reshape.54 = f32[2,3584,128]{1,0,2:T(2,128)} reshape(bf16[7168,128]{0,1:T(8,128)(2,1)} %all-gather.5.cloned.1.call-done) | data formatting | bytes 5505024 | tf_op jit(solution)/shard_map/convert_element_type | solution.py:35
  72.9 6.5 %reduce_sum.69 = bf16[3584,128]{0,1:T(8,128)(2,1)S(1)} reduce(f32[2,3584,128]{1,0,2:T(2,128)} %reshape.54, f32[]{:T(128)} %constant.15.clone.1), dimensions={0}, to_apply=%region_0.0 | reduce | flops 458752 | bytes 4587524 | tf_op jit(solution)/shard_map/reduce_sum | solution.py:35
  79.4 0.6 copy.61
  80.1 0.0 copy-start.6
  80.1 16.5 %all_to_all.57 = bf16[8,224,128]{2,1,0:T(8,128)(2,1)S(1)} all-to-all(bf16[8,224,128]{2,1,0:T(8,128)(2,1)S(1)} %fusion.5), channel_id=1, replica_groups=mesh['rows'=2,'hidden_0'=2,'hidden_1'=4,'latents_0'=16,'latents_1'=2] {'..., dimensions={0} | all-to-all | bytes 917504 | tf_op jit(solution)/shard_map/all_to_all | solution.py:23
  96.6 0.1 reduce_sum.70
  96.7 0.1 copy.62
  96.8 24.9 %all_to_all.58 = bf16[16,8,224]{2,1,0:T(8,128)(2,1)S(1)} all-to-all(bf16[16,8,224]{2,1,0:T(8,128)(2,1)S(1)} %bitcast.57), channel_id=1, replica_groups=mesh['rows'=2,'hidden_0'=2,'hidden_1'=4,'latents_0'=16,'latents_1'=2] {'..., dimensions={0} | all-to-all | bytes 114688 | tf_op jit(solution)/shard_map/all_to_all | solution.py:23
  121.7 0.7 broadcast_in_dim.23
  122.4 3.9 %all-to-all-start.4 = ((bf16[32,8,224]{2,1,0:T(8,128)(2,1)}), bf16[32,8,224]{2,1,0:T(8,128)(2,1)S(1)}, u32[]{:S(2)}, u32[]{:S(2)}) async-start(bf16[32,8,224]{2,1,0:T(8,128)(2,1)} %broadcast_in_dim.23), calls=%async_computation.4 | async-start | bytes 262144 | tf_op jit(solution)/shard_map/all_to_all | solution.py:23
  126.2 0.1 reshape.41
  126.4 0.1 eq.15
  126.5 15.3 %all-to-all-done.4 = bf16[32,8,224]{2,1,0:T(8,128)(2,1)S(1)} async-done(((bf16[32,8,224]{2,1,0:T(8,128)(2,1)}), bf16[32,8,224]{2,1,0:T(8,128)(2,1)S(1)}, u32[]{:S(2)}, u32[]{:S(2)}) %all-to-all-start.4) | async-done | bytes 114720 | tf_op jit(solution)/shard_map/all_to_all | solution.py:23
  141.8 0.1 copy.63
  141.9 2.0 all_gather.28
  143.9 0.2 convolution_convert_fusion.5
  144.1 0.2 convolution_convert_fusion.6
  144.4 0.0 copy-start.1
  144.4 0.5 convolution_convert_fusion.4
  144.9 14.4 %all_to_all.59 = bf16[8,32,1024]{2,1,0:T(8,128)(2,1)S(1)} all-to-all(bf16[8,32,1024]{2,1,0:T(8,128)(2,1)S(1)} %bitcast.54), channel_id=1, replica_groups=mesh['rows'=2,'hidden_0'=2,'hidden_1'=4,'latents_0'=16,'latents_1'=2] {'..., dimensions={0} | all-to-all | bytes 1048576 | tf_op jit(solution)/shard_map/all_to_all | solution.py:23
  159.3 0.1 convert_reduce_fusion.1
  159.4 0.1 fusion.12
  159.5 0.1 broadcast_in_dim.24
  159.6 14.1 %all_to_all.60 = bf16[8,32,1024]{2,1,0:T(8,128)(2,1)S(1)} all-to-all(bf16[8,32,1024]{2,1,0:T(8,128)(2,1)S(1)} %broadcast_in_dim.24), channel_id=1, replica_groups=mesh['rows'=2,'hidden_0'=2,'hidden_1'=4,'latents_0'=16,'latents_1'=2] {'..., dimensions={0} | all-to-all | bytes 1048576 | tf_op jit(solution)/shard_map/all_to_all | solution.py:23
  173.7 0.4 fusion.37
  174.2 2.6 %all-gather.2 = f32[512,448]{0,1:T(8,128)S(1)} all-gather(f32[256,448]{0,1:T(8,128)S(1)} %fusion.37), channel_id=4, replica_groups=mesh['rows'=2,'hidden_0'=2,'hidden_1'=4,'latents_0'=16,'latents_1'=2] {'..., dimensions={0}, use_global_device_ids=true | all-gather | bytes 1376256 | tf_op jit(solution)/shard_map/all_gather | solution.py:31
  176.8 0.6 reshape.53
  177.4 0.0 copy-start.2
  177.4 0.0 copy-start.5
  177.4 1.2 reduce_sum.73
  178.6 0.1 copy.66
  178.8 0.1 reshape.47
  178.8 0.7 fusion.10
  179.6 3.9 %all-to-all-start.7 = ((bf16[32,4,448]{2,1,0:T(4,128)(2,1)}), bf16[32,4,448]{2,1,0:T(4,128)(2,1)S(1)}, u32[]{:S(2)}, u32[]{:S(2)}) async-start(bf16[32,4,448]{2,1,0:T(4,128)(2,1)} %fusion.10), calls=%async_computation.7 | async-start | bytes 262144 | tf_op jit(solution)/shard_map/all_to_all | solution.py:23
  183.4 17.4 %all-to-all-done.7 = bf16[32,4,448]{2,1,0:T(4,128)(2,1)S(1)} async-done(((bf16[32,4,448]{2,1,0:T(4,128)(2,1)}), bf16[32,4,448]{2,1,0:T(4,128)(2,1)S(1)}, u32[]{:S(2)}, u32[]{:S(2)}) %all-to-all-start.7) | async-done | bytes 114720 | tf_op jit(solution)/shard_map/all_to_all | solution.py:23
  200.8 0.1 convert_reduce_fusion.2
  200.9 0.6 multiply_convert_fusion.1
  201.6 19.2 %all_to_all.61 = bf16[32,4,448]{2,1,0:T(4,128)(2,1)S(1)} all-to-all(bf16[32,4,448]{2,1,0:T(4,128)(2,1)S(1)} %broadcast_in_dim.25), channel_id=1, replica_groups=mesh['rows'=2,'hidden_0'=2,'hidden_1'=4,'latents_0'=16,'latents_1'=2] {'..., dimensions={0} | all-to-all | bytes 229376 | tf_op jit(solution)/shard_map/all_to_all | solution.py:23
  220.7 0.1 all_gather_reshape.7
  220.8 0.1 copy.67
  220.9 2.0 all_gather.31
  222.9 0.5 convolution_convert_fusion.3
  223.4 14.6 %all_to_all.62 = bf16[8,32,1024]{2,1,0:T(8,128)(2,1)S(1)} all-to-all(bf16[8,32,1024]{2,1,0:T(8,128)(2,1)S(1)} %bitcast.55), channel_id=1, replica_groups=mesh['rows'=2,'hidden_0'=2,'hidden_1'=4,'latents_0'=16,'latents_1'=2] {'..., dimensions={0} | all-to-all | bytes 1048576 | tf_op jit(solution)/shard_map/all_to_all | solution.py:23
  238.0 0.1 convert_reduce_fusion
  238.1 0.1 multiply_convert_fusion
  238.1 0.9 broadcast_in_dim.26
  239.0 5.5 %all-to-all-start.10 = ((bf16[8,32,1024]{2,1,0:T(8,128)(2,1)}), bf16[8,32,1024]{2,1,0:T(8,128)(2,1)S(1)}, u32[]{:S(2)}, u32[]{:S(2)}) async-start(bf16[8,32,1024]{2,1,0:T(8,128)(2,1)} %broadcast_in_dim.26), calls=%async_computation.10 | async-start | bytes 1048576 | tf_op jit(solution)/shard_map/all_to_all | solution.py:23
  244.5 1.3 convolution_convert_fusion.1
  245.8 8.1 %all-to-all-done.10 = bf16[8,32,1024]{2,1,0:T(8,128)(2,1)S(1)} async-done(((bf16[8,32,1024]{2,1,0:T(8,128)(2,1)}), bf16[8,32,1024]{2,1,0:T(8,128)(2,1)S(1)}, u32[]{:S(2)}, u32[]{:S(2)}) %all-to-all-start.10) | async-done | bytes 524320 | tf_op jit(solution)/shard_map/all_to_all | solution.py:23
  253.9 1.5 convolution_convert_fusion.2
  (15 shorter events, 0.1 us)
Async XLA Ops:
  7.2 166.5 %copy-start = (bf16[1024,448]{0,1:T(8,128)(2,1)S(1)}, bf16[1024,448]{0,1:T(8,128)(2,1)}, u32[]{:S(2)}) copy-start(bf16[1024,448]{0,1:T(8,128)(2,1)} %param.14) | copy-start | bytes 2752516
  7.2 60.0 %all-gather.5.cloned.1.call-start = ((), (), s32[]{:S(2)}) async-start(), calls=%async_computation.11 | async-start | bytes 2752512 | tf_op jit(solution)/shard_map/all_gather | solution.py:31
  53.5 1.8 copy-start.3
  80.1 46.2 %copy-start.6 = (s32[256]{0:T(256)S(1)}, s32[256]{0:T(256)}, u32[]{:S(2)}) copy-start(s32[256]{0:T(256)} %param.17) | copy-start | bytes 3076
  80.1 64.2 %copy-start.7 = (bf16[448,1024]{1,0:T(8,128)(2,1)S(1)}, bf16[448,1024]{1,0:T(8,128)(2,1)}, u32[]{:S(2)}) copy-start(bf16[448,1024]{1,0:T(8,128)(2,1)} %param.13) | copy-start | bytes 2752516
  122.4 19.4 %all-to-all-start.4 = ((bf16[32,8,224]{2,1,0:T(8,128)(2,1)}), bf16[32,8,224]{2,1,0:T(8,128)(2,1)S(1)}, u32[]{:S(2)}, u32[]{:S(2)}) async-start(bf16[32,8,224]{2,1,0:T(8,128)(2,1)} %broadcast_in_dim.23), calls=%async_computation.4 | async-start | bytes 262144 | tf_op jit(solution)/shard_map/all_to_all | solution.py:23
  144.1 15.3 %copy-start.4 = (f32[1024]{0:T(1024)S(1)}, f32[1024]{0:T(1024)}, u32[]{:S(2)}) copy-start(f32[1024]{0:T(1024)} %param.15) | copy-start | bytes 12292
  144.4 15.2 %copy-start.1 = (bf16[256,224]{1,0:T(8,128)(2,1)}, bf16[256,224]{1,0:T(8,128)(2,1)S(1)}, u32[]{:S(2)}) copy-start(bf16[256,224]{1,0:T(8,128)(2,1)S(1)} %convolution_convert_fusion.6) | copy-start | bytes 344068
  177.4 23.5 %copy-start.2 = (bf16[256,224]{1,0:T(8,128)(2,1)S(1)}, bf16[256,224]{1,0:T(8,128)(2,1)}, u32[]{:S(2)}) copy-start(bf16[256,224]{1,0:T(8,128)(2,1)} %copy-done.1) | copy-start | bytes 344068
  177.4 23.5 %copy-start.5 = (f32[448]{0:T(512)S(1)}, f32[448]{0:T(512)}, u32[]{:S(2)}) copy-start(f32[448]{0:T(512)} %param.16) | copy-start | bytes 5380
  179.6 21.3 %all-to-all-start.7 = ((bf16[32,4,448]{2,1,0:T(4,128)(2,1)}), bf16[32,4,448]{2,1,0:T(4,128)(2,1)S(1)}, u32[]{:S(2)}, u32[]{:S(2)}) async-start(bf16[32,4,448]{2,1,0:T(4,128)(2,1)} %fusion.10), calls=%async_computation.7 | async-start | bytes 262144 | tf_op jit(solution)/shard_map/all_to_all | solution.py:23
  239.0 15.0 %all-to-all-start.10 = ((bf16[8,32,1024]{2,1,0:T(8,128)(2,1)}), bf16[8,32,1024]{2,1,0:T(8,128)(2,1)S(1)}, u32[]{:S(2)}, u32[]{:S(2)}) async-start(bf16[8,32,1024]{2,1,0:T(8,128)(2,1)} %broadcast_in_dim.26), calls=%async_computation.10 | async-start | bytes 1048576 | tf_op jit(solution)/shard_map/all_to_all | solution.py:23
Sparse Core Ops, SparseCore 0:
  56.8 10.2 all-gather.4

commit v2 on v1

--- a/solution.py
+++ b/solution.py
@@ -31,6 +31,10 @@
     return lax.all_gather(x, C, axis=0, tiled=False)
 
 
+def swapped(x):
+    return lax.ppermute(x, C, [(0, 1), (1, 0)])
+
+
 def total(blocks):
     return jnp.sum(blocks.astype(F32), axis=0)
 
@@ -52,6 +56,13 @@
     latents = encoder.shape[1]
     units = gate_weight.shape[1]
 
+    blocks = down_weight.reshape(units, n_hidden, 2, half)
+    kept, given = own(blocks, core, 2), own(blocks, 1 - core, 2)
+    taken = swapped(given)
+    down_pair = jnp.concatenate(
+        [jnp.where(core == 0, kept, taken), jnp.where(core == 0, taken, kept)]
+    ).reshape(2 * units, n_hidden * half)
+
     few = sent_to_all(inputs.T, Z)
     more = sent_to_all(few, HIDDEN)
     every = both_cores(more)
@@ -61,12 +72,11 @@
         both_weights, gathered, (((0,), (0,)), ((), ())), preferred_element_type=F32
     )
     hidden = (jax.nn.gelu(acts[:units], approximate=True) * acts[units:]).astype(BF16)
-    part = lax.dot_general(
-        down_weight, hidden, (((0,), (0,)), ((), ())), preferred_element_type=F32
-    ).astype(BF16)
+    hidden_pair = both_cores(hidden).reshape(2 * units, -1)
+    mine = lax.dot_general(
+        down_pair, hidden_pair, (((0,), (0,)), ((), ())), preferred_element_type=F32
+    ).astype(BF16).reshape(n_hidden, half, -1)
 
-    pair = total(both_cores(part)).reshape(n_hidden, 2, half, -1)
-    mine = own(pair, core, 1).astype(BF16)
     summed = total(exchange(mine, HIDDEN)).T.astype(BF16)
     rows_own = total(exchange(summed.reshape(n_z, -1, half), Z)).astype(BF16)
     mlp_out = both_cores(sent_to_all(rows_own, ROWS_Z).reshape(tokens, half))
@@ -81,9 +91,10 @@
     pre_act = total(exchange(pre_local.reshape(n_hidden, -1, latents), HIDDEN)) + enc_bias[None, :]
     latent_own = (smooth_scale * jax.nn.softplus(pre_act / smooth_scale)).astype(BF16)
     latent_act = sent_to_all(latent_own, HIDDEN).reshape(tokens, latents)
-    recon_local = jnp.dot(latent_act, decoder, preferred_element_type=F32)
-    recon_pair = jnp.sum(both_cores(recon_local), axis=0)
-    recon_mine = own(recon_pair.reshape(2, n_rows_z, -1, width), core, 0).astype(BF16)
+    halves = latent_act.reshape(2, -1, latents)
+    recon_other = jnp.dot(own(halves, 1 - core, 0), decoder, preferred_element_type=F32)
+    recon_own = jnp.dot(own(halves, core, 0), decoder, preferred_element_type=F32)
+    recon_mine = (recon_own + swapped(recon_other)).astype(BF16).reshape(n_rows_z, -1, width)
     recon = total(exchange(recon_mine, ROWS_Z)) + dec_bias[None, :]
     recon_out = recon.astype(BF16)
 

time: 266 us -> 222 us (0.83)
  blocking collectives: 155 us -> 103 us
  starting transfers between devices: 13.3 us -> 39.7 us
  between operations: 14.4 us -> 0.97 us
  other arithmetic: 8.75 us -> 1.21 us
  waiting for transfers between devices: 51.2 us -> 57.2 us
    all_to_all x8 -> x6, blocking collectives: 146 us -> 94.9 us  [exchange(): return lax.all_to_all(blocks, axes, 0, 0, tiled=True)]
    all_to_all x3 -> x5, starting transfers between devices: 13.3 us -> 35.9 us  [exchange(): return lax.all_to_all(blocks, axes, 0, 0, tiled=True)]
    all_to_all x3 -> x5, waiting for transfers between devices: 40.8 us -> 55.7 us  [exchange(): return lax.all_to_all(blocks, axes, 0, 0, tiled=True)]
    all_gather x1 -> x0, waiting for transfers between devices: 10.4 us -> none  [both_cores(): return lax.all_gather(x, C, axis=0, tiled=False)]
    reduce_sum x6 -> x5, other arithmetic: 6.81 us -> 0.32 us  [total(): return jnp.sum(blocks.astype(F32), axis=0)]
    convert_element_type x3 -> x1, local copies, waits for them, and re-layouts: 6.53 us -> 0.11 us  [shards(): (recon_own + swapped(recon_other)).astype(BF16).reshape(n_rows_z, -1, width)]
    ppermute x0 -> x2, starting transfers between devices: none -> 3.84 us  [swapped(): return lax.ppermute(x, C, [(0, 1), (1, 0)])]
    reshape x1 -> x3, local copies, waits for them, and re-layouts: 0.08 us -> 2.91 us  [the longest x1 1.71 us: shards(): blocks = down_weight.reshape(units, n_hidden, 2, half)]
  transfers between devices with their start and end apart: 4 -> 7, of which waited for: 4 -> 6; matrix products, arithmetic and copies ran while one was open for 1% -> 3% of each run, Pallas kernels for 0% -> 0%
where the time goes in v2:
time: 222 us; the launch traced here: 218 us
  blocking collectives  103 us (46%)
  waiting for transfers between devices  57.2 us (26%)
  starting transfers between devices  39.7 us (18%)
  local copies, waits for them, and re-layouts  9.05 us (4%)
  matrix products  6.8 us (3%)
    all_to_all x6, blocking collectives, exchange(): return lax.all_to_all(blocks, axes, 0, 0, tiled=True)  94.9 us
    all_to_all x5, waiting for transfers between devices, exchange(): return lax.all_to_all(blocks, axes, 0, 0, tiled=True)  55.7 us
    all_to_all x5, starting transfers between devices, exchange(): return lax.all_to_all(blocks, axes, 0, 0, tiled=True)  35.9 us
    all_gather x4, blocking collectives, both_cores(): return lax.all_gather(x, C, axis=0, tiled=False)  8.22 us
  transfers between devices with their start and end apart: 7, of which 6 were waited for; matrix products, arithmetic and copies ran while one was open for 3% of the time, Pallas kernels for 0%

profile of v2, /device:TPU:6, one launch (start us, length us, event | category | flops | bytes accessed | tf_op | source)
XLA Modules:
  0.0 218.1 jit_solution(1533759084790658769)
XLA Ops:
  0.6 0.0 copy-start
  0.6 1.4 broadcast_in_dim.21
  2.1 15.2 %all-to-all-start = ((bf16[16,14,128]{2,1,0:T(8,128)(2,1)}), bf16[16,14,128]{2,1,0:T(8,128)(2,1)S(1)}, u32[]{:S(2)}, u32[]{:S(2)}) async-start(bf16[16,14,128]{2,1,0:T(8,128)(2,1)} %broadcast_in_dim.21), calls=%async_computation | async-start | bytes 131072 | tf_op jit(solution)/shard_map/all_to_all | solution.py:23
  17.3 1.7 reshape.49
  19.0 1.0 constant_dynamic-slice_fusion.1
  20.0 1.9 collective-permute-start
  21.9 8.1 %all-to-all-done = bf16[16,14,128]{2,1,0:T(8,128)(2,1)S(1)} async-done(((bf16[16,14,128]{2,1,0:T(8,128)(2,1)}), bf16[16,14,128]{2,1,0:T(8,128)(2,1)S(1)}, u32[]{:S(2)}, u32[]{:S(2)}) %all-to-all-start) | async-done | bytes 57376 | tf_op jit(solution)/shard_map/all_to_all | solution.py:23
  30.0 0.8 broadcast_in_dim.22
  30.8 7.4 %all-to-all-start.1 = ((bf16[8,16,14,128]{3,1,2,0:T(8,128)(2,1)}), bf16[8,16,14,128]{3,1,2,0:T(8,128)(2,1)S(1)}, u32[]{:S(2)}, u32[]{:S(2)}) async-start(bf16[8,16,14,128]{3,1,2,0:T(8,128)(2,1)} %broadcast_in_dim.22), calls=%async_computation.1 | async-start | bytes 917504 | tf_op jit(solution)/shard_map/all_to_all | solution.py:23
  38.3 0.1 pad_maximum_fusion
  38.4 0.5 reshape.50
  38.9 6.9 %all-to-all-done.1 = bf16[8,16,14,128]{3,1,2,0:T(8,128)(2,1)S(1)} async-done(((bf16[8,16,14,128]{3,1,2,0:T(8,128)(2,1)}), bf16[8,16,14,128]{3,1,2,0:T(8,128)(2,1)S(1)}, u32[]{:S(2)}, u32[]{:S(2)}) %all-to-all-start.1) | async-done | bytes 458784 | tf_op jit(solution)/shard_map/all_to_all | solution.py:23
  45.7 2.5 %all-gather = bf16[16,16,14,128]{3,1,2,0:T(8,128)(2,1)S(1)} all-gather(bf16[8,16,14,128]{3,1,2,0:T(8,128)(2,1)S(1)} %all-to-all-done.1), channel_id=2, replica_groups=mesh['rows'=2,'hidden_0'=2,'hidden_1'=4,'latents_0'=16,'latents_1'=2] {'..., dimensions={0}, use_global_device_ids=true | all-gather | bytes 1376256 | tf_op jit(solution)/shard_map/all_gather | solution.py:31
  48.2 0.3 copy.49
  48.5 0.3 reshape.51
  48.7 1.5 fusion.1
  50.3 1.8 all-gather.1
  52.1 0.3 convolution_convert_fusion
  52.4 0.0 copy-start.3
  52.4 14.2 %all_to_all.55 = bf16[8,224,128]{2,1,0:T(8,128)(2,1)S(1)} all-to-all(bf16[8,224,128]{2,1,0:T(8,128)(2,1)S(1)} %bitcast.58), channel_id=1, replica_groups=mesh['rows'=2,'hidden_0'=2,'hidden_1'=4,'latents_0'=16,'latents_1'=2] {'..., dimensions={0} | all-to-all | bytes 917504 | tf_op jit(solution)/shard_map/all_to_all | solution.py:23
  66.6 0.1 reduce_sum.51
  66.7 0.0 copy-start.4
  66.7 0.1 copy.50
  66.8 18.4 %all_to_all.56 = bf16[16,8,224]{2,1,0:T(8,128)(2,1)S(1)} all-to-all(bf16[16,8,224]{2,1,0:T(8,128)(2,1)S(1)} %bitcast.62), channel_id=1, replica_groups=mesh['rows'=2,'hidden_0'=2,'hidden_1'=4,'latents_0'=16,'latents_1'=2] {'..., dimensions={0} | all-to-all | bytes 114688 | tf_op jit(solution)/shard_map/all_to_all | solution.py:23
  85.2 0.7 broadcast_in_dim.23
  85.9 3.9 %all-to-all-start.4 = ((bf16[32,8,224]{2,1,0:T(8,128)(2,1)}), bf16[32,8,224]{2,1,0:T(8,128)(2,1)S(1)}, u32[]{:S(2)}, u32[]{:S(2)}) async-start(bf16[32,8,224]{2,1,0:T(8,128)(2,1)} %broadcast_in_dim.23), calls=%async_computation.4 | async-start | bytes 262144 | tf_op jit(solution)/shard_map/all_to_all | solution.py:23
  89.8 0.1 reshape.48
  89.9 0.1 eq.19
  90.0 15.3 %all-to-all-done.4 = bf16[32,8,224]{2,1,0:T(8,128)(2,1)S(1)} async-done(((bf16[32,8,224]{2,1,0:T(8,128)(2,1)}), bf16[32,8,224]{2,1,0:T(8,128)(2,1)S(1)}, u32[]{:S(2)}, u32[]{:S(2)}) %all-to-all-start.4) | async-done | bytes 114720 | tf_op jit(solution)/shard_map/all_to_all | solution.py:23
  105.3 0.1 copy.51
  105.4 2.0 all_gather.22
  107.4 0.2 convolution_convert_fusion.5
  107.6 0.2 convolution_convert_fusion.6
  107.9 0.5 convolution_convert_fusion.4
  108.3 0.0 copy-start.1
  108.4 14.5 %all_to_all.57 = bf16[8,32,1024]{2,1,0:T(8,128)(2,1)S(1)} all-to-all(bf16[8,32,1024]{2,1,0:T(8,128)(2,1)S(1)} %bitcast.59), channel_id=1, replica_groups=mesh['rows'=2,'hidden_0'=2,'hidden_1'=4,'latents_0'=16,'latents_1'=2] {'..., dimensions={0} | all-to-all | bytes 1048576 | tf_op jit(solution)/shard_map/all_to_all | solution.py:23
  122.8 0.1 convert_reduce_fusion.1
  122.9 0.1 fusion.15
  123.0 0.1 broadcast_in_dim.24
  123.1 14.1 %all_to_all.58 = bf16[8,32,1024]{2,1,0:T(8,128)(2,1)S(1)} all-to-all(bf16[8,32,1024]{2,1,0:T(8,128)(2,1)S(1)} %broadcast_in_dim.24), channel_id=1, replica_groups=mesh['rows'=2,'hidden_0'=2,'hidden_1'=4,'latents_0'=16,'latents_1'=2] {'..., dimensions={0} | all-to-all | bytes 1048576 | tf_op jit(solution)/shard_map/all_to_all | solution.py:23
  137.2 0.4 fusion.5
  137.6 0.0 copy-start.2
  137.6 1.9 collective-permute-start.1
  139.6 1.5 collective-permute-done.1
  141.0 0.4 fusion
  141.4 0.1 copy.54
  141.6 0.7 reshape.56
  142.2 3.9 %all-to-all-start.7 = ((bf16[32,4,448]{2,1,0:T(4,128)(2,1)}), bf16[32,4,448]{2,1,0:T(4,128)(2,1)S(1)}, u32[]{:S(2)}, u32[]{:S(2)}) async-start(bf16[32,4,448]{2,1,0:T(4,128)(2,1)} %reshape.56), calls=%async_computation.7 | async-start | bytes 262144 | tf_op jit(solution)/shard_map/all_to_all | solution.py:23
  146.1 17.4 %all-to-all-done.7 = bf16[32,4,448]{2,1,0:T(4,128)(2,1)S(1)} async-done(((bf16[32,4,448]{2,1,0:T(4,128)(2,1)}), bf16[32,4,448]{2,1,0:T(4,128)(2,1)S(1)}, u32[]{:S(2)}, u32[]{:S(2)}) %all-to-all-start.7) | async-done | bytes 114720 | tf_op jit(solution)/shard_map/all_to_all | solution.py:23
  163.5 0.1 convert_reduce_fusion.2
  163.6 0.6 multiply_convert_fusion.1
  164.3 19.2 %all_to_all.59 = bf16[32,4,448]{2,1,0:T(4,128)(2,1)S(1)} all-to-all(bf16[32,4,448]{2,1,0:T(4,128)(2,1)S(1)} %broadcast_in_dim.25), channel_id=1, replica_groups=mesh['rows'=2,'hidden_0'=2,'hidden_1'=4,'latents_0'=16,'latents_1'=2] {'..., dimensions={0} | all-to-all | bytes 229376 | tf_op jit(solution)/shard_map/all_to_all | solution.py:23
  183.4 0.1 all_gather_reshape.7
  183.5 0.1 copy.55
  183.6 2.0 all_gather.23
  185.6 0.5 convolution_convert_fusion.3
  186.1 14.6 %all_to_all.60 = bf16[8,32,1024]{2,1,0:T(8,128)(2,1)S(1)} all-to-all(bf16[8,32,1024]{2,1,0:T(8,128)(2,1)S(1)} %bitcast.60), channel_id=1, replica_groups=mesh['rows'=2,'hidden_0'=2,'hidden_1'=4,'latents_0'=16,'latents_1'=2] {'..., dimensions={0} | all-to-all | bytes 1048576 | tf_op jit(solution)/shard_map/all_to_all | solution.py:23
  200.7 0.1 convert_reduce_fusion
  200.7 0.1 multiply_convert_fusion
  200.8 0.9 broadcast_in_dim.26
  201.7 5.5 %all-to-all-start.10 = ((bf16[8,32,1024]{2,1,0:T(8,128)(2,1)}), bf16[8,32,1024]{2,1,0:T(8,128)(2,1)S(1)}, u32[]{:S(2)}, u32[]{:S(2)}) async-start(bf16[8,32,1024]{2,1,0:T(8,128)(2,1)} %broadcast_in_dim.26), calls=%async_computation.10 | async-start | bytes 1048576 | tf_op jit(solution)/shard_map/all_to_all | solution.py:23
  207.2 1.3 convolution_convert_fusion.1
  208.5 8.1 %all-to-all-done.10 = bf16[8,32,1024]{2,1,0:T(8,128)(2,1)S(1)} async-done(((bf16[8,32,1024]{2,1,0:T(8,128)(2,1)}), bf16[8,32,1024]{2,1,0:T(8,128)(2,1)S(1)}, u32[]{:S(2)}, u32[]{:S(2)}) %all-to-all-start.10) | async-done | bytes 524320 | tf_op jit(solution)/shard_map/all_to_all | solution.py:23
  216.6 1.5 convolution_convert_fusion.2
  (13 shorter events, 0.2 us)
Async XLA Ops:
  0.6 136.6 %copy-start = (bf16[1024,448]{0,1:T(8,128)(2,1)S(1)}, bf16[1024,448]{0,1:T(8,128)(2,1)}, u32[]{:S(2)}) copy-start(bf16[1024,448]{0,1:T(8,128)(2,1)} %param.14) | copy-start | bytes 2752516
  2.1 27.9 %all-to-all-start = ((bf16[16,14,128]{2,1,0:T(8,128)(2,1)}), bf16[16,14,128]{2,1,0:T(8,128)(2,1)S(1)}, u32[]{:S(2)}, u32[]{:S(2)}) async-start(bf16[16,14,128]{2,1,0:T(8,128)(2,1)} %broadcast_in_dim.21), calls=%async_computation | async-start | bytes 131072 | tf_op jit(solution)/shard_map/all_to_all | solution.py:23
  20.0 18.3 %collective-permute-start = (bf16[56,8,224]{2,1,0:T(8,128)(2,1)S(1)}, bf16[56,8,224]{2,1,0:T(8,128)(2,1)S(1)}, u32[]{:S(2)}, u32[]{:S(2)}) collective-permute-start(bf16[56,8,224]{2,1,0:T(8,128)(2,1)S(1)} %bitcast.64), channel_id=1, source_target_pairs={{0,1},{1,0},{2,3},{3,2},{4,5},{5,4},{6,7},{7,6},{8,9},{9,8},{10,11... | collective-permute-start | bytes 602120 | tf_op jit(solution)/shard_map/ppermute | solution.py:35
  30.8 14.9 %all-to-all-start.1 = ((bf16[8,16,14,128]{3,1,2,0:T(8,128)(2,1)}), bf16[8,16,14,128]{3,1,2,0:T(8,128)(2,1)S(1)}, u32[]{:S(2)}, u32[]{:S(2)}) async-start(bf16[8,16,14,128]{3,1,2,0:T(8,128)(2,1)} %broadcast_in_dim.22), calls=%async_computation.1 | async-start | bytes 917504 | tf_op jit(solution)/shard_map/all_to_all | solution.py:23
  52.4 37.3 %copy-start.3 = (s32[256]{0:T(256)S(1)}, s32[256]{0:T(256)}, u32[]{:S(2)}) copy-start(s32[256]{0:T(256)} %param.17) | copy-start | bytes 3076
  66.7 41.2 %copy-start.4 = (bf16[448,1024]{1,0:T(8,128)(2,1)S(1)}, bf16[448,1024]{1,0:T(8,128)(2,1)}, u32[]{:S(2)}) copy-start(bf16[448,1024]{1,0:T(8,128)(2,1)} %param.13) | copy-start | bytes 2752516
  85.9 19.4 %all-to-all-start.4 = ((bf16[32,8,224]{2,1,0:T(8,128)(2,1)}), bf16[32,8,224]{2,1,0:T(8,128)(2,1)S(1)}, u32[]{:S(2)}, u32[]{:S(2)}) async-start(bf16[32,8,224]{2,1,0:T(8,128)(2,1)} %broadcast_in_dim.23), calls=%async_computation.4 | async-start | bytes 262144 | tf_op jit(solution)/shard_map/all_to_all | solution.py:23
  108.3 14.5 %copy-start.1 = (f32[1024]{0:T(1024)S(1)}, f32[1024]{0:T(1024)}, u32[]{:S(2)}) copy-start(f32[1024]{0:T(1024)} %param.15) | copy-start | bytes 12292
  137.6 26.0 %copy-start.2 = (f32[448]{0:T(512)S(1)}, f32[448]{0:T(512)}, u32[]{:S(2)}) copy-start(f32[448]{0:T(512)} %param.16) | copy-start | bytes 5380
  137.6 3.4 %collective-permute-start.1 = (f32[128,448]{0,1:T(8,128)S(1)}, f32[128,448]{0,1:T(8,128)S(1)}, u32[]{:S(2)}, u32[]{:S(2)}) collective-permute-start(f32[128,448]{0,1:T(8,128)S(1)} %fusion.5), channel_id=1, source_target_pairs={{0,1},{1,0},{2,3},{3,2},{4,5},{5,4},{6,7},{7,6},{8,9},{9,8},{10,11... | collective-permute-start | bytes 688136 | tf_op jit(solution)/shard_map/ppermute | solution.py:35
  142.2 21.3 %all-to-all-start.7 = ((bf16[32,4,448]{2,1,0:T(4,128)(2,1)}), bf16[32,4,448]{2,1,0:T(4,128)(2,1)S(1)}, u32[]{:S(2)}, u32[]{:S(2)}) async-start(bf16[32,4,448]{2,1,0:T(4,128)(2,1)} %reshape.56), calls=%async_computation.7 | async-start | bytes 262144 | tf_op jit(solution)/shard_map/all_to_all | solution.py:23
  201.7 15.0 %all-to-all-start.10 = ((bf16[8,32,1024]{2,1,0:T(8,128)(2,1)}), bf16[8,32,1024]{2,1,0:T(8,128)(2,1)S(1)}, u32[]{:S(2)}, u32[]{:S(2)}) async-start(bf16[8,32,1024]{2,1,0:T(8,128)(2,1)} %broadcast_in_dim.26), calls=%async_computation.10 | async-start | bytes 1048576 | tf_op jit(solution)/shard_map/all_to_all | solution.py:23

commit v3 on v2

--- a/solution.py
+++ b/solution.py
@@ -56,21 +56,20 @@
     latents = encoder.shape[1]
     units = gate_weight.shape[1]
 
-    blocks = down_weight.reshape(units, n_hidden, 2, half)
+    weights = lax.optimization_barrier(jnp.concatenate([gate_weight.T, up_weight.T], axis=0))
+    few = sent_to_all(inputs.T, Z)
+
+    few, down = lax.optimization_barrier((few, down_weight))
+    blocks = down.reshape(units, n_hidden, 2, half)
     kept, given = own(blocks, core, 2), own(blocks, 1 - core, 2)
     taken = swapped(given)
     down_pair = jnp.concatenate(
         [jnp.where(core == 0, kept, taken), jnp.where(core == 0, taken, kept)]
     ).reshape(2 * units, n_hidden * half)
 
-    few = sent_to_all(inputs.T, Z)
-    more = sent_to_all(few, HIDDEN)
-    every = both_cores(more)
+    every = both_cores(sent_to_all(few, HIDDEN))
     gathered = every.transpose(1, 2, 0, 3, 4).reshape(-1, inputs.shape[0])
-    both_weights = jnp.concatenate([gate_weight, up_weight], axis=1)
-    acts = lax.dot_general(
-        both_weights, gathered, (((0,), (0,)), ((), ())), preferred_element_type=F32
-    )
+    acts = jnp.dot(weights, gathered, preferred_element_type=F32)
     hidden = (jax.nn.gelu(acts[:units], approximate=True) * acts[units:]).astype(BF16)
     hidden_pair = both_cores(hidden).reshape(2 * units, -1)
     mine = lax.dot_general(
@@ -81,29 +80,35 @@
     rows_own = total(exchange(summed.reshape(n_z, -1, half), Z)).astype(BF16)
     mlp_out = both_cores(sent_to_all(rows_own, ROWS_Z).reshape(tokens, half))
 
-    order = shuffle_order.reshape(n_rows_z, 2, -1).transpose(1, 0, 2).reshape(-1)
-    pick = (order[:, None] == jnp.arange(tokens)[None, :]).astype(BF16)
+    pick = (shuffle_order[:, None] == jnp.arange(tokens)[None, :]).astype(BF16)
     shuffled = jnp.concatenate(
         [jnp.dot(pick, mlp_out[c], preferred_element_type=F32).astype(BF16) for c in range(2)],
         axis=1,
     )
+    shuffled_t = lax.optimization_barrier(shuffled.T)
     pre_local = jnp.dot(shuffled, encoder, preferred_element_type=F32).astype(BF16)
     pre_act = total(exchange(pre_local.reshape(n_hidden, -1, latents), HIDDEN)) + enc_bias[None, :]
     latent_own = (smooth_scale * jax.nn.softplus(pre_act / smooth_scale)).astype(BF16)
     latent_act = sent_to_all(latent_own, HIDDEN).reshape(tokens, latents)
-    halves = latent_act.reshape(2, -1, latents)
-    recon_other = jnp.dot(own(halves, 1 - core, 0), decoder, preferred_element_type=F32)
-    recon_own = jnp.dot(own(halves, core, 0), decoder, preferred_element_type=F32)
-    recon_mine = (recon_own + swapped(recon_other)).astype(BF16).reshape(n_rows_z, -1, width)
-    recon = total(exchange(recon_mine, ROWS_Z)) + dec_bias[None, :]
-    recon_out = recon.astype(BF16)
+    recon_local = lax.dot_general(
+        decoder, latent_act, (((0,), (1,)), ((), ())), preferred_element_type=F32
+    ).astype(BF16)
+    recon_pair = both_cores(recon_local).reshape(2, 2, half, tokens)
+    recon_mine = total(own(recon_pair, core, 1)).T.astype(BF16).reshape(n_rows_z, -1, half)
+    bias_mine = own(dec_bias.reshape(2, half), core, 0)
+    recon = total(exchange(recon_mine, ROWS_Z)) + bias_mine[None, :]
+    count = recon.shape[0]
+    both_recon = both_cores(recon.astype(BF16)).reshape(2, 2, count // 2, half)
+    recon_out = own(both_recon, core, 1).transpose(1, 0, 2).reshape(count // 2, width)
 
     scale = 1.0 / math.sqrt(tokens)
-    count = recon.shape[0]
-    first = (core * n_rows_z + lax.axis_index(ROWS_Z)) * count
-    target = lax.dynamic_slice_in_dim(shuffled, first, count, 0)
+    first = lax.axis_index(ROWS_Z) * count
+    target = own(
+        lax.dynamic_slice_in_dim(shuffled, first, count, 0).reshape(count, 2, half), core, 1
+    )
     err_own = (scale * (recon - target.astype(F32))).astype(BF16)
-    d_err = both_cores(sent_to_all(err_own, ROWS_Z).reshape(-1, width)).reshape(tokens, width)
+    err_pair = both_cores(sent_to_all(err_own, ROWS_Z).reshape(tokens, half))
+    d_err = jnp.concatenate([err_pair[0], err_pair[1]], axis=1)
 
     back_local = lax.dot_general(
         d_err, decoder, (((1,), (1,)), ((), ())), preferred_element_type=F32
@@ -116,9 +121,7 @@
         (d_latent + sparsity_weight * scale) * jax.nn.sigmoid(pre_act / smooth_scale)
     ).astype(BF16)
     d_pre = sent_to_all(d_pre_own, HIDDEN).reshape(tokens, latents)
-    grad_enc = lax.dot_general(
-        shuffled, d_pre, (((0,), (0,)), ((), ())), preferred_element_type=F32
-    ).astype(BF16)
+    grad_enc = jnp.dot(shuffled_t, d_pre, preferred_element_type=F32).astype(BF16)
     return (recon_out, grad_enc, grad_dec)
 
 

time: 222 us -> 217 us (0.977)
  waiting for transfers between devices: 57.2 us -> 47.4 us
  blocking collectives: 103 us -> 109 us
    all_to_all x5, waiting for transfers between devices: 55.7 us -> 46.9 us  [exchange(): return lax.all_to_all(blocks, axes, 0, 0, tiled=True)]
    all_gather x4 -> x6, blocking collectives: 8.22 us -> 12.1 us  [both_cores(): return lax.all_gather(x, C, axis=0, tiled=False)]
  transfers between devices with their start and end apart: 7 -> 6, of which waited for: 6 -> 6; matrix products, arithmetic and copies ran while one was open for 3% -> 3% of each run, Pallas kernels for 0% -> 0%
where the time goes in v3:
time: 217 us; the launch traced here: 214 us
  blocking collectives  109 us (50%)
  waiting for transfers between devices  47.4 us (22%)
  starting transfers between devices  39.8 us (18%)
  local copies, waits for them, and re-layouts  7.94 us (4%)
  matrix products  7.21 us (3%)
    all_to_all x6, blocking collectives, exchange(): return lax.all_to_all(blocks, axes, 0, 0, tiled=True)  96.7 us
    all_to_all x5, waiting for transfers between devices, exchange(): return lax.all_to_all(blocks, axes, 0, 0, tiled=True)  46.9 us
    all_to_all x5, starting transfers between devices, exchange(): return lax.all_to_all(blocks, axes, 0, 0, tiled=True)  37.9 us
    all_gather x6, blocking collectives, both_cores(): return lax.all_gather(x, C, axis=0, tiled=False)  12.1 us
  transfers between devices with their start and end apart: 6, of which 6 were waited for; matrix products, arithmetic and copies ran while one was open for 3% of the time, Pallas kernels for 0%

profile of v3, /device:TPU:6, one launch (start us, length us, event | category | flops | bytes accessed | tf_op | source)
XLA Modules:
  0.0 213.9 jit_solution(10730809922803519371)
XLA Ops:
  0.6 0.0 copy-start
  0.7 1.4 broadcast_in_dim.22
  2.1 15.2 %all-to-all-start = ((bf16[16,14,128]{2,1,0:T(8,128)(2,1)}), bf16[16,14,128]{2,1,0:T(8,128)(2,1)S(1)}, u32[]{:S(2)}, u32[]{:S(2)}) async-start(bf16[16,14,128]{2,1,0:T(8,128)(2,1)} %broadcast_in_dim.22), calls=%async_computation | async-start | bytes 131072 | tf_op jit(solution)/shard_map/all_to_all | solution.py:23
  17.3 12.7 %all-to-all-done = bf16[16,14,128]{2,1,0:T(8,128)(2,1)S(1)} async-done(((bf16[16,14,128]{2,1,0:T(8,128)(2,1)}), bf16[16,14,128]{2,1,0:T(8,128)(2,1)S(1)}, u32[]{:S(2)}, u32[]{:S(2)}) %all-to-all-start) | async-done | bytes 57376 | tf_op jit(solution)/shard_map/all_to_all | solution.py:23
  30.0 0.8 broadcast_in_dim.23
  30.9 7.4 %all-to-all-start.1 = ((bf16[8,16,14,128]{3,1,2,0:T(8,128)(2,1)}), bf16[8,16,14,128]{3,1,2,0:T(8,128)(2,1)S(1)}, u32[]{:S(2)}, u32[]{:S(2)}) async-start(bf16[8,16,14,128]{3,1,2,0:T(8,128)(2,1)} %broadcast_in_dim.23), calls=%async_computation.1 | async-start | bytes 917504 | tf_op jit(solution)/shard_map/all_to_all | solution.py:23
  38.3 0.7 reshape.93
  39.0 0.0 copy-start.1
  39.0 0.0 copy-start.2
  39.0 1.0 constant_dynamic-slice_fusion.2
  40.0 1.9 collective-permute-start
  42.0 0.9 pad_maximum_fusion
  42.9 0.5 collective-permute-done
  43.5 0.1 pad_maximum_fusion.1
  43.6 0.5 reshape.94
  44.1 1.7 all-to-all-done.1
  45.8 2.5 %all-gather = bf16[16,16,14,128]{3,1,2,0:T(8,128)(2,1)S(1)} all-gather(bf16[8,16,14,128]{3,1,2,0:T(8,128)(2,1)S(1)} %all-to-all-done.1), channel_id=2, replica_groups=mesh['rows'=2,'hidden_0'=2,'hidden_1'=4,'latents_0'=16,'latents_1'=2] {'..., dimensions={0}, use_global_device_ids=true | all-gather | bytes 1376256 | tf_op jit(solution)/shard_map/all_gather | solution.py:31
  48.2 0.3 copy.27
  48.5 0.3 reshape.95
  48.8 1.5 fusion.22
  50.3 1.8 all-gather.1
  52.1 0.3 convolution_convert_fusion
  52.5 14.5 %all_to_all.55 = bf16[8,224,128]{2,1,0:T(8,128)(2,1)S(1)} all-to-all(bf16[8,224,128]{2,1,0:T(8,128)(2,1)S(1)} %bitcast.70), channel_id=1, replica_groups=mesh['rows'=2,'hidden_0'=2,'hidden_1'=4,'latents_0'=16,'latents_1'=2] {'..., dimensions={0} | all-to-all | bytes 917504 | tf_op jit(solution)/shard_map/all_to_all | solution.py:23
  67.0 0.1 reduce_sum.65
  67.0 0.0 copy-start.6
  67.0 0.1 copy.28
  67.2 15.7 %all_to_all.56 = bf16[16,8,224]{2,1,0:T(8,128)(2,1)S(1)} all-to-all(bf16[16,8,224]{2,1,0:T(8,128)(2,1)S(1)} %bitcast.78), channel_id=1, replica_groups=mesh['rows'=2,'hidden_0'=2,'hidden_1'=4,'latents_0'=16,'latents_1'=2] {'..., dimensions={0} | all-to-all | bytes 114688 | tf_op jit(solution)/shard_map/all_to_all | solution.py:23
  82.9 18.5 %all_to_all.57 = bf16[32,8,224]{2,1,0:T(8,128)(2,1)S(1)} all-to-all(bf16[32,8,224]{2,1,0:T(8,128)(2,1)S(1)} %broadcast_in_dim.24), channel_id=1, replica_groups=mesh['rows'=2,'hidden_0'=2,'hidden_1'=4,'latents_0'=16,'latents_1'=2] {'..., dimensions={0} | all-to-all | bytes 229376 | tf_op jit(solution)/shard_map/all_to_all | solution.py:23
  101.4 0.1 copy.29
  101.5 2.0 all_gather.32
  103.5 0.0 copy-done.7
  103.5 0.3 convolution_convert_fusion.6
  103.8 0.3 convolution_convert_fusion.7
  104.1 0.5 convolution_convert_fusion.4
  104.5 0.0 copy-start.4
  104.6 15.1 %all_to_all.58 = bf16[8,32,1024]{2,1,0:T(8,128)(2,1)S(1)} all-to-all(bf16[8,32,1024]{2,1,0:T(8,128)(2,1)S(1)} %bitcast.72), channel_id=1, replica_groups=mesh['rows'=2,'hidden_0'=2,'hidden_1'=4,'latents_0'=16,'latents_1'=2] {'..., dimensions={0} | all-to-all | bytes 1048576 | tf_op jit(solution)/shard_map/all_to_all | solution.py:23
  119.6 0.1 convert_reduce_fusion.1
  119.7 0.1 fusion.3
  119.8 0.1 broadcast_in_dim.25
  119.9 13.7 %all_to_all.59 = bf16[8,32,1024]{2,1,0:T(8,128)(2,1)S(1)} all-to-all(bf16[8,32,1024]{2,1,0:T(8,128)(2,1)S(1)} %broadcast_in_dim.25), channel_id=1, replica_groups=mesh['rows'=2,'hidden_0'=2,'hidden_1'=4,'latents_0'=16,'latents_1'=2] {'..., dimensions={0} | all-to-all | bytes 1048576 | tf_op jit(solution)/shard_map/all_to_all | solution.py:23
  133.6 0.4 fusion
  134.1 0.0 copy-start.5
  134.1 2.1 all-gather.2
  136.3 0.8 copy.30
  137.0 3.9 %all-to-all-start.7 = ((bf16[32,8,224]{2,1,0:T(8,128)(2,1)}), bf16[32,8,224]{2,1,0:T(8,128)(2,1)S(1)}, u32[]{:S(2)}, u32[]{:S(2)}) async-start(bf16[32,8,224]{2,1,0:T(8,128)(2,1)} %bitcast.16), calls=%async_computation.7 | async-start | bytes 262144 | tf_op jit(solution)/shard_map/all_to_all | solution.py:23
  140.9 0.1 reshape.103
  141.0 0.1 fusion.6
  141.1 0.1 copy.39
  141.2 17.1 %all-to-all-done.7 = bf16[32,8,224]{2,1,0:T(8,128)(2,1)S(1)} async-done(((bf16[32,8,224]{2,1,0:T(8,128)(2,1)}), bf16[32,8,224]{2,1,0:T(8,128)(2,1)S(1)}, u32[]{:S(2)}, u32[]{:S(2)}) %all-to-all-start.7) | async-done | bytes 114720 | tf_op jit(solution)/shard_map/all_to_all | solution.py:23
  158.4 19.2 %all_to_all.60 = bf16[32,8,224]{2,1,0:T(8,128)(2,1)S(1)} all-to-all(bf16[32,8,224]{2,1,0:T(8,128)(2,1)S(1)} %broadcast_in_dim.26), channel_id=1, replica_groups=mesh['rows'=2,'hidden_0'=2,'hidden_1'=4,'latents_0'=16,'latents_1'=2] {'..., dimensions={0} | all-to-all | bytes 229376 | tf_op jit(solution)/shard_map/all_to_all | solution.py:23
  177.5 0.1 copy.33
  177.7 2.0 all_gather.36
  179.6 1.3 convolution_convert_fusion.3
  180.9 5.5 %all-to-all-start.9 = ((bf16[8,32,1024]{2,1,0:T(8,128)(2,1)}), bf16[8,32,1024]{2,1,0:T(8,128)(2,1)S(1)}, u32[]{:S(2)}, u32[]{:S(2)}) async-start(bf16[8,32,1024]{2,1,0:T(8,128)(2,1)} %bitcast.27), calls=%async_computation.9 | async-start | bytes 1048576 | tf_op jit(solution)/shard_map/all_to_all | solution.py:23
  186.5 9.7 %all-to-all-done.9 = bf16[8,32,1024]{2,1,0:T(8,128)(2,1)S(1)} async-done(((bf16[8,32,1024]{2,1,0:T(8,128)(2,1)}), bf16[8,32,1024]{2,1,0:T(8,128)(2,1)S(1)}, u32[]{:S(2)}, u32[]{:S(2)}) %all-to-all-start.9) | async-done | bytes 524320 | tf_op jit(solution)/shard_map/all_to_all | solution.py:23
  196.2 0.1 convert_reduce_fusion
  196.2 0.1 multiply_convert_fusion
  196.3 0.9 broadcast_in_dim.27
  197.2 5.9 %all-to-all-start.10 = ((bf16[8,32,1024]{2,1,0:T(8,128)(2,1)}), bf16[8,32,1024]{2,1,0:T(8,128)(2,1)S(1)}, u32[]{:S(2)}, u32[]{:S(2)}) async-start(bf16[8,32,1024]{2,1,0:T(8,128)(2,1)} %broadcast_in_dim.27), calls=%async_computation.10 | async-start | bytes 1048576 | tf_op jit(solution)/shard_map/all_to_all | solution.py:23
  203.1 1.8 all_gather.35
  204.9 0.7 reshape.105
  205.6 1.3 convolution_convert_fusion.1
  206.9 5.6 %all-to-all-done.10 = bf16[8,32,1024]{2,1,0:T(8,128)(2,1)S(1)} async-done(((bf16[8,32,1024]{2,1,0:T(8,128)(2,1)}), bf16[8,32,1024]{2,1,0:T(8,128)(2,1)S(1)}, u32[]{:S(2)}, u32[]{:S(2)}) %all-to-all-start.10) | async-done | bytes 524320 | tf_op jit(solution)/shard_map/all_to_all | solution.py:23
  212.5 1.3 convolution_convert_fusion.2
  (26 shorter events, 0.3 us)
Async XLA Ops:
  0.6 133.0 %copy-start = (bf16[1024,448]{0,1:T(8,128)(2,1)S(1)}, bf16[1024,448]{0,1:T(8,128)(2,1)}, u32[]{:S(2)}) copy-start(bf16[1024,448]{0,1:T(8,128)(2,1)} %param.14) | copy-start | bytes 2752516
  0.6 37.6 %copy-start.3 = (bf16[56,3584]{1,0:T(8,128)(2,1)S(1)}, bf16[56,3584]{1,0:T(8,128)(2,1)}, u32[]{:S(2)}) copy-start(bf16[56,3584]{1,0:T(8,128)(2,1)} %param.12) | copy-start | bytes 1204228
  2.1 27.9 %all-to-all-start = ((bf16[16,14,128]{2,1,0:T(8,128)(2,1)}), bf16[16,14,128]{2,1,0:T(8,128)(2,1)S(1)}, u32[]{:S(2)}, u32[]{:S(2)}) async-start(bf16[16,14,128]{2,1,0:T(8,128)(2,1)} %broadcast_in_dim.22), calls=%async_computation | async-start | bytes 131072 | tf_op jit(solution)/shard_map/all_to_all | solution.py:23
  30.9 14.9 %all-to-all-start.1 = ((bf16[8,16,14,128]{3,1,2,0:T(8,128)(2,1)}), bf16[8,16,14,128]{3,1,2,0:T(8,128)(2,1)S(1)}, u32[]{:S(2)}, u32[]{:S(2)}) async-start(bf16[8,16,14,128]{3,1,2,0:T(8,128)(2,1)} %broadcast_in_dim.23), calls=%async_computation.1 | async-start | bytes 917504 | tf_op jit(solution)/shard_map/all_to_all | solution.py:23
  39.0 3.0 %copy-start.1 = (bf16[3584,56]{0,1:T(8,128)(2,1)S(1)}, bf16[3584,56]{0,1:T(8,128)(2,1)}, u32[]{:S(2)}) copy-start(bf16[3584,56]{0,1:T(8,128)(2,1)} %param.11) | copy-start | bytes 1204228
  39.0 3.0 %copy-start.2 = (bf16[3584,56]{0,1:T(8,128)(2,1)S(1)}, bf16[3584,56]{0,1:T(8,128)(2,1)}, u32[]{:S(2)}) copy-start(bf16[3584,56]{0,1:T(8,128)(2,1)} %param.10) | copy-start | bytes 1204228
  40.0 3.4 %collective-permute-start = (bf16[56,8,224]{2,1,0:T(8,128)(2,1)S(1)}, bf16[56,8,224]{2,1,0:T(8,128)(2,1)S(1)}, u32[]{:S(2)}, u32[]{:S(2)}) collective-permute-start(bf16[56,8,224]{2,1,0:T(8,128)(2,1)S(1)} %bitcast.81), channel_id=1, source_target_pairs={{0,1},{1,0},{2,3},{3,2},{4,5},{5,4},{6,7},{7,6},{8,9},{9,8},{10,11... | collective-permute-start | bytes 602120 | tf_op jit(solution)/shard_map/ppermute | solution.py:35
  67.0 36.5 %copy-start.7 = (s32[256]{0:T(256)S(1)}, s32[256]{0:T(256)}, u32[]{:S(2)}) copy-start(s32[256]{0:T(256)} %param.17) | copy-start | bytes 3076
  67.0 37.0 %copy-start.6 = (bf16[448,1024]{1,0:T(8,128)(2,1)S(1)}, bf16[448,1024]{1,0:T(8,128)(2,1)}, u32[]{:S(2)}) copy-start(bf16[448,1024]{1,0:T(8,128)(2,1)} %param.13) | copy-start | bytes 2752516
  104.5 15.2 %copy-start.4 = (f32[1024]{0:T(1024)S(1)}, f32[1024]{0:T(1024)}, u32[]{:S(2)}) copy-start(f32[1024]{0:T(1024)} %param.15) | copy-start | bytes 12292
  134.1 6.8 %copy-start.5 = (f32[448]{0:T(512)S(1)}, f32[448]{0:T(512)}, u32[]{:S(2)}) copy-start(f32[448]{0:T(512)} %param.16) | copy-start | bytes 5380
  137.0 21.3 %all-to-all-start.7 = ((bf16[32,8,224]{2,1,0:T(8,128)(2,1)}), bf16[32,8,224]{2,1,0:T(8,128)(2,1)S(1)}, u32[]{:S(2)}, u32[]{:S(2)}) async-start(bf16[32,8,224]{2,1,0:T(8,128)(2,1)} %bitcast.16), calls=%async_computation.7 | async-start | bytes 262144 | tf_op jit(solution)/shard_map/all_to_all | solution.py:23
  180.9 15.3 %all-to-all-start.9 = ((bf16[8,32,1024]{2,1,0:T(8,128)(2,1)}), bf16[8,32,1024]{2,1,0:T(8,128)(2,1)S(1)}, u32[]{:S(2)}, u32[]{:S(2)}) async-start(bf16[8,32,1024]{2,1,0:T(8,128)(2,1)} %bitcast.27), calls=%async_computation.9 | async-start | bytes 1048576 | tf_op jit(solution)/shard_map/all_to_all | solution.py:23
  197.2 15.4 %all-to-all-start.10 = ((bf16[8,32,1024]{2,1,0:T(8,128)(2,1)}), bf16[8,32,1024]{2,1,0:T(8,128)(2,1)S(1)}, u32[]{:S(2)}, u32[]{:S(2)}) async-start(bf16[8,32,1024]{2,1,0:T(8,128)(2,1)} %broadcast_in_dim.27), calls=%async_computation.10 | async-start | bytes 1048576 | tf_op jit(solution)/shard_map/all_to_all | solution.py:23

commit v4 on v3

--- a/solution.py
+++ b/solution.py
@@ -12,6 +12,7 @@
 HIDDEN_LATENTS = (Y, X, Z, C)
 ROWS_LATENTS = (R, Z, C)
 ROWS_Z = (R, Z)
+ROWS_HIDDEN = (R, Y, X)
 
 smooth_scale = 0.1
 sparsity_weight = 0.5
@@ -31,8 +32,8 @@
     return lax.all_gather(x, C, axis=0, tiled=False)
 
 
-def swapped(x):
-    return lax.ppermute(x, C, [(0, 1), (1, 0)])
+def swapped(x, axis):
+    return lax.ppermute(x, axis, [(0, 1), (1, 0)])
 
 
 def total(blocks):
@@ -49,8 +50,8 @@
     tokens = shuffle_order.shape[0]
     n_hidden = lax.axis_size(HIDDEN)
     n_z = lax.axis_size(Z)
-    n_rows_z = lax.axis_size(ROWS_Z)
     core = lax.axis_index(C)
+    row = lax.axis_index(R)
     width = decoder.shape[1]
     half = width // 2
     latents = encoder.shape[1]
@@ -62,7 +63,7 @@
     few, down = lax.optimization_barrier((few, down_weight))
     blocks = down.reshape(units, n_hidden, 2, half)
     kept, given = own(blocks, core, 2), own(blocks, 1 - core, 2)
-    taken = swapped(given)
+    taken = swapped(given, C)
     down_pair = jnp.concatenate(
         [jnp.where(core == 0, kept, taken), jnp.where(core == 0, taken, kept)]
     ).reshape(2 * units, n_hidden * half)
@@ -77,51 +78,84 @@
     ).astype(BF16).reshape(n_hidden, half, -1)
 
     summed = total(exchange(mine, HIDDEN)).T.astype(BF16)
+
+    summed, decoder_own, bias_own = lax.optimization_barrier((summed, decoder, enc_bias))
+    decoder_far, bias_far = swapped(decoder_own, R), swapped(bias_own, R)
+
     rows_own = total(exchange(summed.reshape(n_z, -1, half), Z)).astype(BF16)
-    mlp_out = both_cores(sent_to_all(rows_own, ROWS_Z).reshape(tokens, half))
+    rows_all = sent_to_all(rows_own, ROWS_Z)
+    rows_all, decoder_far, bias_far = lax.optimization_barrier((rows_all, decoder_far, bias_far))
+    mlp_out = both_cores(rows_all.reshape(tokens, half))
+    decoder_both = jnp.concatenate([decoder_own, decoder_far])
+    bias_both = jnp.concatenate([bias_own, bias_far])
+    low = row == 0
 
     pick = (shuffle_order[:, None] == jnp.arange(tokens)[None, :]).astype(BF16)
     shuffled = jnp.concatenate(
         [jnp.dot(pick, mlp_out[c], preferred_element_type=F32).astype(BF16) for c in range(2)],
         axis=1,
     )
-    shuffled_t = lax.optimization_barrier(shuffled.T)
+
+    group = tokens // 2
     pre_local = jnp.dot(shuffled, encoder, preferred_element_type=F32).astype(BF16)
-    pre_act = total(exchange(pre_local.reshape(n_hidden, -1, latents), HIDDEN)) + enc_bias[None, :]
+    pre_parts = exchange(pre_local.reshape(2 * n_hidden, -1, latents), ROWS_HIDDEN)
+    pre_sums = jnp.sum(pre_parts.reshape(2, n_hidden, -1, latents).astype(F32), axis=1)
+    pre_act = jnp.concatenate(
+        [jnp.where(low, *pre_sums), jnp.where(low, pre_sums[1], pre_sums[0])], axis=1
+    ) + bias_both[None, :]
     latent_own = (smooth_scale * jax.nn.softplus(pre_act / smooth_scale)).astype(BF16)
-    latent_act = sent_to_all(latent_own, HIDDEN).reshape(tokens, latents)
-    recon_local = lax.dot_general(
-        decoder, latent_act, (((0,), (1,)), ((), ())), preferred_element_type=F32
-    ).astype(BF16)
-    recon_pair = both_cores(recon_local).reshape(2, 2, half, tokens)
-    recon_mine = total(own(recon_pair, core, 1)).T.astype(BF16).reshape(n_rows_z, -1, half)
-    bias_mine = own(dec_bias.reshape(2, half), core, 0)
-    recon = total(exchange(recon_mine, ROWS_Z)) + bias_mine[None, :]
-    count = recon.shape[0]
-    both_recon = both_cores(recon.astype(BF16)).reshape(2, 2, count // 2, half)
-    recon_out = own(both_recon, core, 1).transpose(1, 0, 2).reshape(count // 2, width)
-
+    latent_act = sent_to_all(latent_own, HIDDEN).reshape(group, 2 * latents)
     scale = 1.0 / math.sqrt(tokens)
+    count = group // n_z
     first = lax.axis_index(ROWS_Z) * count
     target = own(
         lax.dynamic_slice_in_dim(shuffled, first, count, 0).reshape(count, 2, half), core, 1
     )
+    bias_mine = own(dec_bias.reshape(2, half), core, 0)
+    latent_act, decoder_both, target, bias_mine = lax.optimization_barrier(
+        (latent_act, decoder_both, target, bias_mine)
+    )
+    recon_local = lax.dot_general(
+        decoder_both, latent_act, (((0,), (1,)), ((), ())), preferred_element_type=F32
+    ).astype(BF16)
+    recon_pair = both_cores(recon_local).reshape(2, 2, half, group)
+    recon_mine = total(own(recon_pair, core, 1)).T.astype(BF16).reshape(n_z, -1, half)
+    recon = total(exchange(recon_mine, Z)) + bias_mine[None, :]
     err_own = (scale * (recon - target.astype(F32))).astype(BF16)
-    err_pair = both_cores(sent_to_all(err_own, ROWS_Z).reshape(tokens, half))
+    err_pair = both_cores(sent_to_all(err_own, Z).reshape(group, half))
     d_err = jnp.concatenate([err_pair[0], err_pair[1]], axis=1)
 
     back_local = lax.dot_general(
-        d_err, decoder, (((1,), (1,)), ((), ())), preferred_element_type=F32
+        d_err, decoder_both, (((1,), (1,)), ((), ())), preferred_element_type=F32
     ).astype(BF16)
-    d_latent = total(exchange(back_local.reshape(n_hidden, -1, latents), HIDDEN))
-    grad_dec = lax.dot_general(
-        latent_act, d_err, (((0,), (0,)), ((), ())), preferred_element_type=F32
-    ).astype(BF16)
+    d_latent = total(exchange(back_local.reshape(n_hidden, -1, 2 * latents), HIDDEN))
     d_pre_own = (
         (d_latent + sparsity_weight * scale) * jax.nn.sigmoid(pre_act / smooth_scale)
     ).astype(BF16)
-    d_pre = sent_to_all(d_pre_own, HIDDEN).reshape(tokens, latents)
-    grad_enc = jnp.dot(shuffled_t, d_pre, preferred_element_type=F32).astype(BF16)
+    d_pre_near, d_pre_far = d_pre_own[:, :latents], d_pre_own[:, latents:]
+    d_pre_cut = jnp.stack(
+        [jnp.where(low, d_pre_near, d_pre_far), jnp.where(low, d_pre_far, d_pre_near)]
+    )
+    d_pre = exchange(
+        jnp.broadcast_to(d_pre_cut[:, None], (2, n_hidden, *d_pre_cut.shape[1:])).reshape(
+            2 * n_hidden, -1, latents
+        ),
+        ROWS_HIDDEN,
+    ).reshape(tokens, latents)
+
+    latent_all = jnp.concatenate(
+        [latent_act[:, :latents], swapped(latent_act[:, latents:], R)]
+    )
+    err_all = jnp.concatenate([d_err, swapped(d_err, R)])
+    grad_dec = lax.dot_general(
+        latent_all, err_all, (((0,), (0,)), ((), ())), preferred_element_type=F32
+    ).astype(BF16)
+    grad_enc = lax.dot_general(
+        shuffled, d_pre, (((0,), (0,)), ((), ())), preferred_element_type=F32
+    ).astype(BF16)
+
+    both_recon = both_cores(recon.astype(BF16)).reshape(2, 2, count // 2, half)
+    recon_out = own(both_recon, core, 1).transpose(1, 0, 2).reshape(count // 2, width)
     return (recon_out, grad_enc, grad_dec)
 
 

time: 217 us -> 222 us (1.023)
  blocking collectives: 109 us -> 73.3 us
  starting transfers between devices: 39.8 us -> 63.4 us
  waiting for transfers between devices: 47.4 us -> 60.2 us
    all_to_all x6 -> x4, blocking collectives: 96.7 us -> 61.3 us  [exchange(): return lax.all_to_all(blocks, axes, 0, 0, tiled=True)]
    ppermute x1 -> x5, starting transfers between devices: 1.92 us -> 13.9 us  [swapped(): return lax.ppermute(x, axis, [(0, 1), (1, 0)])]
    all_to_all x5 -> x7, starting transfers between devices: 37.9 us -> 49.5 us  [exchange(): return lax.all_to_all(blocks, axes, 0, 0, tiled=True)]
    all_to_all x5 -> x7, waiting for transfers between devices: 46.9 us -> 54.4 us  [exchange(): return lax.all_to_all(blocks, axes, 0, 0, tiled=True)]
    ppermute x1 -> x5, waiting for transfers between devices: 0.5 us -> 5.88 us  [swapped(): return lax.ppermute(x, axis, [(0, 1), (1, 0)])]
  transfers between devices with their start and end apart: 6 -> 12, of which waited for: 6 -> 8; matrix products, arithmetic and copies ran while one was open for 3% -> 4% of each run, Pallas kernels for 0% -> 0%
where the time goes in v4:
time: 222 us; the launch traced here: 219 us
  blocking collectives  73.3 us (33%)
  starting transfers between devices  63.4 us (29%)
  waiting for transfers between devices  60.2 us (27%)
  local copies, waits for them, and re-layouts  9.74 us (4%)
  matrix products  8.3 us (4%)
  other arithmetic  3.28 us (1%)
    all_to_all x4, blocking collectives, exchange(): return lax.all_to_all(blocks, axes, 0, 0, tiled=True)  61.3 us
    all_to_all x7, waiting for transfers between devices, exchange(): return lax.all_to_all(blocks, axes, 0, 0, tiled=True)  54.4 us
    all_to_all x7, starting transfers between devices, exchange(): return lax.all_to_all(blocks, axes, 0, 0, tiled=True)  49.5 us
    ppermute x5, starting transfers between devices, swapped(): return lax.ppermute(x, axis, [(0, 1), (1, 0)])  13.9 us
    all_gather x6, blocking collectives, both_cores(): return lax.all_gather(x, C, axis=0, tiled=False)  12 us
    ppermute x5, waiting for transfers between devices, swapped(): return lax.ppermute(x, axis, [(0, 1), (1, 0)])  5.88 us
  transfers between devices with their start and end apart: 12, of which 8 were waited for; matrix products, arithmetic and copies ran while one was open for 4% of the time, Pallas kernels for 0%

profile of v4, /device:TPU:6, one launch (start us, length us, event | category | flops | bytes accessed | tf_op | source)
XLA Modules:
  0.0 219.3 jit_solution(11662844928498559465)
XLA Ops:
  0.6 1.4 broadcast_in_dim.12
  2.1 15.2 %all-to-all-start = ((bf16[16,14,128]{2,1,0:T(8,128)(2,1)}), bf16[16,14,128]{2,1,0:T(8,128)(2,1)S(1)}, u32[]{:S(2)}, u32[]{:S(2)}) async-start(bf16[16,14,128]{2,1,0:T(8,128)(2,1)} %broadcast_in_dim.12), calls=%async_computation | async-start | bytes 131072 | tf_op jit(solution)/shard_map/all_to_all | solution.py:24
  17.3 12.7 %all-to-all-done = bf16[16,14,128]{2,1,0:T(8,128)(2,1)S(1)} async-done(((bf16[16,14,128]{2,1,0:T(8,128)(2,1)}), bf16[16,14,128]{2,1,0:T(8,128)(2,1)S(1)}, u32[]{:S(2)}, u32[]{:S(2)}) %all-to-all-start) | async-done | bytes 57376 | tf_op jit(solution)/shard_map/all_to_all | solution.py:24
  30.0 1.7 reshape.100
  31.7 1.0 constant_dynamic-slice_fusion.3
  32.7 1.9 collective-permute-start
  34.7 0.8 broadcast_in_dim.26
  35.5 7.4 %all-to-all-start.1 = ((bf16[8,16,14,128]{3,1,2,0:T(8,128)(2,1)}), bf16[8,16,14,128]{3,1,2,0:T(8,128)(2,1)S(1)}, u32[]{:S(2)}, u32[]{:S(2)}) async-start(bf16[8,16,14,128]{3,1,2,0:T(8,128)(2,1)} %broadcast_in_dim.26), calls=%async_computation.1 | async-start | bytes 917504 | tf_op jit(solution)/shard_map/all_to_all | solution.py:24
  42.9 0.9 pad_maximum_fusion.1
  43.9 0.1 pad_maximum_fusion.2
  44.0 0.5 reshape.101
  44.5 7.6 %all-to-all-done.1 = bf16[8,16,14,128]{3,1,2,0:T(8,128)(2,1)S(1)} async-done(((bf16[8,16,14,128]{3,1,2,0:T(8,128)(2,1)}), bf16[8,16,14,128]{3,1,2,0:T(8,128)(2,1)S(1)}, u32[]{:S(2)}, u32[]{:S(2)}) %all-to-all-start.1) | async-done | bytes 458784 | tf_op jit(solution)/shard_map/all_to_all | solution.py:24
  52.1 2.5 %all-gather = bf16[16,16,14,128]{3,1,2,0:T(8,128)(2,1)S(1)} all-gather(bf16[8,16,14,128]{3,1,2,0:T(8,128)(2,1)S(1)} %all-to-all-done.1), channel_id=2, replica_groups=mesh['rows'=2,'hidden_0'=2,'hidden_1'=4,'latents_0'=16,'latents_1'=2] {'..., dimensions={0}, use_global_device_ids=true | all-gather | bytes 1376256 | tf_op jit(solution)/shard_map/all_gather | solution.py:32
  54.5 0.3 copy.31
  54.8 0.3 reshape.102
  55.1 1.6 fusion.28
  56.7 1.8 all-gather.1
  58.5 0.3 convolution_convert_fusion.1
  58.9 14.3 %all_to_all.55 = bf16[8,224,128]{2,1,0:T(8,128)(2,1)S(1)} all-to-all(bf16[8,224,128]{2,1,0:T(8,128)(2,1)S(1)} %bitcast.74), channel_id=1, replica_groups=mesh['rows'=2,'hidden_0'=2,'hidden_1'=4,'latents_0'=16,'latents_1'=2] {'..., dimensions={0} | all-to-all | bytes 917504 | tf_op jit(solution)/shard_map/all_to_all | solution.py:24
  73.1 0.1 reduce_sum.65
  73.2 2.6 %collective-permute-start.1 = (bf16[1024,448]{0,1:T(8,128)(2,1)S(1)}, bf16[1024,448]{0,1:T(8,128)(2,1)S(1)}, u32[]{:S(2)}, u32[]{:S(2)}) collective-permute-start(bf16[1024,448]{0,1:T(8,128)(2,1)S(1)} %copy-done.1), channel_id=1, source_target_pairs={{0,256},{256,0},{1,257},{257,1},{2,258},{258,2},{3,259},{259,3},{4... | collective-permute-start | bytes 2752520 | tf_op jit(solution)/shard_map/ppermute | solution.py:36
  75.8 0.1 copy.32
  75.9 15.6 %all_to_all.56 = bf16[16,8,224]{2,1,0:T(8,128)(2,1)S(1)} all-to-all(bf16[16,8,224]{2,1,0:T(8,128)(2,1)S(1)} %bitcast.79), channel_id=1, replica_groups=mesh['rows'=2,'hidden_0'=2,'hidden_1'=4,'latents_0'=16,'latents_1'=2] {'..., dimensions={0} | all-to-all | bytes 114688 | tf_op jit(solution)/shard_map/all_to_all | solution.py:24
  91.6 0.7 broadcast_in_dim.27
  92.2 4.0 %all-to-all-start.4 = ((bf16[32,8,224]{2,1,0:T(8,128)(2,1)}), bf16[32,8,224]{2,1,0:T(8,128)(2,1)S(1)}, u32[]{:S(2)}, u32[]{:S(2)}) async-start(bf16[32,8,224]{2,1,0:T(8,128)(2,1)} %broadcast_in_dim.27), calls=%async_computation.4 | async-start | bytes 262144 | tf_op jit(solution)/shard_map/all_to_all | solution.py:24
  96.2 3.7 %collective-permute-start.2 = (f32[1024]{0:T(1024)S(1)}, f32[1024]{0:T(1024)S(1)}, u32[]{:S(2)}, u32[]{:S(2)}) collective-permute-start(f32[1024]{0:T(1024)S(1)} %copy-done.9), channel_id=1, source_target_pairs={{0,256},{256,0},{1,257},{257,1},{2,258},{258,2},{3,259},{259,3},{4... | collective-permute-start | bytes 12296 | tf_op jit(solution)/shard_map/ppermute | solution.py:36
  99.9 1.8 collective-permute-done.2
  101.7 10.0 %all-to-all-done.4 = bf16[32,8,224]{2,1,0:T(8,128)(2,1)S(1)} async-done(((bf16[32,8,224]{2,1,0:T(8,128)(2,1)}), bf16[32,8,224]{2,1,0:T(8,128)(2,1)S(1)}, u32[]{:S(2)}, u32[]{:S(2)}) %all-to-all-start.4) | async-done | bytes 114720 | tf_op jit(solution)/shard_map/all_to_all | solution.py:24
  111.7 0.1 copy.33
  111.9 2.1 all_gather.32
  114.0 0.3 convolution_convert_fusion.6
  114.3 0.3 convolution_convert_fusion.7
  114.6 1.3 convolution_convert_fusion.4
  115.9 5.3 %all-to-all-start.5 = ((bf16[16,16,1024]{2,1,0:T(8,128)(2,1)}), bf16[16,16,1024]{2,1,0:T(8,128)(2,1)S(1)}, u32[]{:S(2)}, u32[]{:S(2)}) async-start(bf16[16,16,1024]{2,1,0:T(8,128)(2,1)} %bitcast.11), calls=%async_computation.5 | async-start | bytes 1048576 | tf_op jit(solution)/shard_map/all_to_all | solution.py:24
  121.1 0.1 reshape.109
  121.2 9.6 %all-to-all-done.5 = bf16[16,16,1024]{2,1,0:T(8,128)(2,1)S(1)} async-done(((bf16[16,16,1024]{2,1,0:T(8,128)(2,1)}), bf16[16,16,1024]{2,1,0:T(8,128)(2,1)S(1)}, u32[]{:S(2)}, u32[]{:S(2)}) %all-to-all-start.5) | async-done | bytes 524320 | tf_op jit(solution)/shard_map/all_to_all | solution.py:24
  130.8 0.1 convert_reduce_fusion
  130.9 0.1 fusion.9
  131.0 0.8 broadcast_in_dim.28
  131.9 5.9 %all-to-all-start.6 = ((bf16[8,16,2048]{2,1,0:T(8,128)(2,1)}), bf16[8,16,2048]{2,1,0:T(8,128)(2,1)S(1)}, u32[]{:S(2)}, u32[]{:S(2)}) async-start(bf16[8,16,2048]{2,1,0:T(8,128)(2,1)} %broadcast_in_dim.28), calls=%async_computation.6 | async-start | bytes 1048576 | tf_op jit(solution)/shard_map/all_to_all | solution.py:24
  137.8 0.1 fusion.13
  138.0 0.1 copy.42
  138.0 1.6 pad_maximum_fusion
  139.7 7.0 %all-to-all-done.6 = bf16[8,16,2048]{2,1,0:T(8,128)(2,1)S(1)} async-done(((bf16[8,16,2048]{2,1,0:T(8,128)(2,1)}), bf16[8,16,2048]{2,1,0:T(8,128)(2,1)S(1)}, u32[]{:S(2)}, u32[]{:S(2)}) %all-to-all-start.6) | async-done | bytes 524320 | tf_op jit(solution)/shard_map/all_to_all | solution.py:24
  146.7 0.6 convolution_convert_fusion.5
  147.3 2.0 all-gather.2
  149.3 0.1 copy.35
  149.4 15.9 %all_to_all.57 = bf16[16,8,224]{2,1,0:T(8,128)(2,1)S(1)} all-to-all(bf16[16,8,224]{2,1,0:T(8,128)(2,1)S(1)} %bitcast.80), channel_id=1, replica_groups=mesh['rows'=2,'hidden_0'=2,'hidden_1'=4,'latents_0'=16,'latents_1'=2] {'..., dimensions={0} | all-to-all | bytes 114688 | tf_op jit(solution)/shard_map/all_to_all | solution.py:24
  165.4 15.5 %all_to_all.58 = bf16[16,8,224]{2,1,0:T(8,128)(2,1)S(1)} all-to-all(bf16[16,8,224]{2,1,0:T(8,128)(2,1)S(1)} %broadcast_in_dim.29), channel_id=1, replica_groups=mesh['rows'=2,'hidden_0'=2,'hidden_1'=4,'latents_0'=16,'latents_1'=2] {'..., dimensions={0} | all-to-all | bytes 114688 | tf_op jit(solution)/shard_map/all_to_all | solution.py:24
  180.9 0.1 copy.38
  181.0 1.9 all_gather.36
  182.9 1.3 convolution_convert_fusion
  184.2 5.8 %all-to-all-start.9 = ((bf16[8,16,2048]{2,1,0:T(8,128)(2,1)}), bf16[8,16,2048]{2,1,0:T(8,128)(2,1)S(1)}, u32[]{:S(2)}, u32[]{:S(2)}) async-start(bf16[8,16,2048]{2,1,0:T(8,128)(2,1)} %bitcast.73), calls=%async_computation.9 | async-start | bytes 1048576 | tf_op jit(solution)/shard_map/all_to_all | solution.py:24
  190.0 2.2 %collective-permute-start.3 = (bf16[128,1024]{1,0:T(8,128)(2,1)S(1)}, bf16[128,1024]{1,0:T(8,128)(2,1)S(1)}, u32[]{:S(2)}, u32[]{:S(2)}) collective-permute-start(bf16[128,1024]{1,0:T(8,128)(2,1)S(1)} %get-tuple-element.30), channel_id=1, source_target_pairs={{0,256},{256,0},{1,257},{257,1},{2,258},{258,2},{3,259},{259,3},{4... | collective-permute-start | bytes 786440 | tf_op jit(solution)/shard_map/ppermute | solution.py:36
  192.2 7.5 %all-to-all-done.9 = bf16[8,16,2048]{2,1,0:T(8,128)(2,1)S(1)} async-done(((bf16[8,16,2048]{2,1,0:T(8,128)(2,1)}), bf16[8,16,2048]{2,1,0:T(8,128)(2,1)S(1)}, u32[]{:S(2)}, u32[]{:S(2)}) %all-to-all-start.9) | async-done | bytes 524320 | tf_op jit(solution)/shard_map/all_to_all | solution.py:24
  199.7 0.1 convert_reduce_fusion.1
  199.8 0.9 broadcast_in_dim.30
  200.7 5.9 %all-to-all-start.10 = ((bf16[16,16,1024]{2,1,0:T(8,128)(2,1)}), bf16[16,16,1024]{2,1,0:T(8,128)(2,1)S(1)}, u32[]{:S(2)}, u32[]{:S(2)}) async-start(bf16[16,16,1024]{2,1,0:T(8,128)(2,1)} %bitcast.30), calls=%async_computation.10 | async-start | bytes 1048576 | tf_op jit(solution)/shard_map/all_to_all | solution.py:24
  206.6 3.4 %collective-permute-start.4 = (bf16[128,448]{0,1:T(8,128)(2,1)S(1)}, bf16[128,448]{0,1:T(8,128)(2,1)S(1)}, u32[]{:S(2)}, u32[]{:S(2)}) collective-permute-start(bf16[128,448]{0,1:T(8,128)(2,1)S(1)} %pad_maximum_fusion.6), channel_id=1, source_target_pairs={{0,256},{256,0},{1,257},{257,1},{2,258},{258,2},{3,259},{259,3},{4... | collective-permute-start | bytes 344072 | tf_op jit(solution)/shard_map/ppermute | solution.py:36
  210.1 1.8 all_gather.35
  211.9 0.7 reshape.113
  212.6 4.1 %collective-permute-done.4 = bf16[128,448]{0,1:T(8,128)(2,1)S(1)} collective-permute-done((bf16[128,448]{0,1:T(8,128)(2,1)S(1)}, bf16[128,448]{0,1:T(8,128)(2,1)S(1)}, u32[]{:S(2)}, u32[]{:S(2)}) %collective-permute-start.4) | collective-permute-done | bytes 114720 | tf_op jit(solution)/shard_map/ppermute | solution.py:36
  216.7 1.3 convolution_convert_fusion.2
  218.0 1.3 convolution_convert_fusion.3
  (51 shorter events, 0.5 us)
Async XLA Ops:
  0.6 113.9 %copy-start = (bf16[448,1024]{1,0:T(8,128)(2,1)S(1)}, bf16[448,1024]{1,0:T(8,128)(2,1)}, u32[]{:S(2)}) copy-start(bf16[448,1024]{1,0:T(8,128)(2,1)} %param.13) | copy-start | bytes 2752516
  2.1 27.9 %all-to-all-start = ((bf16[16,14,128]{2,1,0:T(8,128)(2,1)}), bf16[16,14,128]{2,1,0:T(8,128)(2,1)S(1)}, u32[]{:S(2)}, u32[]{:S(2)}) async-start(bf16[16,14,128]{2,1,0:T(8,128)(2,1)} %broadcast_in_dim.12), calls=%async_computation | async-start | bytes 131072 | tf_op jit(solution)/shard_map/all_to_all | solution.py:24
  31.7 11.2 %copy-start.7 = (bf16[3584,56]{0,1:T(8,128)(2,1)S(1)}, bf16[3584,56]{0,1:T(8,128)(2,1)}, u32[]{:S(2)}) copy-start(bf16[3584,56]{0,1:T(8,128)(2,1)} %param.11) | copy-start | bytes 1204228
  31.7 11.2 %copy-start.8 = (bf16[3584,56]{0,1:T(8,128)(2,1)S(1)}, bf16[3584,56]{0,1:T(8,128)(2,1)}, u32[]{:S(2)}) copy-start(bf16[3584,56]{0,1:T(8,128)(2,1)} %param.10) | copy-start | bytes 1204228
  32.7 11.1 %collective-permute-start = (bf16[56,8,224]{2,1,0:T(8,128)(2,1)S(1)}, bf16[56,8,224]{2,1,0:T(8,128)(2,1)S(1)}, u32[]{:S(2)}, u32[]{:S(2)}) collective-permute-start(bf16[56,8,224]{2,1,0:T(8,128)(2,1)S(1)} %bitcast.85), channel_id=1, source_target_pairs={{0,1},{1,0},{2,3},{3,2},{4,5},{5,4},{6,7},{7,6},{8,9},{9,8},{10,11... | collective-permute-start | bytes 602120 | tf_op jit(solution)/shard_map/ppermute | solution.py:36
  35.5 16.6 %all-to-all-start.1 = ((bf16[8,16,14,128]{3,1,2,0:T(8,128)(2,1)}), bf16[8,16,14,128]{3,1,2,0:T(8,128)(2,1)S(1)}, u32[]{:S(2)}, u32[]{:S(2)}) async-start(bf16[8,16,14,128]{3,1,2,0:T(8,128)(2,1)} %broadcast_in_dim.26), calls=%async_computation.1 | async-start | bytes 917504 | tf_op jit(solution)/shard_map/all_to_all | solution.py:24
  55.1 18.1 %copy-start.1 = (bf16[1024,448]{0,1:T(8,128)(2,1)S(1)}, bf16[1024,448]{0,1:T(8,128)(2,1)}, u32[]{:S(2)}) copy-start(bf16[1024,448]{0,1:T(8,128)(2,1)} %param.14) | copy-start | bytes 2752516
  56.7 39.6 %copy-start.9 = (f32[1024]{0:T(1024)S(1)}, f32[1024]{0:T(1024)}, u32[]{:S(2)}) copy-start(f32[1024]{0:T(1024)} %param.15) | copy-start | bytes 12292
  56.7 57.3 %copy-start.11 = (s32[256]{0:T(256)S(1)}, s32[256]{0:T(256)}, u32[]{:S(2)}) copy-start(s32[256]{0:T(256)} %param.17) | copy-start | bytes 3076
  73.2 38.6 %collective-permute-start.1 = (bf16[1024,448]{0,1:T(8,128)(2,1)S(1)}, bf16[1024,448]{0,1:T(8,128)(2,1)S(1)}, u32[]{:S(2)}, u32[]{:S(2)}) collective-permute-start(bf16[1024,448]{0,1:T(8,128)(2,1)S(1)} %copy-done.1), channel_id=1, source_target_pairs={{0,256},{256,0},{1,257},{257,1},{2,258},{258,2},{3,259},{259,3},{4... | collective-permute-start | bytes 2752520 | tf_op jit(solution)/shard_map/ppermute | solution.py:36
  92.2 19.5 %all-to-all-start.4 = ((bf16[32,8,224]{2,1,0:T(8,128)(2,1)}), bf16[32,8,224]{2,1,0:T(8,128)(2,1)S(1)}, u32[]{:S(2)}, u32[]{:S(2)}) async-start(bf16[32,8,224]{2,1,0:T(8,128)(2,1)} %broadcast_in_dim.27), calls=%async_computation.4 | async-start | bytes 262144 | tf_op jit(solution)/shard_map/all_to_all | solution.py:24
  96.2 5.5 %collective-permute-start.2 = (f32[1024]{0:T(1024)S(1)}, f32[1024]{0:T(1024)S(1)}, u32[]{:S(2)}, u32[]{:S(2)}) collective-permute-start(f32[1024]{0:T(1024)S(1)} %copy-done.9), channel_id=1, source_target_pairs={{0,256},{256,0},{1,257},{257,1},{2,258},{258,2},{3,259},{259,3},{4... | collective-permute-start | bytes 12296 | tf_op jit(solution)/shard_map/ppermute | solution.py:36
  111.7 26.2 %copy-start.2 = (bf16[1024,448]{0,1:T(8,128)(2,1)}, bf16[1024,448]{0,1:T(8,128)(2,1)S(1)}, u32[]{:S(2)}) copy-start(bf16[1024,448]{0,1:T(8,128)(2,1)S(1)} %collective-permute-done.1) | copy-start | bytes 2752516
  111.9 9.3 %copy-start.10 = (f32[448]{0:T(512)S(1)}, f32[448]{0:T(512)}, u32[]{:S(2)}) copy-start(f32[448]{0:T(512)} %param.16) | copy-start | bytes 5380
  114.3 23.6 %copy-start.3 = (bf16[256,224]{0,1:T(8,128)(2,1)}, bf16[256,224]{0,1:T(8,128)(2,1)S(1)}, u32[]{:S(2)}) copy-start(bf16[256,224]{0,1:T(8,128)(2,1)S(1)} %convolution_convert_fusion.6) | copy-start | bytes 344068
  114.6 23.3 %copy-start.5 = (bf16[256,224]{0,1:T(8,128)(2,1)}, bf16[256,224]{0,1:T(8,128)(2,1)S(1)}, u32[]{:S(2)}) copy-start(bf16[256,224]{0,1:T(8,128)(2,1)S(1)} %convolution_convert_fusion.7) | copy-start | bytes 344068
  115.9 15.0 %all-to-all-start.5 = ((bf16[16,16,1024]{2,1,0:T(8,128)(2,1)}), bf16[16,16,1024]{2,1,0:T(8,128)(2,1)S(1)}, u32[]{:S(2)}, u32[]{:S(2)}) async-start(bf16[16,16,1024]{2,1,0:T(8,128)(2,1)} %bitcast.11), calls=%async_computation.5 | async-start | bytes 1048576 | tf_op jit(solution)/shard_map/all_to_all | solution.py:24
  131.9 14.8 %all-to-all-start.6 = ((bf16[8,16,2048]{2,1,0:T(8,128)(2,1)}), bf16[8,16,2048]{2,1,0:T(8,128)(2,1)S(1)}, u32[]{:S(2)}, u32[]{:S(2)}) async-start(bf16[8,16,2048]{2,1,0:T(8,128)(2,1)} %broadcast_in_dim.28), calls=%async_computation.6 | async-start | bytes 1048576 | tf_op jit(solution)/shard_map/all_to_all | solution.py:24
  184.2 15.5 %all-to-all-start.9 = ((bf16[8,16,2048]{2,1,0:T(8,128)(2,1)}), bf16[8,16,2048]{2,1,0:T(8,128)(2,1)S(1)}, u32[]{:S(2)}, u32[]{:S(2)}) async-start(bf16[8,16,2048]{2,1,0:T(8,128)(2,1)} %bitcast.73), calls=%async_computation.9 | async-start | bytes 1048576 | tf_op jit(solution)/shard_map/all_to_all | solution.py:24
  190.0 22.6 %collective-permute-start.3 = (bf16[128,1024]{1,0:T(8,128)(2,1)S(1)}, bf16[128,1024]{1,0:T(8,128)(2,1)S(1)}, u32[]{:S(2)}, u32[]{:S(2)}) collective-permute-start(bf16[128,1024]{1,0:T(8,128)(2,1)S(1)} %get-tuple-element.30), channel_id=1, source_target_pairs={{0,256},{256,0},{1,257},{257,1},{2,258},{258,2},{3,259},{259,3},{4... | collective-permute-start | bytes 786440 | tf_op jit(solution)/shard_map/ppermute | solution.py:36
  199.8 18.2 %copy-start.4 = (bf16[256,224]{0,1:T(8,128)(2,1)S(1)}, bf16[256,224]{0,1:T(8,128)(2,1)}, u32[]{:S(2)}) copy-start(bf16[256,224]{0,1:T(8,128)(2,1)} %copy-done.3) | copy-start | bytes 344068
  199.8 18.2 %copy-start.6 = (bf16[256,224]{0,1:T(8,128)(2,1)S(1)}, bf16[256,224]{0,1:T(8,128)(2,1)}, u32[]{:S(2)}) copy-start(bf16[256,224]{0,1:T(8,128)(2,1)} %copy-done.5) | copy-start | bytes 344068
  200.7 17.3 %all-to-all-start.10 = ((bf16[16,16,1024]{2,1,0:T(8,128)(2,1)}), bf16[16,16,1024]{2,1,0:T(8,128)(2,1)S(1)}, u32[]{:S(2)}, u32[]{:S(2)}) async-start(bf16[16,16,1024]{2,1,0:T(8,128)(2,1)} %bitcast.30), calls=%async_computation.10 | async-start | bytes 1048576 | tf_op jit(solution)/shard_map/all_to_all | solution.py:24
  206.6 10.0 %collective-permute-start.4 = (bf16[128,448]{0,1:T(8,128)(2,1)S(1)}, bf16[128,448]{0,1:T(8,128)(2,1)S(1)}, u32[]{:S(2)}, u32[]{:S(2)}) collective-permute-start(bf16[128,448]{0,1:T(8,128)(2,1)S(1)} %pad_maximum_fusion.6), channel_id=1, source_target_pairs={{0,256},{256,0},{1,257},{257,1},{2,258},{258,2},{3,259},{259,3},{4... | collective-permute-start | bytes 344072 | tf_op jit(solution)/shard_map/ppermute | solution.py:36

commit v5 on v4

v5 whole, which is shorter than its diff:
```python
import math

import jax
import jax.numpy as jnp
from jax import lax
from jax.sharding import Mesh
from jax.sharding import PartitionSpec as P

R, Y, X, Z, C = "rows", "hidden_0", "hidden_1", "latents_0", "latents_1"
HIDDEN = (Y, X)
LATENTS = (Z, C)
HIDDEN_LATENTS = (Y, X, Z, C)
ROWS_LATENTS = (R, Z, C)
ROWS_Z = (R, Z)
ROWS_HIDDEN = (R, Y, X)

smooth_scale = 0.1
sparsity_weight = 0.5
F32 = jnp.float32
BF16 = jnp.bfloat16


def exchange(blocks, axes):
    return lax.all_to_all(blocks, axes, 0, 0, tiled=True)


def sent_to_all(x, axes):
    return exchange(jnp.broadcast_to(x, (lax.axis_size(axes), *x.shape)), axes)


def both_cores(x):
    return lax.all_gather(x, C, axis=0, tiled=False)


def both_rows(x):
    return lax.all_gather(x, R, axis=0, tiled=False)


def tied(*arrays):
    return lax.optimization_barrier(arrays)


def total(blocks):
    return jnp.sum(blocks.astype(F32), axis=0)


def own(x, index, dim):
    return lax.dynamic_index_in_dim(x, index, dim, keepdims=False)


def shards(
    inputs, gate_weight, up_weight, down_weight, encoder, decoder, enc_bias, dec_bias, shuffle_order
):
    tokens = shuffle_order.shape[0]
    n_hidden = lax.axis_size(HIDDEN)
    n_z = lax.axis_size(Z)
    core = lax.axis_index(C)
    row = lax.axis_index(R)
    width = decoder.shape[1]
    half = width // 2
    latents = encoder.shape[1]
    units = gate_weight.shape[1]

    low = row == 0

    mine, gate_own, up_own, bias_own, out_bias = tied(
        inputs.T, gate_weight, up_weight, enc_bias, dec_bias
    )
    few = sent_to_all(mine, Z)
    weights = jnp.concatenate([gate_own.T, up_own.T], axis=0)
    bias_both = jnp.concatenate([bias_own, own(both_rows(bias_own), 1 - row, 0)])
    bias_mine = own(out_bias.reshape(2, half), core, 0)
    few, weights, bias_both, bias_mine = tied(few, weights, bias_both, bias_mine)

    few, down_own = tied(few, down_weight)
    more = sent_to_all(few, HIDDEN)
    down_pair = own(both_cores(down_own).reshape(2 * units, n_hidden, 2, half), core, 2)
    more, down_pair = tied(more, down_pair.reshape(2 * units, n_hidden * half))

    every = both_cores(more)
    gathered = every.transpose(1, 2, 0, 3, 4).reshape(-1, inputs.shape[0])
    acts = jnp.dot(weights, gathered, preferred_element_type=F32)
    hidden = (jax.nn.gelu(acts[:units], approximate=True) * acts[units:]).astype(BF16)
    hidden_pair = both_cores(hidden).reshape(2 * units, -1)
    mine = lax.dot_general(
        down_pair, hidden_pair, (((0,), (0,)), ((), ())), preferred_element_type=F32
    ).astype(BF16).reshape(n_hidden, half, -1)

    summed = total(exchange(mine, HIDDEN)).T.astype(BF16)

    decoder_t = decoder.T
    summed, decoder_left = tied(summed, decoder_t[:half])
    row_parts = exchange(summed.reshape(n_z, -1, half), Z)
    decoder_left = both_rows(decoder_left)
    row_parts, decoder_left = tied(row_parts, decoder_left)
    rows_own = total(row_parts).astype(BF16)
    rows_own, decoder_right = tied(rows_own, decoder_t[half:])
    rows_all = sent_to_all(rows_own, ROWS_Z)
    decoder_right = both_rows(decoder_right)
    rows_all, decoder_right = tied(rows_all, decoder_right)
    mlp_out = both_cores(rows_all.reshape(tokens, half))

    def picked(order):
        return (order[:, None] == jnp.arange(tokens)[None, :]).astype(BF16)

    scale = 1.0 / math.sqrt(tokens)
    group = tokens // 2
    count = group // n_z
    order_own = lax.dynamic_slice_in_dim(shuffle_order, lax.axis_index(ROWS_Z) * count, count, 0)
    target = jnp.dot(picked(order_own), own(mlp_out, core, 0), preferred_element_type=F32)
    mlp_out, target = tied(mlp_out, target)
    pick = picked(shuffle_order)
    shuffled = jnp.concatenate(
        [jnp.dot(pick, mlp_out[c], preferred_element_type=F32).astype(BF16) for c in range(2)],
        axis=1,
    )

    pre_local = jnp.dot(shuffled, encoder, preferred_element_type=F32).astype(BF16)
    pre_parts = exchange(pre_local.reshape(2 * n_hidden, -1, latents), ROWS_HIDDEN)
    pre_sums = jnp.sum(pre_parts.reshape(2, n_hidden, -1, latents).astype(F32), axis=1)
    pre_act = jnp.concatenate(
        [jnp.where(low, *pre_sums), jnp.where(low, pre_sums[1], pre_sums[0])], axis=1
    ) + bias_both[None, :]
    latent_own = (smooth_scale * jax.nn.softplus(pre_act / smooth_scale)).astype(BF16)
    latent_own, decoder_left, decoder_right, pre_act = tied(
        latent_own, decoder_left, decoder_right, pre_act
    )
    latent_act = sent_to_all(latent_own, HIDDEN).reshape(group, 2 * latents)
    decoder_far = jnp.concatenate([own(decoder_left, 1 - row, 0), own(decoder_right, 1 - row, 0)])
    decoder_both = jnp.concatenate([decoder_t, decoder_far], axis=1)
    slope = jax.nn.sigmoid(pre_act / smooth_scale)
    latent_act, decoder_both, slope = tied(latent_act, decoder_both, slope)
    recon_local = lax.dot_general(
        decoder_both, latent_act, (((1,), (1,)), ((), ())), preferred_element_type=F32
    ).astype(BF16)
    recon_pair = both_cores(recon_local).reshape(2, 2, half, group)
    recon_mine = total(own(recon_pair, core, 1)).T.astype(BF16).reshape(n_z, -1, half)
    recon_mine, latent_far = tied(recon_mine, latent_act[:, latents:])
    recon_parts = exchange(recon_mine, Z)
    latent_far = own(both_rows(latent_far), 1 - row, 0)
    recon_parts, latent_far = tied(recon_parts, latent_far)
    recon = total(recon_parts) + bias_mine[None, :]
    err_own = (scale * (recon - target)).astype(BF16)
    err_pair = both_cores(sent_to_all(err_own, Z).reshape(group, half))
    d_err = jnp.concatenate([err_pair[0], err_pair[1]], axis=1)

    back_local = jnp.dot(d_err, decoder_both, preferred_element_type=F32).astype(BF16)
    back_local, err_near = tied(back_local, err_pair)
    back_parts = exchange(back_local.reshape(n_hidden, -1, 2 * latents), HIDDEN)
    err_far = own(both_rows(err_near), 1 - row, 0)
    err_far = jnp.concatenate([err_far[0], err_far[1]], axis=1)
    back_parts, err_far = tied(back_parts, err_far)
    d_latent = total(back_parts)
    d_pre_own = ((d_latent + sparsity_weight * scale) * slope).astype(BF16)
    d_pre_near, d_pre_far = d_pre_own[:, :latents], d_pre_own[:, latents:]
    d_pre_cut = jnp.stack(
        [jnp.where(low, d_pre_near, d_pre_far), jnp.where(low, d_pre_far, d_pre_near)]
    )
    d_pre = exchange(
        jnp.broadcast_to(d_pre_cut[:, None], (2, n_hidden, *d_pre_cut.shape[1:])).reshape(
            2 * n_hidden, -1, latents
        ),
        ROWS_HIDDEN,
    ).reshape(tokens, latents)

    latent_all = jnp.concatenate([latent_act[:, :latents], latent_far])
    err_all = jnp.concatenate([d_err, err_far])
    grad_dec = lax.dot_general(
        latent_all, err_all, (((0,), (0,)), ((), ())), preferred_element_type=F32
    ).astype(BF16)
    grad_enc = lax.dot_general(
        shuffled, d_pre, (((0,), (0,)), ((), ())), preferred_element_type=F32
    ).astype(BF16)

    both_recon = both_cores(recon.astype(BF16)).reshape(2, 2, count // 2, half)
    recon_out = own(both_recon, core, 1).transpose(1, 0, 2).reshape(count // 2, width)
    return (recon_out, grad_enc, grad_dec)


def solution(mesh):
    finer = Mesh(
        mesh.devices.reshape(mesh.shape["rows"], 2, 4, 16, 2),
        (R, Y, X, Z, C),
    )
    return jax.shard_map(
        shards,
        mesh=finer,
        in_specs=(
            P(R, HIDDEN_LATENTS),
            P(None, HIDDEN_LATENTS),
            P(None, HIDDEN_LATENTS),
            P(HIDDEN_LATENTS, None),
            P(HIDDEN, ROWS_LATENTS),
            P(ROWS_LATENTS, HIDDEN),
            P(ROWS_LATENTS),
            P(HIDDEN),
            P(),
        ),
        out_specs=(P(ROWS_LATENTS, HIDDEN), P(HIDDEN, ROWS_LATENTS), P(ROWS_LATENTS, HIDDEN)),
        check_vma=False,
    )
```

time: 222 us -> 240 us (1.081)
  starting transfers between devices: 63.4 us -> 81.3 us
  waiting for transfers between devices: 60.2 us -> 47.2 us
  local copies, waits for them, and re-layouts: 9.74 us -> 15.5 us
  blocking collectives: 73.3 us -> 78.2 us
    all_gather x0 -> x5, blocking collectives: none -> 43.9 us  [both_rows(): return lax.all_gather(x, R, axis=0, tiled=False)]
    all_to_all x4 -> x1, blocking collectives: 61.3 us -> 20.1 us  [exchange(): return lax.all_to_all(blocks, axes, 0, 0, tiled=True)]
    all_to_all x7 -> x10, starting transfers between devices: 49.5 us -> 81.3 us  [exchange(): return lax.all_to_all(blocks, axes, 0, 0, tiled=True)]
    ppermute x5 -> x0, starting transfers between devices: 13.9 us -> none  [swapped(): return lax.ppermute(x, axis, [(0, 1), (1, 0)])]
    all_to_all x7 -> x10, waiting for transfers between devices: 54.4 us -> 47.2 us  [exchange(): return lax.all_to_all(blocks, axes, 0, 0, tiled=True)]
    ppermute x5 -> x0, waiting for transfers between devices: 5.88 us -> none  [swapped(): return lax.ppermute(x, axis, [(0, 1), (1, 0)])]
    all_gather x6 -> x7, blocking collectives: 12 us -> 14.3 us  [both_cores(): return lax.all_gather(x, C, axis=0, tiled=False)]
  transfers between devices with their start and end apart: 12 -> 10, of which waited for: 8 -> 10; matrix products, arithmetic and copies ran while one was open for 4% -> 5% of each run, Pallas kernels for 0% -> 0%
where the time goes in v5:
time: 240 us; the launch traced here: 237 us
  starting transfers between devices  81.3 us (34%)
  blocking collectives  78.2 us (33%)
  waiting for transfers between devices  47.2 us (20%)
  local copies, waits for them, and re-layouts  15.5 us (6%)
  matrix products  9.25 us (4%)
  other arithmetic  4.56 us (2%)
    all_to_all x10, starting transfers between devices, exchange(): return lax.all_to_all(blocks, axes, 0, 0, tiled=True)  81.3 us
    all_to_all x10, waiting for transfers between devices, exchange(): return lax.all_to_all(blocks, axes, 0, 0, tiled=True)  47.2 us
    all_gather x5, blocking collectives, both_rows(): return lax.all_gather(x, R, axis=0, tiled=False)  43.9 us
    all_to_all x1, blocking collectives, exchange(): return lax.all_to_all(blocks, axes, 0, 0, tiled=True)  20.1 us
    all_gather x7, blocking collectives, both_cores(): return lax.all_gather(x, C, axis=0, tiled=False)  14.3 us
  transfers between devices with their start and end apart: 10, of which 10 were waited for; matrix products, arithmetic and copies ran while one was open for 5% of the time, Pallas kernels for 0%

profile of v5, /device:TPU:6, one launch (start us, length us, event | category | flops | bytes accessed | tf_op | source)
XLA Modules:
  0.0 237.1 jit_solution(3442452287822532293)
XLA Ops:
  0.7 1.4 broadcast_in_dim.12
  2.1 15.2 %all-to-all-start = ((bf16[16,14,128]{2,1,0:T(8,128)(2,1)}), bf16[16,14,128]{2,1,0:T(8,128)(2,1)S(1)}, u32[]{:S(2)}, u32[]{:S(2)}) async-start(bf16[16,14,128]{2,1,0:T(8,128)(2,1)} %broadcast_in_dim.12), calls=%async_computation | async-start | bytes 131072 | tf_op jit(solution)/shard_map/all_to_all | solution.py:24
  17.3 4.5 %all-gather = f32[2048]{0:T(1024)S(1)} all-gather(f32[1024]{0:T(1024)} %param.15), channel_id=2, replica_groups=mesh['rows'=2,'hidden_0'=2,'hidden_1'=4,'latents_0'=16,'latents_1'=2] {'..., dimensions={0}, use_global_device_ids=true | all-gather | bytes 12288 | tf_op jit(solution)/shard_map/all_gather | solution.py:36
  21.8 0.8 reshape.103
  22.6 2.1 pad_maximum_fusion
  24.6 5.4 %all-to-all-done = bf16[16,14,128]{2,1,0:T(8,128)(2,1)S(1)} async-done(((bf16[16,14,128]{2,1,0:T(8,128)(2,1)}), bf16[16,14,128]{2,1,0:T(8,128)(2,1)S(1)}, u32[]{:S(2)}, u32[]{:S(2)}) %all-to-all-start) | async-done | bytes 57376 | tf_op jit(solution)/shard_map/all_to_all | solution.py:24
  30.0 0.8 broadcast_in_dim.13
  30.9 7.4 %all-to-all-start.1 = ((bf16[8,16,14,128]{3,1,2,0:T(8,128)(2,1)}), bf16[8,16,14,128]{3,1,2,0:T(8,128)(2,1)S(1)}, u32[]{:S(2)}, u32[]{:S(2)}) async-start(bf16[8,16,14,128]{3,1,2,0:T(8,128)(2,1)} %broadcast_in_dim.13), calls=%async_computation.1 | async-start | bytes 917504 | tf_op jit(solution)/shard_map/all_to_all | solution.py:24
  38.3 2.4 all-gather.1
  40.6 1.4 reshape.104
  42.1 2.9 %dynamic-slice_reduce_fusion = bf16[112,8,224]{2,1,0:T(8,128)(2,1)S(1)} fusion(bf16[112,8,2,224]{3,2,1,0:T(2,128)(2,1)S(1)} %reshape.104, s32[]{:T(128)S(6)} %select_n.62), kind=kLoop, calls=%fused_computation.11 | loop fusion | bytes 802820 | tf_op jit(solution)/shard_map/jit(dynamic_index_in_dim)/dynamic_slice | solution.py:48
  44.9 0.5 reshape.105
  45.5 0.3 all-to-all-done.1
  45.8 2.5 %all-gather.2 = bf16[16,16,14,128]{3,1,2,0:T(8,128)(2,1)S(1)} all-gather(bf16[8,16,14,128]{3,1,2,0:T(8,128)(2,1)S(1)} %all-to-all-done.1), channel_id=4, replica_groups=mesh['rows'=2,'hidden_0'=2,'hidden_1'=4,'latents_0'=16,'latents_1'=2] {'..., dimensions={0}, use_global_device_ids=true | all-gather | bytes 1376256 | tf_op jit(solution)/shard_map/all_gather | solution.py:32
  48.2 0.3 copy.28
  48.5 0.3 reshape.106
  48.8 1.6 fusion.40
  50.4 1.8 all-gather.3
  52.2 1.1 convolution_convert_fusion.1
  53.3 6.9 %all-to-all-start.2 = ((bf16[8,224,128]{2,1,0:T(8,128)(2,1)}), bf16[8,224,128]{2,1,0:T(8,128)(2,1)S(1)}, u32[]{:S(2)}, u32[]{:S(2)}) async-start(bf16[8,224,128]{2,1,0:T(8,128)(2,1)} %bitcast.7), calls=%async_computation.2 | async-start | bytes 917504 | tf_op jit(solution)/shard_map/all_to_all | solution.py:24
  60.3 8.8 %all-to-all-done.2 = bf16[8,224,128]{2,1,0:T(8,128)(2,1)S(1)} async-done(((bf16[8,224,128]{2,1,0:T(8,128)(2,1)}), bf16[8,224,128]{2,1,0:T(8,128)(2,1)S(1)}, u32[]{:S(2)}, u32[]{:S(2)}) %all-to-all-start.2) | async-done | bytes 458784 | tf_op jit(solution)/shard_map/all_to_all | solution.py:24
  69.2 0.7 copy.29
  69.9 6.6 %all-to-all-start.3 = ((bf16[16,8,224]{2,1,0:T(8,128)(2,1)}), bf16[16,8,224]{2,1,0:T(8,128)(2,1)S(1)}, u32[]{:S(2)}, u32[]{:S(2)}) async-start(bf16[16,8,224]{2,1,0:T(8,128)(2,1)} %bitcast.10), calls=%async_computation.3 | async-start | bytes 131072 | tf_op jit(solution)/shard_map/all_to_all | solution.py:24
  76.6 10.9 %all-gather.4 = bf16[448,1024]{1,0:T(8,128)(2,1)S(1)} all-gather(bf16[224,1024]{1,0:T(8,128)(2,1)S(1)} %get-tuple-element.53), channel_id=6, replica_groups=mesh['rows'=2,'hidden_0'=2,'hidden_1'=4,'latents_0'=16,'latents_1'=2] {'..., dimensions={0}, use_global_device_ids=true | all-gather | bytes 1376256 | tf_op jit(solution)/shard_map/all_gather | solution.py:36
  87.5 2.0 all-to-all-done.3
  89.5 0.7 broadcast_in_dim.14
  90.1 10.2 %all-to-all-start.4 = ((bf16[32,8,224]{2,1,0:T(8,128)(2,1)}), bf16[32,8,224]{2,1,0:T(8,128)(2,1)S(1)}, u32[]{:S(2)}, u32[]{:S(2)}) async-start(bf16[32,8,224]{2,1,0:T(8,128)(2,1)} %broadcast_in_dim.14), calls=%async_computation.4 | async-start | bytes 262144 | tf_op jit(solution)/shard_map/all_to_all | solution.py:24
  100.4 10.6 %all-gather.5 = bf16[448,1024]{1,0:T(8,128)(2,1)} all-gather(bf16[224,1024]{1,0:T(8,128)(2,1)S(1)} %get-tuple-element.56), channel_id=7, replica_groups=mesh['rows'=2,'hidden_0'=2,'hidden_1'=4,'latents_0'=16,'latents_1'=2] {'..., dimensions={0}, use_global_device_ids=true | all-gather | bytes 1376256 | tf_op jit(solution)/shard_map/all_gather | solution.py:36
  110.9 5.0 %all-to-all-done.4 = bf16[32,8,224]{2,1,0:T(8,128)(2,1)S(1)} async-done(((bf16[32,8,224]{2,1,0:T(8,128)(2,1)}), bf16[32,8,224]{2,1,0:T(8,128)(2,1)S(1)}, u32[]{:S(2)}, u32[]{:S(2)}) %all-to-all-start.4) | async-done | bytes 114720 | tf_op jit(solution)/shard_map/all_to_all | solution.py:24
  116.1 2.0 all_gather.76
  118.0 0.2 fusion.17
  118.2 0.3 convolution_convert_fusion.6
  118.5 0.3 convolution_convert_fusion.7
  118.8 0.4 copy-done.5
  119.2 1.3 convolution_convert_fusion.4
  120.4 7.3 %all-to-all-start.5 = ((bf16[16,16,1024]{2,1,0:T(8,128)(2,1)}), bf16[16,16,1024]{2,1,0:T(8,128)(2,1)S(1)}, u32[]{:S(2)}, u32[]{:S(2)}) async-start(bf16[16,16,1024]{2,1,0:T(8,128)(2,1)} %bitcast.17), calls=%async_computation.5 | async-start | bytes 1048576 | tf_op jit(solution)/shard_map/all_to_all | solution.py:24
  127.7 9.8 %all-to-all-done.5 = bf16[16,16,1024]{2,1,0:T(8,128)(2,1)S(1)} async-done(((bf16[16,16,1024]{2,1,0:T(8,128)(2,1)}), bf16[16,16,1024]{2,1,0:T(8,128)(2,1)S(1)}, u32[]{:S(2)}, u32[]{:S(2)}) %all-to-all-start.5) | async-done | bytes 524320 | tf_op jit(solution)/shard_map/all_to_all | solution.py:24
  137.7 0.8 broadcast_in_dim.30
  138.6 5.9 %all-to-all-start.6 = ((bf16[8,16,2048]{2,1,0:T(8,128)(2,1)}), bf16[8,16,2048]{2,1,0:T(8,128)(2,1)S(1)}, u32[]{:S(2)}, u32[]{:S(2)}) async-start(bf16[8,16,2048]{2,1,0:T(8,128)(2,1)} %broadcast_in_dim.30), calls=%async_computation.6 | async-start | bytes 1048576 | tf_op jit(solution)/shard_map/all_to_all | solution.py:24
  144.5 1.1 dynamic-slice_bitcast_fusion
  145.6 1.3 maximum_maximum_fusion
  146.9 0.7 add_divide_fusion
  147.6 5.7 %all-to-all-done.6 = bf16[8,16,2048]{2,1,0:T(8,128)(2,1)S(1)} async-done(((bf16[8,16,2048]{2,1,0:T(8,128)(2,1)}), bf16[8,16,2048]{2,1,0:T(8,128)(2,1)S(1)}, u32[]{:S(2)}, u32[]{:S(2)}) %all-to-all-start.6) | async-done | bytes 524320 | tf_op jit(solution)/shard_map/all_to_all | solution.py:24
  153.3 0.7 fusion.39
  154.0 0.6 convolution_convert_fusion.5
  154.7 2.0 all-gather.6
  156.7 0.7 copy.31
  157.4 8.4 %all-to-all-start.7 = ((bf16[16,8,224]{2,1,0:T(8,128)(2,1)}), bf16[16,8,224]{2,1,0:T(8,128)(2,1)S(1)}, u32[]{:S(2)}, u32[]{:S(2)}) async-start(bf16[16,8,224]{2,1,0:T(8,128)(2,1)} %bitcast.26), calls=%async_computation.7 | async-start | bytes 131072 | tf_op jit(solution)/shard_map/all_to_all | solution.py:24
  165.8 8.8 %all-gather.7 = bf16[256,1024]{1,0:T(8,128)(2,1)S(1)} all-gather(bf16[128,1024]{1,0:T(8,128)(2,1)S(1)} %get-tuple-element.69), channel_id=9, replica_groups=mesh['rows'=2,'hidden_0'=2,'hidden_1'=4,'latents_0'=16,'latents_1'=2] {'..., dimensions={0}, use_global_device_ids=true | all-gather | bytes 786432 | tf_op jit(solution)/shard_map/all_gather | solution.py:36
  174.6 4.3 %all-to-all-done.7 = bf16[16,8,224]{2,1,0:T(8,128)(2,1)S(1)} async-done(((bf16[16,8,224]{2,1,0:T(8,128)(2,1)}), bf16[16,8,224]{2,1,0:T(8,128)(2,1)S(1)}, u32[]{:S(2)}, u32[]{:S(2)}) %all-to-all-start.7) | async-done | bytes 57376 | tf_op jit(solution)/shard_map/all_to_all | solution.py:24
  178.9 20.1 %all_to_all.55 = bf16[16,8,224]{2,1,0:T(8,128)(2,1)S(1)} all-to-all(bf16[16,8,224]{2,1,0:T(8,128)(2,1)S(1)} %broadcast_in_dim.31), channel_id=1, replica_groups=mesh['rows'=2,'hidden_0'=2,'hidden_1'=4,'latents_0'=16,'latents_1'=2] {'..., dimensions={0} | all-to-all | bytes 114688 | tf_op jit(solution)/shard_map/all_to_all | solution.py:24
  198.9 0.1 copy.34
  199.1 1.9 all_gather.82
  201.0 1.3 convolution_convert_fusion
  202.2 5.9 %all-to-all-start.9 = ((bf16[8,16,2048]{2,1,0:T(8,128)(2,1)}), bf16[8,16,2048]{2,1,0:T(8,128)(2,1)S(1)}, u32[]{:S(2)}, u32[]{:S(2)}) async-start(bf16[8,16,2048]{2,1,0:T(8,128)(2,1)} %bitcast.35), calls=%async_computation.9 | async-start | bytes 1048576 | tf_op jit(solution)/shard_map/all_to_all | solution.py:24
  208.1 9.2 %all-gather.8 = bf16[4,128,224]{1,2,0:T(8,128)(2,1)S(1)} all-gather(bf16[2,128,224]{1,2,0:T(8,128)(2,1)S(1)} %all_gather.82), channel_id=10, replica_groups=mesh['rows'=2,'hidden_0'=2,'hidden_1'=4,'latents_0'=16,'latents_1'=2] {'..., dimensions={0}, use_global_device_ids=true | all-gather | bytes 344064 | tf_op jit(solution)/shard_map/all_gather | solution.py:36
  217.3 0.5 all-to-all-done.9
  218.0 0.9 broadcast_in_dim.32
  218.9 7.6 %all-to-all-start.10 = ((bf16[16,16,1024]{2,1,0:T(8,128)(2,1)}), bf16[16,16,1024]{2,1,0:T(8,128)(2,1)S(1)}, u32[]{:S(2)}, u32[]{:S(2)}) async-start(bf16[16,16,1024]{2,1,0:T(8,128)(2,1)} %bitcast.41), calls=%async_computation.10 | async-start | bytes 1048576 | tf_op jit(solution)/shard_map/all_to_all | solution.py:24
  226.4 1.8 all_gather.81
  228.3 0.7 reshape.115
  229.0 1.3 convolution_convert_fusion.2
  230.3 5.5 %all-to-all-done.10 = bf16[16,16,1024]{2,1,0:T(8,128)(2,1)S(1)} async-done(((bf16[16,16,1024]{2,1,0:T(8,128)(2,1)}), bf16[16,16,1024]{2,1,0:T(8,128)(2,1)S(1)}, u32[]{:S(2)}, u32[]{:S(2)}) %all-to-all-start.10) | async-done | bytes 524320 | tf_op jit(solution)/shard_map/all_to_all | solution.py:24
  235.8 1.3 convolution_convert_fusion.3
  (51 shorter events, 0.9 us)
Async XLA Ops:
  0.6 118.5 %copy-start = (bf16[448,1024]{1,0:T(8,128)(2,1)S(1)}, bf16[448,1024]{1,0:T(8,128)(2,1)}, u32[]{:S(2)}) copy-start(bf16[448,1024]{1,0:T(8,128)(2,1)} %param.13) | copy-start | bytes 2752516
  0.6 24.0 %copy-start.9 = (f32[1024]{0:T(1024)S(1)}, f32[1024]{0:T(1024)}, u32[]{:S(2)}) copy-start(f32[1024]{0:T(1024)} %param.15) | copy-start | bytes 12292
  0.7 37.6 %copy-start.3 = (bf16[56,3584]{1,0:T(8,128)(2,1)S(1)}, bf16[56,3584]{1,0:T(8,128)(2,1)}, u32[]{:S(2)}) copy-start(bf16[56,3584]{1,0:T(8,128)(2,1)} %param.12) | copy-start | bytes 1204228
  2.1 27.9 %all-to-all-start = ((bf16[16,14,128]{2,1,0:T(8,128)(2,1)}), bf16[16,14,128]{2,1,0:T(8,128)(2,1)S(1)}, u32[]{:S(2)}, u32[]{:S(2)}) async-start(bf16[16,14,128]{2,1,0:T(8,128)(2,1)} %broadcast_in_dim.12), calls=%async_computation | async-start | bytes 131072 | tf_op jit(solution)/shard_map/all_to_all | solution.py:24
  30.9 14.9 %all-to-all-start.1 = ((bf16[8,16,14,128]{3,1,2,0:T(8,128)(2,1)}), bf16[8,16,14,128]{3,1,2,0:T(8,128)(2,1)S(1)}, u32[]{:S(2)}, u32[]{:S(2)}) async-start(bf16[8,16,14,128]{3,1,2,0:T(8,128)(2,1)} %broadcast_in_dim.13), calls=%async_computation.1 | async-start | bytes 917504 | tf_op jit(solution)/shard_map/all_to_all | solution.py:24
  48.8 11.4 %copy-start.1 = (bf16[1024,448]{0,1:T(8,128)(2,1)S(1)}, bf16[1024,448]{0,1:T(8,128)(2,1)}, u32[]{:S(2)}) copy-start(bf16[1024,448]{0,1:T(8,128)(2,1)} %param.14) | copy-start | bytes 2752516
  53.3 15.8 %all-to-all-start.2 = ((bf16[8,224,128]{2,1,0:T(8,128)(2,1)}), bf16[8,224,128]{2,1,0:T(8,128)(2,1)S(1)}, u32[]{:S(2)}, u32[]{:S(2)}) async-start(bf16[8,224,128]{2,1,0:T(8,128)(2,1)} %bitcast.7), calls=%async_computation.2 | async-start | bytes 917504 | tf_op jit(solution)/shard_map/all_to_all | solution.py:24
  60.2 40.1 %copy-start.10 = (s32[256]{0:T(256)S(1)}, s32[256]{0:T(256)}, u32[]{:S(2)}) copy-start(s32[256]{0:T(256)} %param.17) | copy-start | bytes 3076
  69.9 19.5 %all-to-all-start.3 = ((bf16[16,8,224]{2,1,0:T(8,128)(2,1)}), bf16[16,8,224]{2,1,0:T(8,128)(2,1)S(1)}, u32[]{:S(2)}, u32[]{:S(2)}) async-start(bf16[16,8,224]{2,1,0:T(8,128)(2,1)} %bitcast.10), calls=%async_computation.3 | async-start | bytes 131072 | tf_op jit(solution)/shard_map/all_to_all | solution.py:24
  90.1 25.8 %all-to-all-start.4 = ((bf16[32,8,224]{2,1,0:T(8,128)(2,1)}), bf16[32,8,224]{2,1,0:T(8,128)(2,1)S(1)}, u32[]{:S(2)}, u32[]{:S(2)}) async-start(bf16[32,8,224]{2,1,0:T(8,128)(2,1)} %broadcast_in_dim.14), calls=%async_computation.4 | async-start | bytes 262144 | tf_op jit(solution)/shard_map/all_to_all | solution.py:24
  118.5 0.7 copy-start.5
  119.2 1.3 copy-start.7
  120.4 17.1 %all-to-all-start.5 = ((bf16[16,16,1024]{2,1,0:T(8,128)(2,1)}), bf16[16,16,1024]{2,1,0:T(8,128)(2,1)S(1)}, u32[]{:S(2)}, u32[]{:S(2)}) async-start(bf16[16,16,1024]{2,1,0:T(8,128)(2,1)} %bitcast.17), calls=%async_computation.5 | async-start | bytes 1048576 | tf_op jit(solution)/shard_map/all_to_all | solution.py:24
  138.6 14.7 %all-to-all-start.6 = ((bf16[8,16,2048]{2,1,0:T(8,128)(2,1)}), bf16[8,16,2048]{2,1,0:T(8,128)(2,1)S(1)}, u32[]{:S(2)}, u32[]{:S(2)}) async-start(bf16[8,16,2048]{2,1,0:T(8,128)(2,1)} %broadcast_in_dim.30), calls=%async_computation.6 | async-start | bytes 1048576 | tf_op jit(solution)/shard_map/all_to_all | solution.py:24
  157.4 21.4 %all-to-all-start.7 = ((bf16[16,8,224]{2,1,0:T(8,128)(2,1)}), bf16[16,8,224]{2,1,0:T(8,128)(2,1)S(1)}, u32[]{:S(2)}, u32[]{:S(2)}) async-start(bf16[16,8,224]{2,1,0:T(8,128)(2,1)} %bitcast.26), calls=%async_computation.7 | async-start | bytes 131072 | tf_op jit(solution)/shard_map/all_to_all | solution.py:24
  202.2 15.7 %copy-start.2 = (f32[16,2048]{1,0:T(8,128)S(1)}, f32[16,2048]{1,0:T(8,128)}, u32[]{:S(2)}) copy-start(f32[16,2048]{1,0:T(8,128)} %add_divide_fusion) | copy-start | bytes 393220
  202.2 15.6 %all-to-all-start.9 = ((bf16[8,16,2048]{2,1,0:T(8,128)(2,1)}), bf16[8,16,2048]{2,1,0:T(8,128)(2,1)S(1)}, u32[]{:S(2)}, u32[]{:S(2)}) async-start(bf16[8,16,2048]{2,1,0:T(8,128)(2,1)} %bitcast.35), calls=%async_computation.9 | async-start | bytes 1048576 | tf_op jit(solution)/shard_map/all_to_all | solution.py:24
  208.1 20.9 %copy-start.4 = (bf16[128,1024]{1,0:T(8,128)(2,1)S(1)}, bf16[128,1024]{1,0:T(8,128)(2,1)}, u32[]{:S(2)}) copy-start(bf16[128,1024]{1,0:T(8,128)(2,1)} %get-tuple-element.83) | copy-start | bytes 786436
  218.0 17.8 %copy-start.6 = (bf16[256,224]{0,1:T(8,128)(2,1)S(1)}, bf16[256,224]{0,1:T(8,128)(2,1)}, u32[]{:S(2)}) copy-start(bf16[256,224]{0,1:T(8,128)(2,1)} %copy-done.5) | copy-start | bytes 344068
  218.0 17.8 %copy-start.8 = (bf16[256,224]{0,1:T(8,128)(2,1)S(1)}, bf16[256,224]{0,1:T(8,128)(2,1)}, u32[]{:S(2)}) copy-start(bf16[256,224]{0,1:T(8,128)(2,1)} %copy-done.7) | copy-start | bytes 344068
  218.9 16.9 %all-to-all-start.10 = ((bf16[16,16,1024]{2,1,0:T(8,128)(2,1)}), bf16[16,16,1024]{2,1,0:T(8,128)(2,1)S(1)}, u32[]{:S(2)}, u32[]{:S(2)}) async-start(bf16[16,16,1024]{2,1,0:T(8,128)(2,1)} %bitcast.41), calls=%async_computation.10 | async-start | bytes 1048576 | tf_op jit(solution)/shard_map/all_to_all | solution.py:24

commit v6 on v5

--- a/solution.py
+++ b/solution.py
@@ -30,6 +30,10 @@
 
 def both_cores(x):
     return lax.all_gather(x, C, axis=0, tiled=False)
+
+
+def swapped_rows(x):
+    return lax.ppermute(x, R, [(0, 1), (1, 0)])
 
 
 def both_rows(x):
@@ -74,8 +78,7 @@
 
     few, down_own = tied(few, down_weight)
     more = sent_to_all(few, HIDDEN)
-    down_pair = own(both_cores(down_own).reshape(2 * units, n_hidden, 2, half), core, 2)
-    more, down_pair = tied(more, down_pair.reshape(2 * units, n_hidden * half))
+    more, down_pair = tied(more, both_cores(down_own).reshape(2 * units, -1))
 
     every = both_cores(more)
     gathered = every.transpose(1, 2, 0, 3, 4).reshape(-1, inputs.shape[0])
@@ -84,20 +87,16 @@
     hidden_pair = both_cores(hidden).reshape(2 * units, -1)
     mine = lax.dot_general(
         down_pair, hidden_pair, (((0,), (0,)), ((), ())), preferred_element_type=F32
-    ).astype(BF16).reshape(n_hidden, half, -1)
+    ).astype(BF16)
+    mine = own(mine.reshape(n_hidden, 2, half, -1), core, 1)
 
     summed = total(exchange(mine, HIDDEN)).T.astype(BF16)
 
-    decoder_t = decoder.T
-    summed, decoder_left = tied(summed, decoder_t[:half])
-    row_parts = exchange(summed.reshape(n_z, -1, half), Z)
-    decoder_left = both_rows(decoder_left)
-    row_parts, decoder_left = tied(row_parts, decoder_left)
-    rows_own = total(row_parts).astype(BF16)
-    rows_own, decoder_right = tied(rows_own, decoder_t[half:])
+    summed, decoder_near = tied(summed, decoder.T)
+    decoder_far = swapped_rows(decoder_near)
+    rows_own = total(exchange(summed.reshape(n_z, -1, half), Z)).astype(BF16)
     rows_all = sent_to_all(rows_own, ROWS_Z)
-    decoder_right = both_rows(decoder_right)
-    rows_all, decoder_right = tied(rows_all, decoder_right)
+    rows_all, decoder_far = tied(rows_all, decoder_far)
     mlp_out = both_cores(rows_all.reshape(tokens, half))
 
     def picked(order):
@@ -122,12 +121,9 @@
         [jnp.where(low, *pre_sums), jnp.where(low, pre_sums[1], pre_sums[0])], axis=1
     ) + bias_both[None, :]
     latent_own = (smooth_scale * jax.nn.softplus(pre_act / smooth_scale)).astype(BF16)
-    latent_own, decoder_left, decoder_right, pre_act = tied(
-        latent_own, decoder_left, decoder_right, pre_act
-    )
+    latent_own, decoder_far, pre_act = tied(latent_own, decoder_far, pre_act)
     latent_act = sent_to_all(latent_own, HIDDEN).reshape(group, 2 * latents)
-    decoder_far = jnp.concatenate([own(decoder_left, 1 - row, 0), own(decoder_right, 1 - row, 0)])
-    decoder_both = jnp.concatenate([decoder_t, decoder_far], axis=1)
+    decoder_both = jnp.concatenate([decoder_near, decoder_far], axis=1)
     slope = jax.nn.sigmoid(pre_act / smooth_scale)
     latent_act, decoder_both, slope = tied(latent_act, decoder_both, slope)
     recon_local = lax.dot_general(
@@ -135,21 +131,18 @@
     ).astype(BF16)
     recon_pair = both_cores(recon_local).reshape(2, 2, half, group)
     recon_mine = total(own(recon_pair, core, 1)).T.astype(BF16).reshape(n_z, -1, half)
-    recon_mine, latent_far = tied(recon_mine, latent_act[:, latents:])
     recon_parts = exchange(recon_mine, Z)
-    latent_far = own(both_rows(latent_far), 1 - row, 0)
-    recon_parts, latent_far = tied(recon_parts, latent_far)
     recon = total(recon_parts) + bias_mine[None, :]
     err_own = (scale * (recon - target)).astype(BF16)
     err_pair = both_cores(sent_to_all(err_own, Z).reshape(group, half))
     d_err = jnp.concatenate([err_pair[0], err_pair[1]], axis=1)
 
     back_local = jnp.dot(d_err, decoder_both, preferred_element_type=F32).astype(BF16)
-    back_local, err_near = tied(back_local, err_pair)
+    back_local, err_near, latent_far = tied(back_local, d_err, latent_act[:, latents:])
     back_parts = exchange(back_local.reshape(n_hidden, -1, 2 * latents), HIDDEN)
-    err_far = own(both_rows(err_near), 1 - row, 0)
-    err_far = jnp.concatenate([err_far[0], err_far[1]], axis=1)
-    back_parts, err_far = tied(back_parts, err_far)
+    back_parts, err_far, latent_far = tied(
+        back_parts, swapped_rows(err_near), swapped_rows(latent_far)
+    )
     d_latent = total(back_parts)
     d_pre_own = ((d_latent + sparsity_weight * scale) * slope).astype(BF16)
     d_pre_near, d_pre_far = d_pre_own[:, :latents], d_pre_own[:, latents:]

time: 240 us -> 227 us (0.946)
  waiting for transfers between devices: 47.2 us -> 69.2 us
  starting transfers between devices: 81.3 us -> 63.5 us
  blocking collectives: 78.2 us -> 68.3 us
  local copies, waits for them, and re-layouts: 15.5 us -> 9.06 us
    all_gather x5 -> x1, blocking collectives: 43.9 us -> 4.48 us  [both_rows(): return lax.all_gather(x, R, axis=0, tiled=False)]
    all_to_all x1 -> x3, blocking collectives: 20.1 us -> 49.4 us  [exchange(): return lax.all_to_all(blocks, axes, 0, 0, tiled=True)]
    all_to_all x10 -> x8, starting transfers between devices: 81.3 us -> 55 us  [exchange(): return lax.all_to_all(blocks, axes, 0, 0, tiled=True)]
    all_to_all x10 -> x8, waiting for transfers between devices: 47.2 us -> 60.2 us  [exchange(): return lax.all_to_all(blocks, axes, 0, 0, tiled=True)]
    ppermute x0 -> x3, waiting for transfers between devices: none -> 9.06 us  [swapped_rows(): return lax.ppermute(x, R, [(0, 1), (1, 0)])]
    ppermute x0 -> x3, starting transfers between devices: none -> 8.41 us  [swapped_rows(): return lax.ppermute(x, R, [(0, 1), (1, 0)])]
    dynamic_slice x3 -> x2, local copies, waits for them, and re-layouts: 2.87 us -> 0.01 us  [own(): return lax.dynamic_index_in_dim(x, index, dim, keepdims=False)]
  transfers between devices with their start and end apart: 10 -> 11, of which waited for: 10 -> 8; matrix products, arithmetic and copies ran while one was open for 5% -> 4% of each run, Pallas kernels for 0% -> 0%
where the time goes in v6:
time: 227 us; the launch traced here: 224 us
  waiting for transfers between devices  69.2 us (30%)
  blocking collectives  68.3 us (30%)
  starting transfers between devices  63.5 us (28%)
  local copies, waits for them, and re-layouts  9.06 us (4%)
  matrix products  8.6 us (4%)
  other arithmetic  4.16 us (2%)
    all_to_all x8, waiting for transfers between devices, exchange(): return lax.all_to_all(blocks, axes, 0, 0, tiled=True)  60.2 us
    all_to_all x8, starting transfers between devices, exchange(): return lax.all_to_all(blocks, axes, 0, 0, tiled=True)  55 us
    all_to_all x3, blocking collectives, exchange(): return lax.all_to_all(blocks, axes, 0, 0, tiled=True)  49.4 us
    all_gather x7, blocking collectives, both_cores(): return lax.all_gather(x, C, axis=0, tiled=False)  14.4 us
    ppermute x3, waiting for transfers between devices, swapped_rows(): return lax.ppermute(x, R, [(0, 1), (1, 0)])  9.06 us
    ppermute x3, starting transfers between devices, swapped_rows(): return lax.ppermute(x, R, [(0, 1), (1, 0)])  8.41 us
  transfers between devices with their start and end apart: 11, of which 8 were waited for; matrix products, arithmetic and copies ran while one was open for 4% of the time, Pallas kernels for 0%

profile of v6, /device:TPU:6, one launch (start us, length us, event | category | flops | bytes accessed | tf_op | source)
XLA Modules:
  0.0 223.8 jit_solution(8919640962182835204)
XLA Ops:
  0.6 0.0 copy-start
  0.7 1.4 broadcast_in_dim.12
  2.1 15.2 %all-to-all-start = ((bf16[16,14,128]{2,1,0:T(8,128)(2,1)}), bf16[16,14,128]{2,1,0:T(8,128)(2,1)S(1)}, u32[]{:S(2)}, u32[]{:S(2)}) async-start(bf16[16,14,128]{2,1,0:T(8,128)(2,1)} %broadcast_in_dim.12), calls=%async_computation | async-start | bytes 131072 | tf_op jit(solution)/shard_map/all_to_all | solution.py:24
  17.3 4.5 %all-gather = f32[2048]{0:T(1024)S(1)} all-gather(f32[1024]{0:T(1024)} %param.15), channel_id=2, replica_groups=mesh['rows'=2,'hidden_0'=2,'hidden_1'=4,'latents_0'=16,'latents_1'=2] {'..., dimensions={0}, use_global_device_ids=true | all-gather | bytes 12288 | tf_op jit(solution)/shard_map/all_gather | solution.py:40
  21.8 0.8 reshape.95
  22.6 2.1 pad_maximum_fusion.1
  24.6 5.4 %all-to-all-done = bf16[16,14,128]{2,1,0:T(8,128)(2,1)S(1)} async-done(((bf16[16,14,128]{2,1,0:T(8,128)(2,1)}), bf16[16,14,128]{2,1,0:T(8,128)(2,1)S(1)}, u32[]{:S(2)}, u32[]{:S(2)}) %all-to-all-start) | async-done | bytes 57376 | tf_op jit(solution)/shard_map/all_to_all | solution.py:24
  30.0 0.8 broadcast_in_dim.13
  30.9 7.4 %all-to-all-start.1 = ((bf16[8,16,14,128]{3,1,2,0:T(8,128)(2,1)}), bf16[8,16,14,128]{3,1,2,0:T(8,128)(2,1)S(1)}, u32[]{:S(2)}, u32[]{:S(2)}) async-start(bf16[8,16,14,128]{3,1,2,0:T(8,128)(2,1)} %broadcast_in_dim.13), calls=%async_computation.1 | async-start | bytes 917504 | tf_op jit(solution)/shard_map/all_to_all | solution.py:24
  38.3 2.5 %all-gather.1 = bf16[112,3584]{1,0:T(8,128)(2,1)} all-gather(bf16[56,3584]{1,0:T(8,128)(2,1)S(1)} %copy-done.4), channel_id=3, replica_groups=mesh['rows'=2,'hidden_0'=2,'hidden_1'=4,'latents_0'=16,'latents_1'=2] {'..., dimensions={0}, use_global_device_ids=true | all-gather | bytes 1204224 | tf_op jit(solution)/shard_map/all_gather | solution.py:32
  40.8 5.0 %all-to-all-done.1 = bf16[8,16,14,128]{3,1,2,0:T(8,128)(2,1)S(1)} async-done(((bf16[8,16,14,128]{3,1,2,0:T(8,128)(2,1)}), bf16[8,16,14,128]{3,1,2,0:T(8,128)(2,1)S(1)}, u32[]{:S(2)}, u32[]{:S(2)}) %all-to-all-start.1) | async-done | bytes 458784 | tf_op jit(solution)/shard_map/all_to_all | solution.py:24
  45.8 2.5 %all-gather.2 = bf16[16,16,14,128]{3,1,2,0:T(8,128)(2,1)S(1)} all-gather(bf16[8,16,14,128]{3,1,2,0:T(8,128)(2,1)S(1)} %all-to-all-done.1), channel_id=4, replica_groups=mesh['rows'=2,'hidden_0'=2,'hidden_1'=4,'latents_0'=16,'latents_1'=2] {'..., dimensions={0}, use_global_device_ids=true | all-gather | bytes 1376256 | tf_op jit(solution)/shard_map/all_gather | solution.py:32
  48.2 0.3 copy.24
  48.5 0.3 reshape.97
  48.8 1.6 fusion.35
  50.4 1.8 all-gather.3
  52.2 0.4 convolution_convert_fusion
  52.7 14.2 %all_to_all.55 = bf16[8,224,128]{2,1,0:T(8,128)(2,1)S(1)} all-to-all(bf16[8,224,128]{2,1,0:T(8,128)(2,1)S(1)} %dynamic-slice_bitcast_fusion), channel_id=1, replica_groups=mesh['rows'=2,'hidden_0'=2,'hidden_1'=4,'latents_0'=16,'latents_1'=2] {'..., dimensions={0} | all-to-all | bytes 917504 | tf_op jit(solution)/shard_map/all_to_all | solution.py:24
  66.9 0.1 reduce_sum.65
  67.0 2.6 %collective-permute-start = (bf16[448,1024]{1,0:T(8,128)(2,1)S(1)}, bf16[448,1024]{1,0:T(8,128)(2,1)S(1)}, u32[]{:S(2)}, u32[]{:S(2)}) collective-permute-start(bf16[448,1024]{1,0:T(8,128)(2,1)S(1)} %bitcast.73), channel_id=1, source_target_pairs={{0,256},{256,0},{1,257},{257,1},{2,258},{258,2},{3,259},{259,3},{4... | collective-permute-start | bytes 2752520 | tf_op jit(solution)/shard_map/ppermute | solution.py:36
  69.6 0.1 copy.25
  69.7 19.3 %all_to_all.56 = bf16[16,8,224]{2,1,0:T(8,128)(2,1)S(1)} all-to-all(bf16[16,8,224]{2,1,0:T(8,128)(2,1)S(1)} %bitcast.79), channel_id=1, replica_groups=mesh['rows'=2,'hidden_0'=2,'hidden_1'=4,'latents_0'=16,'latents_1'=2] {'..., dimensions={0} | all-to-all | bytes 114688 | tf_op jit(solution)/shard_map/all_to_all | solution.py:24
  89.1 0.7 broadcast_in_dim.14
  89.7 3.9 %all-to-all-start.4 = ((bf16[32,8,224]{2,1,0:T(8,128)(2,1)}), bf16[32,8,224]{2,1,0:T(8,128)(2,1)S(1)}, u32[]{:S(2)}, u32[]{:S(2)}) async-start(bf16[32,8,224]{2,1,0:T(8,128)(2,1)} %broadcast_in_dim.14), calls=%async_computation.4 | async-start | bytes 262144 | tf_op jit(solution)/shard_map/all_to_all | solution.py:24
  93.7 0.1 dynamic_slice.30
  93.8 15.4 %all-to-all-done.4 = bf16[32,8,224]{2,1,0:T(8,128)(2,1)S(1)} async-done(((bf16[32,8,224]{2,1,0:T(8,128)(2,1)}), bf16[32,8,224]{2,1,0:T(8,128)(2,1)S(1)}, u32[]{:S(2)}, u32[]{:S(2)}) %all-to-all-start.4) | async-done | bytes 114720 | tf_op jit(solution)/shard_map/all_to_all | solution.py:24
  109.2 0.1 copy.26
  109.3 2.0 all_gather.48
  111.3 0.2 fusion.14
  111.5 0.3 convolution_convert_fusion.6
  111.8 0.3 convolution_convert_fusion.7
  112.1 0.3 copy-done.6
  112.4 1.3 convolution_convert_fusion.4
  113.7 5.2 %all-to-all-start.5 = ((bf16[16,16,1024]{2,1,0:T(8,128)(2,1)}), bf16[16,16,1024]{2,1,0:T(8,128)(2,1)S(1)}, u32[]{:S(2)}, u32[]{:S(2)}) async-start(bf16[16,16,1024]{2,1,0:T(8,128)(2,1)} %bitcast.16), calls=%async_computation.5 | async-start | bytes 1048576 | tf_op jit(solution)/shard_map/all_to_all | solution.py:24
  118.9 9.8 %all-to-all-done.5 = bf16[16,16,1024]{2,1,0:T(8,128)(2,1)S(1)} async-done(((bf16[16,16,1024]{2,1,0:T(8,128)(2,1)}), bf16[16,16,1024]{2,1,0:T(8,128)(2,1)S(1)}, u32[]{:S(2)}, u32[]{:S(2)}) %all-to-all-start.5) | async-done | bytes 524320 | tf_op jit(solution)/shard_map/all_to_all | solution.py:24
  128.7 0.1 convert_reduce_fusion
  128.8 0.1 fusion.9
  128.9 0.8 broadcast_in_dim.30
  129.8 5.9 %all-to-all-start.6 = ((bf16[8,16,2048]{2,1,0:T(8,128)(2,1)}), bf16[8,16,2048]{2,1,0:T(8,128)(2,1)S(1)}, u32[]{:S(2)}, u32[]{:S(2)}) async-start(bf16[8,16,2048]{2,1,0:T(8,128)(2,1)} %broadcast_in_dim.30), calls=%async_computation.6 | async-start | bytes 1048576 | tf_op jit(solution)/shard_map/all_to_all | solution.py:24
  135.7 1.6 pad_maximum_fusion
  137.3 7.1 %all-to-all-done.6 = bf16[8,16,2048]{2,1,0:T(8,128)(2,1)S(1)} async-done(((bf16[8,16,2048]{2,1,0:T(8,128)(2,1)}), bf16[8,16,2048]{2,1,0:T(8,128)(2,1)S(1)}, u32[]{:S(2)}, u32[]{:S(2)}) %all-to-all-start.6) | async-done | bytes 524320 | tf_op jit(solution)/shard_map/all_to_all | solution.py:24
  144.5 0.6 convolution_convert_fusion.5
  145.1 2.0 all-gather.4
  147.1 0.1 copy.27
  147.2 15.9 %all_to_all.57 = bf16[16,8,224]{2,1,0:T(8,128)(2,1)S(1)} all-to-all(bf16[16,8,224]{2,1,0:T(8,128)(2,1)S(1)} %bitcast.80), channel_id=1, replica_groups=mesh['rows'=2,'hidden_0'=2,'hidden_1'=4,'latents_0'=16,'latents_1'=2] {'..., dimensions={0} | all-to-all | bytes 114688 | tf_op jit(solution)/shard_map/all_to_all | solution.py:24
  163.2 0.6 broadcast_in_dim.31
  163.8 3.5 %all-to-all-start.8 = ((bf16[16,8,224]{2,1,0:T(8,128)(2,1)}), bf16[16,8,224]{2,1,0:T(8,128)(2,1)S(1)}, u32[]{:S(2)}, u32[]{:S(2)}) async-start(bf16[16,8,224]{2,1,0:T(8,128)(2,1)} %broadcast_in_dim.31), calls=%async_computation.8 | async-start | bytes 131072 | tf_op jit(solution)/shard_map/all_to_all | solution.py:24
  167.3 0.8 fusion.34
  168.2 11.9 %all-to-all-done.8 = bf16[16,8,224]{2,1,0:T(8,128)(2,1)S(1)} async-done(((bf16[16,8,224]{2,1,0:T(8,128)(2,1)}), bf16[16,8,224]{2,1,0:T(8,128)(2,1)S(1)}, u32[]{:S(2)}, u32[]{:S(2)}) %all-to-all-start.8) | async-done | bytes 57376 | tf_op jit(solution)/shard_map/all_to_all | solution.py:24
  180.1 0.1 copy.30
  180.2 1.9 all_gather.52
  182.1 1.3 convolution_convert_fusion.1
  183.4 5.9 %all-to-all-start.9 = ((bf16[8,16,2048]{2,1,0:T(8,128)(2,1)}), bf16[8,16,2048]{2,1,0:T(8,128)(2,1)S(1)}, u32[]{:S(2)}, u32[]{:S(2)}) async-start(bf16[8,16,2048]{2,1,0:T(8,128)(2,1)} %bitcast.30), calls=%async_computation.9 | async-start | bytes 1048576 | tf_op jit(solution)/shard_map/all_to_all | solution.py:24
  189.3 2.4 %collective-permute-start.2 = (bf16[128,1024]{1,0:T(8,128)(2,1)}, bf16[128,1024]{1,0:T(8,128)(2,1)S(1)}, u32[]{:S(2)}, u32[]{:S(2)}) collective-permute-start(bf16[128,1024]{1,0:T(8,128)(2,1)} %get-tuple-element.60), channel_id=1, source_target_pairs={{0,256},{256,0},{1,257},{257,1},{2,258},{258,2},{3,259},{259,3},{4... | collective-permute-start | bytes 786440 | tf_op jit(solution)/shard_map/ppermute | solution.py:36
  191.6 3.5 %collective-permute-start.1 = (bf16[128,448]{0,1:T(8,128)(2,1)S(1)}, bf16[128,448]{0,1:T(8,128)(2,1)S(1)}, u32[]{:S(2)}, u32[]{:S(2)}) collective-permute-start(bf16[128,448]{0,1:T(8,128)(2,1)S(1)} %pad_maximum_fusion.5), channel_id=1, source_target_pairs={{0,256},{256,0},{1,257},{257,1},{2,258},{258,2},{3,259},{259,3},{4... | collective-permute-start | bytes 344072 | tf_op jit(solution)/shard_map/ppermute | solution.py:36
  195.1 9.1 %collective-permute-done.1 = bf16[128,448]{0,1:T(8,128)(2,1)S(1)} collective-permute-done((bf16[128,448]{0,1:T(8,128)(2,1)S(1)}, bf16[128,448]{0,1:T(8,128)(2,1)S(1)}, u32[]{:S(2)}, u32[]{:S(2)}) %collective-permute-start.1) | collective-permute-done | bytes 114720 | tf_op jit(solution)/shard_map/ppermute | solution.py:36
  204.2 0.1 convert_reduce_fusion.1
  204.3 0.9 broadcast_in_dim.32
  205.2 8.0 %all-to-all-start.10 = ((bf16[16,16,1024]{2,1,0:T(8,128)(2,1)}), bf16[16,16,1024]{2,1,0:T(8,128)(2,1)S(1)}, u32[]{:S(2)}, u32[]{:S(2)}) async-start(bf16[16,16,1024]{2,1,0:T(8,128)(2,1)} %bitcast.33), calls=%async_computation.10 | async-start | bytes 1048576 | tf_op jit(solution)/shard_map/all_to_all | solution.py:24
  213.2 1.8 all_gather.51
  215.0 0.7 reshape.106
  215.7 1.3 convolution_convert_fusion.2
  217.0 5.5 %all-to-all-done.10 = bf16[16,16,1024]{2,1,0:T(8,128)(2,1)S(1)} async-done(((bf16[16,16,1024]{2,1,0:T(8,128)(2,1)}), bf16[16,16,1024]{2,1,0:T(8,128)(2,1)S(1)}, u32[]{:S(2)}, u32[]{:S(2)}) %all-to-all-start.10) | async-done | bytes 524320 | tf_op jit(solution)/shard_map/all_to_all | solution.py:24
  222.5 1.3 convolution_convert_fusion.3
  (47 shorter events, 0.4 us)
Async XLA Ops:
  0.6 111.8 %copy-start = (bf16[448,1024]{1,0:T(8,128)(2,1)S(1)}, bf16[448,1024]{1,0:T(8,128)(2,1)}, u32[]{:S(2)}) copy-start(bf16[448,1024]{1,0:T(8,128)(2,1)} %param.13) | copy-start | bytes 2752516
  0.6 24.0 %copy-start.10 = (f32[1024]{0:T(1024)S(1)}, f32[1024]{0:T(1024)}, u32[]{:S(2)}) copy-start(f32[1024]{0:T(1024)} %param.15) | copy-start | bytes 12292
  0.7 37.6 %copy-start.4 = (bf16[56,3584]{1,0:T(8,128)(2,1)S(1)}, bf16[56,3584]{1,0:T(8,128)(2,1)}, u32[]{:S(2)}) copy-start(bf16[56,3584]{1,0:T(8,128)(2,1)} %param.12) | copy-start | bytes 1204228
  2.1 27.9 %all-to-all-start = ((bf16[16,14,128]{2,1,0:T(8,128)(2,1)}), bf16[16,14,128]{2,1,0:T(8,128)(2,1)S(1)}, u32[]{:S(2)}, u32[]{:S(2)}) async-start(bf16[16,14,128]{2,1,0:T(8,128)(2,1)} %broadcast_in_dim.12), calls=%async_computation | async-start | bytes 131072 | tf_op jit(solution)/shard_map/all_to_all | solution.py:24
  30.9 14.9 %all-to-all-start.1 = ((bf16[8,16,14,128]{3,1,2,0:T(8,128)(2,1)}), bf16[8,16,14,128]{3,1,2,0:T(8,128)(2,1)S(1)}, u32[]{:S(2)}, u32[]{:S(2)}) async-start(bf16[8,16,14,128]{3,1,2,0:T(8,128)(2,1)} %broadcast_in_dim.13), calls=%async_computation.1 | async-start | bytes 917504 | tf_op jit(solution)/shard_map/all_to_all | solution.py:24
  48.8 3.5 %copy-start.1 = (bf16[112,3584]{1,0:T(8,128)(2,1)S(1)}, bf16[112,3584]{1,0:T(8,128)(2,1)}, u32[]{:S(2)}) copy-start(bf16[112,3584]{1,0:T(8,128)(2,1)} %all-gather.1) | copy-start | bytes 2408452
  52.2 14.8 %copy-start.2 = (bf16[1024,448]{0,1:T(8,128)(2,1)S(1)}, bf16[1024,448]{0,1:T(8,128)(2,1)}, u32[]{:S(2)}) copy-start(bf16[1024,448]{0,1:T(8,128)(2,1)} %param.14) | copy-start | bytes 2752516
  52.7 41.0 %copy-start.11 = (s32[256]{0:T(256)S(1)}, s32[256]{0:T(256)}, u32[]{:S(2)}) copy-start(s32[256]{0:T(256)} %param.17) | copy-start | bytes 3076
  67.0 42.2 %collective-permute-start = (bf16[448,1024]{1,0:T(8,128)(2,1)S(1)}, bf16[448,1024]{1,0:T(8,128)(2,1)S(1)}, u32[]{:S(2)}, u32[]{:S(2)}) collective-permute-start(bf16[448,1024]{1,0:T(8,128)(2,1)S(1)} %bitcast.73), channel_id=1, source_target_pairs={{0,256},{256,0},{1,257},{257,1},{2,258},{258,2},{3,259},{259,3},{4... | collective-permute-start | bytes 2752520 | tf_op jit(solution)/shard_map/ppermute | solution.py:36
  89.7 19.5 %all-to-all-start.4 = ((bf16[32,8,224]{2,1,0:T(8,128)(2,1)}), bf16[32,8,224]{2,1,0:T(8,128)(2,1)S(1)}, u32[]{:S(2)}, u32[]{:S(2)}) async-start(bf16[32,8,224]{2,1,0:T(8,128)(2,1)} %broadcast_in_dim.14), calls=%async_computation.4 | async-start | bytes 262144 | tf_op jit(solution)/shard_map/all_to_all | solution.py:24
  109.2 4.5 %copy-start.3 = (bf16[448,1024]{1,0:T(8,128)(2,1)}, bf16[448,1024]{1,0:T(8,128)(2,1)S(1)}, u32[]{:S(2)}) copy-start(bf16[448,1024]{1,0:T(8,128)(2,1)S(1)} %collective-permute-done) | copy-start | bytes 2752516
  111.8 0.6 copy-start.6
  112.4 1.3 copy-start.8
  113.7 15.0 %all-to-all-start.5 = ((bf16[16,16,1024]{2,1,0:T(8,128)(2,1)}), bf16[16,16,1024]{2,1,0:T(8,128)(2,1)S(1)}, u32[]{:S(2)}, u32[]{:S(2)}) async-start(bf16[16,16,1024]{2,1,0:T(8,128)(2,1)} %bitcast.16), calls=%async_computation.5 | async-start | bytes 1048576 | tf_op jit(solution)/shard_map/all_to_all | solution.py:24
  129.8 14.7 %all-to-all-start.6 = ((bf16[8,16,2048]{2,1,0:T(8,128)(2,1)}), bf16[8,16,2048]{2,1,0:T(8,128)(2,1)S(1)}, u32[]{:S(2)}, u32[]{:S(2)}) async-start(bf16[8,16,2048]{2,1,0:T(8,128)(2,1)} %broadcast_in_dim.30), calls=%async_computation.6 | async-start | bytes 1048576 | tf_op jit(solution)/shard_map/all_to_all | solution.py:24
  163.8 16.3 %all-to-all-start.8 = ((bf16[16,8,224]{2,1,0:T(8,128)(2,1)}), bf16[16,8,224]{2,1,0:T(8,128)(2,1)S(1)}, u32[]{:S(2)}, u32[]{:S(2)}) async-start(bf16[16,8,224]{2,1,0:T(8,128)(2,1)} %broadcast_in_dim.31), calls=%async_computation.8 | async-start | bytes 131072 | tf_op jit(solution)/shard_map/all_to_all | solution.py:24
  183.4 32.3 %copy-start.5 = (bf16[128,1024]{1,0:T(8,128)(2,1)S(1)}, bf16[128,1024]{1,0:T(8,128)(2,1)}, u32[]{:S(2)}) copy-start(bf16[128,1024]{1,0:T(8,128)(2,1)} %get-tuple-element.67) | copy-start | bytes 786436
  183.4 20.8 %all-to-all-start.9 = ((bf16[8,16,2048]{2,1,0:T(8,128)(2,1)}), bf16[8,16,2048]{2,1,0:T(8,128)(2,1)S(1)}, u32[]{:S(2)}, u32[]{:S(2)}) async-start(bf16[8,16,2048]{2,1,0:T(8,128)(2,1)} %bitcast.30), calls=%async_computation.9 | async-start | bytes 1048576 | tf_op jit(solution)/shard_map/all_to_all | solution.py:24
  189.3 14.9 %collective-permute-start.2 = (bf16[128,1024]{1,0:T(8,128)(2,1)}, bf16[128,1024]{1,0:T(8,128)(2,1)S(1)}, u32[]{:S(2)}, u32[]{:S(2)}) collective-permute-start(bf16[128,1024]{1,0:T(8,128)(2,1)} %get-tuple-element.60), channel_id=1, source_target_pairs={{0,256},{256,0},{1,257},{257,1},{2,258},{258,2},{3,259},{259,3},{4... | collective-permute-start | bytes 786440 | tf_op jit(solution)/shard_map/ppermute | solution.py:36
  191.6 12.5 %collective-permute-start.1 = (bf16[128,448]{0,1:T(8,128)(2,1)S(1)}, bf16[128,448]{0,1:T(8,128)(2,1)S(1)}, u32[]{:S(2)}, u32[]{:S(2)}) collective-permute-start(bf16[128,448]{0,1:T(8,128)(2,1)S(1)} %pad_maximum_fusion.5), channel_id=1, source_target_pairs={{0,256},{256,0},{1,257},{257,1},{2,258},{258,2},{3,259},{259,3},{4... | collective-permute-start | bytes 344072 | tf_op jit(solution)/shard_map/ppermute | solution.py:36
  204.3 18.2 %copy-start.7 = (bf16[256,224]{0,1:T(8,128)(2,1)S(1)}, bf16[256,224]{0,1:T(8,128)(2,1)}, u32[]{:S(2)}) copy-start(bf16[256,224]{0,1:T(8,128)(2,1)} %copy-done.6) | copy-start | bytes 344068
  204.3 18.2 %copy-start.9 = (bf16[256,224]{0,1:T(8,128)(2,1)S(1)}, bf16[256,224]{0,1:T(8,128)(2,1)}, u32[]{:S(2)}) copy-start(bf16[256,224]{0,1:T(8,128)(2,1)} %copy-done.8) | copy-start | bytes 344068
  205.2 17.3 %all-to-all-start.10 = ((bf16[16,16,1024]{2,1,0:T(8,128)(2,1)}), bf16[16,16,1024]{2,1,0:T(8,128)(2,1)S(1)}, u32[]{:S(2)}, u32[]{:S(2)}) async-start(bf16[16,16,1024]{2,1,0:T(8,128)(2,1)} %bitcast.33), calls=%async_computation.10 | async-start | bytes 1048576 | tf_op jit(solution)/shard_map/all_to_all | solution.py:24

commit v7 on v3

--- a/solution.py
+++ b/solution.py
@@ -31,8 +31,8 @@
     return lax.all_gather(x, C, axis=0, tiled=False)
 
 
-def swapped(x):
-    return lax.ppermute(x, C, [(0, 1), (1, 0)])
+def tied(*arrays):
+    return lax.optimization_barrier(arrays)
 
 
 def total(blocks):
@@ -56,36 +56,42 @@
     latents = encoder.shape[1]
     units = gate_weight.shape[1]
 
-    weights = lax.optimization_barrier(jnp.concatenate([gate_weight.T, up_weight.T], axis=0))
     few = sent_to_all(inputs.T, Z)
-
-    few, down = lax.optimization_barrier((few, down_weight))
-    blocks = down.reshape(units, n_hidden, 2, half)
-    kept, given = own(blocks, core, 2), own(blocks, 1 - core, 2)
-    taken = swapped(given)
-    down_pair = jnp.concatenate(
-        [jnp.where(core == 0, kept, taken), jnp.where(core == 0, taken, kept)]
-    ).reshape(2 * units, n_hidden * half)
-
-    every = both_cores(sent_to_all(few, HIDDEN))
+    few, gate_own, up_own, down_own, out_bias = tied(
+        few, gate_weight, up_weight, down_weight, dec_bias
+    )
+    more = sent_to_all(few, HIDDEN)
+    weights = jnp.concatenate([gate_own.T, up_own.T], axis=0)
+    down_pair = both_cores(down_own).reshape(2 * units, -1)
+    bias_mine = own(out_bias.reshape(2, half), core, 0)
+    more, weights, down_pair, bias_mine = tied(more, weights, down_pair, bias_mine)
+    every = both_cores(more)
     gathered = every.transpose(1, 2, 0, 3, 4).reshape(-1, inputs.shape[0])
     acts = jnp.dot(weights, gathered, preferred_element_type=F32)
     hidden = (jax.nn.gelu(acts[:units], approximate=True) * acts[units:]).astype(BF16)
     hidden_pair = both_cores(hidden).reshape(2 * units, -1)
     mine = lax.dot_general(
         down_pair, hidden_pair, (((0,), (0,)), ((), ())), preferred_element_type=F32
-    ).astype(BF16).reshape(n_hidden, half, -1)
+    ).astype(BF16)
+    mine = own(mine.reshape(n_hidden, 2, half, -1), core, 1)
 
     summed = total(exchange(mine, HIDDEN)).T.astype(BF16)
     rows_own = total(exchange(summed.reshape(n_z, -1, half), Z)).astype(BF16)
     mlp_out = both_cores(sent_to_all(rows_own, ROWS_Z).reshape(tokens, half))
 
-    pick = (shuffle_order[:, None] == jnp.arange(tokens)[None, :]).astype(BF16)
+    def picked(order):
+        return (order[:, None] == jnp.arange(tokens)[None, :]).astype(BF16)
+
+    scale = 1.0 / math.sqrt(tokens)
+    count = tokens // n_rows_z
+    order_own = lax.dynamic_slice_in_dim(shuffle_order, lax.axis_index(ROWS_Z) * count, count, 0)
+    target = jnp.dot(picked(order_own), own(mlp_out, core, 0), preferred_element_type=F32)
+    mlp_out, target = tied(mlp_out, target)
+    pick = picked(shuffle_order)
     shuffled = jnp.concatenate(
         [jnp.dot(pick, mlp_out[c], preferred_element_type=F32).astype(BF16) for c in range(2)],
         axis=1,
     )
-    shuffled_t = lax.optimization_barrier(shuffled.T)
     pre_local = jnp.dot(shuffled, encoder, preferred_element_type=F32).astype(BF16)
     pre_act = total(exchange(pre_local.reshape(n_hidden, -1, latents), HIDDEN)) + enc_bias[None, :]
     latent_own = (smooth_scale * jax.nn.softplus(pre_act / smooth_scale)).astype(BF16)
@@ -95,18 +101,8 @@
     ).astype(BF16)
     recon_pair = both_cores(recon_local).reshape(2, 2, half, tokens)
     recon_mine = total(own(recon_pair, core, 1)).T.astype(BF16).reshape(n_rows_z, -1, half)
-    bias_mine = own(dec_bias.reshape(2, half), core, 0)
     recon = total(exchange(recon_mine, ROWS_Z)) + bias_mine[None, :]
-    count = recon.shape[0]
-    both_recon = both_cores(recon.astype(BF16)).reshape(2, 2, count // 2, half)
-    recon_out = own(both_recon, core, 1).transpose(1, 0, 2).reshape(count // 2, width)
-
-    scale = 1.0 / math.sqrt(tokens)
-    first = lax.axis_index(ROWS_Z) * count
-    target = own(
-        lax.dynamic_slice_in_dim(shuffled, first, count, 0).reshape(count, 2, half), core, 1
-    )
-    err_own = (scale * (recon - target.astype(F32))).astype(BF16)
+    err_own = (scale * (recon - target)).astype(BF16)
     err_pair = both_cores(sent_to_all(err_own, ROWS_Z).reshape(tokens, half))
     d_err = jnp.concatenate([err_pair[0], err_pair[1]], axis=1)
 
@@ -121,7 +117,11 @@
         (d_latent + sparsity_weight * scale) * jax.nn.sigmoid(pre_act / smooth_scale)
     ).astype(BF16)
     d_pre = sent_to_all(d_pre_own, HIDDEN).reshape(tokens, latents)
-    grad_enc = jnp.dot(shuffled_t, d_pre, preferred_element_type=F32).astype(BF16)
+    grad_enc = lax.dot_general(
+        shuffled, d_pre, (((0,), (0,)), ((), ())), preferred_element_type=F32
+    ).astype(BF16)
+    both_recon = both_cores(recon.astype(BF16)).reshape(2, 2, count // 2, half)
+    recon_out = own(both_recon, core, 1).transpose(1, 0, 2).reshape(count // 2, width)
     return (recon_out, grad_enc, grad_dec)
 
 

time: 217 us -> 216 us (level)
  blocking collectives: 109 us -> 128 us
  waiting for transfers between devices: 47.4 us -> 37.6 us
  starting transfers between devices: 39.8 us -> 32.1 us
    all_to_all x6 -> x7, blocking collectives: 96.7 us -> 113 us  [exchange(): return lax.all_to_all(blocks, axes, 0, 0, tiled=True)]
    all_to_all x5 -> x4, waiting for transfers between devices: 46.9 us -> 37.6 us  [exchange(): return lax.all_to_all(blocks, axes, 0, 0, tiled=True)]
    all_to_all x5 -> x4, starting transfers between devices: 37.9 us -> 32.1 us  [exchange(): return lax.all_to_all(blocks, axes, 0, 0, tiled=True)]
    all_gather x6 -> x7, blocking collectives: 12.1 us -> 14.6 us  [both_cores(): return lax.all_gather(x, C, axis=0, tiled=False)]
  transfers between devices with their start and end apart: 6 -> 4, of which waited for: 6 -> 4; matrix products, arithmetic and copies ran while one was open for 3% -> 1% of each run, Pallas kernels for 0% -> 0%
where the time goes in v7:
time: 216 us; the launch traced here: 213 us
  blocking collectives  128 us (59%)
  waiting for transfers between devices  37.6 us (17%)
  starting transfers between devices  32.1 us (15%)
  matrix products  6.84 us (3%)
  local copies, waits for them, and re-layouts  6.44 us (3%)
    all_to_all x7, blocking collectives, exchange(): return lax.all_to_all(blocks, axes, 0, 0, tiled=True)  113 us
    all_to_all x4, waiting for transfers between devices, exchange(): return lax.all_to_all(blocks, axes, 0, 0, tiled=True)  37.6 us
    all_to_all x4, starting transfers between devices, exchange(): return lax.all_to_all(blocks, axes, 0, 0, tiled=True)  32.1 us
    all_gather x7, blocking collectives, both_cores(): return lax.all_gather(x, C, axis=0, tiled=False)  14.6 us
  transfers between devices with their start and end apart: 4, of which 4 were waited for; matrix products, arithmetic and copies ran while one was open for 1% of the time, Pallas kernels for 0%

profile of v7, /device:TPU:6, one launch (start us, length us, event | category | flops | bytes accessed | tf_op | source)
XLA Modules:
  0.0 213.1 jit_solution(14880867137789439458)
XLA Ops:
  0.6 0.0 copy-start
  0.6 0.0 copy-start.2
  0.7 1.4 broadcast_in_dim.24
  2.1 15.2 %all-to-all-start = ((bf16[16,14,128]{2,1,0:T(8,128)(2,1)}), bf16[16,14,128]{2,1,0:T(8,128)(2,1)S(1)}, u32[]{:S(2)}, u32[]{:S(2)}) async-start(bf16[16,14,128]{2,1,0:T(8,128)(2,1)} %broadcast_in_dim.24), calls=%async_computation | async-start | bytes 131072 | tf_op jit(solution)/shard_map/all_to_all | solution.py:23
  17.3 12.7 %all-to-all-done = bf16[16,14,128]{2,1,0:T(8,128)(2,1)S(1)} async-done(((bf16[16,14,128]{2,1,0:T(8,128)(2,1)}), bf16[16,14,128]{2,1,0:T(8,128)(2,1)S(1)}, u32[]{:S(2)}, u32[]{:S(2)}) %all-to-all-start) | async-done | bytes 57376 | tf_op jit(solution)/shard_map/all_to_all | solution.py:23
  30.0 0.8 reshape.85
  30.8 0.8 broadcast_in_dim.25
  31.6 7.5 %all-to-all-start.1 = ((bf16[8,16,14,128]{3,1,2,0:T(8,128)(2,1)}), bf16[8,16,14,128]{3,1,2,0:T(8,128)(2,1)S(1)}, u32[]{:S(2)}, u32[]{:S(2)}) async-start(bf16[8,16,14,128]{3,1,2,0:T(8,128)(2,1)} %broadcast_in_dim.25), calls=%async_computation.1 | async-start | bytes 917504 | tf_op jit(solution)/shard_map/all_to_all | solution.py:23
  39.2 0.0 copy-done.2
  39.2 2.5 %all-gather = bf16[112,3584]{1,0:T(8,128)(2,1)} all-gather(bf16[56,3584]{1,0:T(8,128)(2,1)S(1)} %copy-done.2), channel_id=2, replica_groups=mesh['rows'=2,'hidden_0'=2,'hidden_1'=4,'latents_0'=16,'latents_1'=2] {'..., dimensions={0}, use_global_device_ids=true | all-gather | bytes 1204224 | tf_op jit(solution)/shard_map/all_gather | solution.py:31
  41.7 0.0 copy-done.3
  41.7 0.0 copy-done.4
  41.7 0.9 pad_maximum_fusion
  42.6 4.0 %all-to-all-done.1 = bf16[8,16,14,128]{3,1,2,0:T(8,128)(2,1)S(1)} async-done(((bf16[8,16,14,128]{3,1,2,0:T(8,128)(2,1)}), bf16[8,16,14,128]{3,1,2,0:T(8,128)(2,1)S(1)}, u32[]{:S(2)}, u32[]{:S(2)}) %all-to-all-start.1) | async-done | bytes 458784 | tf_op jit(solution)/shard_map/all_to_all | solution.py:23
  46.7 2.5 %all-gather.1 = bf16[16,16,14,128]{3,1,2,0:T(8,128)(2,1)S(1)} all-gather(bf16[8,16,14,128]{3,1,2,0:T(8,128)(2,1)S(1)} %all-to-all-done.1), channel_id=3, replica_groups=mesh['rows'=2,'hidden_0'=2,'hidden_1'=4,'latents_0'=16,'latents_1'=2] {'..., dimensions={0}, use_global_device_ids=true | all-gather | bytes 1376256 | tf_op jit(solution)/shard_map/all_gather | solution.py:31
  49.1 0.3 copy.24
  49.4 0.3 reshape.86
  49.7 0.0 copy-start.1
  49.7 1.6 fusion.28
  51.3 1.8 all-gather.2
  53.2 0.0 copy-done.1
  53.2 0.4 convolution_convert_fusion
  53.7 0.0 copy-start.7
  53.7 14.2 %all_to_all.55 = bf16[8,224,128]{2,1,0:T(8,128)(2,1)S(1)} all-to-all(bf16[8,224,128]{2,1,0:T(8,128)(2,1)S(1)} %dynamic-slice_bitcast_fusion), channel_id=1, replica_groups=mesh['rows'=2,'hidden_0'=2,'hidden_1'=4,'latents_0'=16,'latents_1'=2] {'..., dimensions={0} | all-to-all | bytes 917504 | tf_op jit(solution)/shard_map/all_to_all | solution.py:23
  67.9 0.1 reduce_sum.65
  67.9 0.0 copy-start.6
  67.9 0.1 copy.25
  68.0 15.8 %all_to_all.56 = bf16[16,8,224]{2,1,0:T(8,128)(2,1)S(1)} all-to-all(bf16[16,8,224]{2,1,0:T(8,128)(2,1)S(1)} %bitcast.70), channel_id=1, replica_groups=mesh['rows'=2,'hidden_0'=2,'hidden_1'=4,'latents_0'=16,'latents_1'=2] {'..., dimensions={0} | all-to-all | bytes 114688 | tf_op jit(solution)/shard_map/all_to_all | solution.py:23
  83.8 0.7 broadcast_in_dim.26
  84.5 3.9 %all-to-all-start.4 = ((bf16[32,8,224]{2,1,0:T(8,128)(2,1)}), bf16[32,8,224]{2,1,0:T(8,128)(2,1)S(1)}, u32[]{:S(2)}, u32[]{:S(2)}) async-start(bf16[32,8,224]{2,1,0:T(8,128)(2,1)} %broadcast_in_dim.26), calls=%async_computation.4 | async-start | bytes 262144 | tf_op jit(solution)/shard_map/all_to_all | solution.py:23
  88.4 0.1 dynamic_slice.25
  88.5 15.2 %all-to-all-done.4 = bf16[32,8,224]{2,1,0:T(8,128)(2,1)S(1)} async-done(((bf16[32,8,224]{2,1,0:T(8,128)(2,1)}), bf16[32,8,224]{2,1,0:T(8,128)(2,1)S(1)}, u32[]{:S(2)}, u32[]{:S(2)}) %all-to-all-start.4) | async-done | bytes 114720 | tf_op jit(solution)/shard_map/all_to_all | solution.py:23
  103.7 0.1 copy.26
  103.8 2.0 all_gather.40
  105.8 0.2 fusion.7
  105.9 0.3 convolution_convert_fusion.6
  106.3 0.3 convolution_convert_fusion.7
  106.6 0.0 copy-done.6
  106.6 0.5 convolution_convert_fusion.4
  107.0 0.0 copy-start.5
  107.1 14.8 %all_to_all.57 = bf16[8,32,1024]{2,1,0:T(8,128)(2,1)S(1)} all-to-all(bf16[8,32,1024]{2,1,0:T(8,128)(2,1)S(1)} %bitcast.62), channel_id=1, replica_groups=mesh['rows'=2,'hidden_0'=2,'hidden_1'=4,'latents_0'=16,'latents_1'=2] {'..., dimensions={0} | all-to-all | bytes 1048576 | tf_op jit(solution)/shard_map/all_to_all | solution.py:23
  121.8 0.1 convert_reduce_fusion.1
  121.9 0.1 fusion.2
  122.0 0.1 broadcast_in_dim.27
  122.1 14.1 %all_to_all.58 = bf16[8,32,1024]{2,1,0:T(8,128)(2,1)S(1)} all-to-all(bf16[8,32,1024]{2,1,0:T(8,128)(2,1)S(1)} %broadcast_in_dim.27), channel_id=1, replica_groups=mesh['rows'=2,'hidden_0'=2,'hidden_1'=4,'latents_0'=16,'latents_1'=2] {'..., dimensions={0} | all-to-all | bytes 1048576 | tf_op jit(solution)/shard_map/all_to_all | solution.py:23
  136.2 0.0 copy-done
  136.2 0.4 fusion
  136.7 2.1 %all-gather.3 = bf16[896,256]{1,0:T(8,128)(2,1)S(1)} all-gather(bf16[448,256]{1,0:T(8,128)(2,1)S(1)} %fusion), channel_id=5, replica_groups=mesh['rows'=2,'hidden_0'=2,'hidden_1'=4,'latents_0'=16,'latents_1'=2] {'..., dimensions={0}, use_global_device_ids=true | all-gather | bytes 688128 | tf_op jit(solution)/shard_map/all_gather | solution.py:31
  138.9 0.1 copy.27
  139.0 20.4 %all_to_all.59 = bf16[32,8,224]{2,1,0:T(8,128)(2,1)S(1)} all-to-all(bf16[32,8,224]{2,1,0:T(8,128)(2,1)S(1)} %bitcast.65), channel_id=1, replica_groups=mesh['rows'=2,'hidden_0'=2,'hidden_1'=4,'latents_0'=16,'latents_1'=2] {'..., dimensions={0} | all-to-all | bytes 229376 | tf_op jit(solution)/shard_map/all_to_all | solution.py:23
  159.4 19.2 %all_to_all.60 = bf16[32,8,224]{2,1,0:T(8,128)(2,1)S(1)} all-to-all(bf16[32,8,224]{2,1,0:T(8,128)(2,1)S(1)} %broadcast_in_dim.28), channel_id=1, replica_groups=mesh['rows'=2,'hidden_0'=2,'hidden_1'=4,'latents_0'=16,'latents_1'=2] {'..., dimensions={0} | all-to-all | bytes 229376 | tf_op jit(solution)/shard_map/all_to_all | solution.py:23
  178.6 0.1 copy.30
  178.7 2.0 all_gather.44
  180.7 0.5 convolution_convert_fusion.3
  181.2 14.6 %all_to_all.61 = bf16[8,32,1024]{2,1,0:T(8,128)(2,1)S(1)} all-to-all(bf16[8,32,1024]{2,1,0:T(8,128)(2,1)S(1)} %bitcast.63), channel_id=1, replica_groups=mesh['rows'=2,'hidden_0'=2,'hidden_1'=4,'latents_0'=16,'latents_1'=2] {'..., dimensions={0} | all-to-all | bytes 1048576 | tf_op jit(solution)/shard_map/all_to_all | solution.py:23
  195.8 0.1 convert_reduce_fusion
  195.8 0.1 multiply_convert_fusion
  195.9 0.9 broadcast_in_dim.29
  196.8 5.5 %all-to-all-start.10 = ((bf16[8,32,1024]{2,1,0:T(8,128)(2,1)}), bf16[8,32,1024]{2,1,0:T(8,128)(2,1)S(1)}, u32[]{:S(2)}, u32[]{:S(2)}) async-start(bf16[8,32,1024]{2,1,0:T(8,128)(2,1)} %broadcast_in_dim.29), calls=%async_computation.10 | async-start | bytes 1048576 | tf_op jit(solution)/shard_map/all_to_all | solution.py:23
  202.3 1.8 all_gather.43
  204.1 0.7 reshape.95
  204.8 1.3 convolution_convert_fusion.1
  206.1 5.6 %all-to-all-done.10 = bf16[8,32,1024]{2,1,0:T(8,128)(2,1)S(1)} async-done(((bf16[8,32,1024]{2,1,0:T(8,128)(2,1)}), bf16[8,32,1024]{2,1,0:T(8,128)(2,1)S(1)}, u32[]{:S(2)}, u32[]{:S(2)}) %all-to-all-start.10) | async-done | bytes 524320 | tf_op jit(solution)/shard_map/all_to_all | solution.py:23
  211.7 1.3 convolution_convert_fusion.2
  (18 shorter events, 0.2 us)
Async XLA Ops:
  0.6 135.6 %copy-start = (bf16[1024,448]{0,1:T(8,128)(2,1)S(1)}, bf16[1024,448]{0,1:T(8,128)(2,1)}, u32[]{:S(2)}) copy-start(bf16[1024,448]{0,1:T(8,128)(2,1)} %param.14) | copy-start | bytes 2752516
  0.6 38.5 %copy-start.2 = (bf16[56,3584]{1,0:T(8,128)(2,1)S(1)}, bf16[56,3584]{1,0:T(8,128)(2,1)}, u32[]{:S(2)}) copy-start(bf16[56,3584]{1,0:T(8,128)(2,1)} %param.12) | copy-start | bytes 1204228
  2.1 27.9 %all-to-all-start = ((bf16[16,14,128]{2,1,0:T(8,128)(2,1)}), bf16[16,14,128]{2,1,0:T(8,128)(2,1)S(1)}, u32[]{:S(2)}, u32[]{:S(2)}) async-start(bf16[16,14,128]{2,1,0:T(8,128)(2,1)} %broadcast_in_dim.24), calls=%async_computation | async-start | bytes 131072 | tf_op jit(solution)/shard_map/all_to_all | solution.py:23
  31.6 10.1 %copy-start.3 = (bf16[3584,56]{0,1:T(8,128)(2,1)S(1)}, bf16[3584,56]{0,1:T(8,128)(2,1)}, u32[]{:S(2)}) copy-start(bf16[3584,56]{0,1:T(8,128)(2,1)} %param.11) | copy-start | bytes 1204228
  31.6 10.1 %copy-start.4 = (bf16[3584,56]{0,1:T(8,128)(2,1)S(1)}, bf16[3584,56]{0,1:T(8,128)(2,1)}, u32[]{:S(2)}) copy-start(bf16[3584,56]{0,1:T(8,128)(2,1)} %param.10) | copy-start | bytes 1204228
  31.6 15.0 %all-to-all-start.1 = ((bf16[8,16,14,128]{3,1,2,0:T(8,128)(2,1)}), bf16[8,16,14,128]{3,1,2,0:T(8,128)(2,1)S(1)}, u32[]{:S(2)}, u32[]{:S(2)}) async-start(bf16[8,16,14,128]{3,1,2,0:T(8,128)(2,1)} %broadcast_in_dim.25), calls=%async_computation.1 | async-start | bytes 917504 | tf_op jit(solution)/shard_map/all_to_all | solution.py:23
  49.7 3.5 %copy-start.1 = (bf16[112,3584]{1,0:T(8,128)(2,1)S(1)}, bf16[112,3584]{1,0:T(8,128)(2,1)}, u32[]{:S(2)}) copy-start(bf16[112,3584]{1,0:T(8,128)(2,1)} %all-gather) | copy-start | bytes 2408452
  53.7 34.7 %copy-start.7 = (s32[256]{0:T(256)S(1)}, s32[256]{0:T(256)}, u32[]{:S(2)}) copy-start(s32[256]{0:T(256)} %param.17) | copy-start | bytes 3076
  67.9 38.6 %copy-start.6 = (bf16[448,1024]{1,0:T(8,128)(2,1)S(1)}, bf16[448,1024]{1,0:T(8,128)(2,1)}, u32[]{:S(2)}) copy-start(bf16[448,1024]{1,0:T(8,128)(2,1)} %param.13) | copy-start | bytes 2752516
  84.5 19.2 %all-to-all-start.4 = ((bf16[32,8,224]{2,1,0:T(8,128)(2,1)}), bf16[32,8,224]{2,1,0:T(8,128)(2,1)S(1)}, u32[]{:S(2)}, u32[]{:S(2)}) async-start(bf16[32,8,224]{2,1,0:T(8,128)(2,1)} %broadcast_in_dim.26), calls=%async_computation.4 | async-start | bytes 262144 | tf_op jit(solution)/shard_map/all_to_all | solution.py:23
  107.0 14.9 %copy-start.5 = (f32[1024]{0:T(1024)S(1)}, f32[1024]{0:T(1024)}, u32[]{:S(2)}) copy-start(f32[1024]{0:T(1024)} %param.15) | copy-start | bytes 12292
  196.8 15.0 %all-to-all-start.10 = ((bf16[8,32,1024]{2,1,0:T(8,128)(2,1)}), bf16[8,32,1024]{2,1,0:T(8,128)(2,1)S(1)}, u32[]{:S(2)}, u32[]{:S(2)}) async-start(bf16[8,32,1024]{2,1,0:T(8,128)(2,1)} %broadcast_in_dim.29), calls=%async_computation.10 | async-start | bytes 1048576 | tf_op jit(solution)/shard_map/all_to_all | solution.py:23

commit v8 on v7

--- a/solution.py
+++ b/solution.py
@@ -23,8 +23,12 @@
     return lax.all_to_all(blocks, axes, 0, 0, tiled=True)
 
 
+def copies_of(x, axes):
+    return jnp.broadcast_to(x, (lax.axis_size(axes), *x.shape))
+
+
 def sent_to_all(x, axes):
-    return exchange(jnp.broadcast_to(x, (lax.axis_size(axes), *x.shape)), axes)
+    return exchange(copies_of(x, axes), axes)
 
 
 def both_cores(x):
@@ -57,14 +61,18 @@
     units = gate_weight.shape[1]
 
     few = sent_to_all(inputs.T, Z)
-    few, gate_own, up_own, down_own, out_bias = tied(
-        few, gate_weight, up_weight, down_weight, dec_bias
+    copies, gate_own, up_own, down_own, order, out_bias = tied(
+        copies_of(few, HIDDEN), gate_weight, up_weight, down_weight, shuffle_order, dec_bias
     )
-    more = sent_to_all(few, HIDDEN)
+    more = exchange(copies, HIDDEN)
     weights = jnp.concatenate([gate_own.T, up_own.T], axis=0)
     down_pair = both_cores(down_own).reshape(2 * units, -1)
-    bias_mine = own(out_bias.reshape(2, half), core, 0)
-    more, weights, down_pair, bias_mine = tied(more, weights, down_pair, bias_mine)
+    count = tokens // n_rows_z
+    order_own = lax.dynamic_slice_in_dim(order, lax.axis_index(ROWS_Z) * count, count, 0)
+    bias_mine = lax.dynamic_slice_in_dim(out_bias, core * half, half, 0)
+    more, weights, down_pair, order_own, bias_mine = tied(
+        more, weights, down_pair, order_own, bias_mine
+    )
     every = both_cores(more)
     gathered = every.transpose(1, 2, 0, 3, 4).reshape(-1, inputs.shape[0])
     acts = jnp.dot(weights, gathered, preferred_element_type=F32)
@@ -83,8 +91,6 @@
         return (order[:, None] == jnp.arange(tokens)[None, :]).astype(BF16)
 
     scale = 1.0 / math.sqrt(tokens)
-    count = tokens // n_rows_z
-    order_own = lax.dynamic_slice_in_dim(shuffle_order, lax.axis_index(ROWS_Z) * count, count, 0)
     target = jnp.dot(picked(order_own), own(mlp_out, core, 0), preferred_element_type=F32)
     mlp_out, target = tied(mlp_out, target)
     pick = picked(shuffle_order)

time: 216 us -> 214 us (level)
  blocking collectives: 128 us -> 146 us
  waiting for transfers between devices: 37.6 us -> 22.2 us
  starting transfers between devices: 32.1 us -> 28.3 us
    all_to_all x7 -> x8, blocking collectives: 113 us -> 131 us  [exchange(): return lax.all_to_all(blocks, axes, 0, 0, tiled=True)]
    all_to_all x4 -> x3, waiting for transfers between devices: 37.6 us -> 22.2 us  [exchange(): return lax.all_to_all(blocks, axes, 0, 0, tiled=True)]
    all_to_all x4 -> x3, starting transfers between devices: 32.1 us -> 28.3 us  [exchange(): return lax.all_to_all(blocks, axes, 0, 0, tiled=True)]
  transfers between devices with their start and end apart: 4 -> 3, of which waited for: 4 -> 3; matrix products, arithmetic and copies ran while one was open for 1% -> 1% of each run, Pallas kernels for 0% -> 0%
where the time goes in v8:
time: 214 us; the launch traced here: 211 us
  blocking collectives  146 us (68%)
  starting transfers between devices  28.3 us (13%)
  waiting for transfers between devices  22.2 us (10%)
  matrix products  6.81 us (3%)
  local copies, waits for them, and re-layouts  5.09 us (2%)
    all_to_all x8, blocking collectives, exchange(): return lax.all_to_all(blocks, axes, 0, 0, tiled=True)  131 us
    all_to_all x3, starting transfers between devices, exchange(): return lax.all_to_all(blocks, axes, 0, 0, tiled=True)  28.3 us
    all_to_all x3, waiting for transfers between devices, exchange(): return lax.all_to_all(blocks, axes, 0, 0, tiled=True)  22.2 us
    all_gather x7, blocking collectives, both_cores(): return lax.all_gather(x, C, axis=0, tiled=False)  14.6 us
  transfers between devices with their start and end apart: 3, of which 3 were waited for; matrix products, arithmetic and copies ran while one was open for 1% of the time, Pallas kernels for 0%

profile of v8, /device:TPU:6, one launch (start us, length us, event | category | flops | bytes accessed | tf_op | source)
XLA Modules:
  0.0 210.8 jit_solution(3733474141199971630)
XLA Ops:
  0.6 0.0 copy-start
  0.6 0.0 copy-start.2
  0.7 1.4 broadcast_in_dim.24
  2.1 15.2 %all-to-all-start = ((bf16[16,14,128]{2,1,0:T(8,128)(2,1)}), bf16[16,14,128]{2,1,0:T(8,128)(2,1)S(1)}, u32[]{:S(2)}, u32[]{:S(2)}) async-start(bf16[16,14,128]{2,1,0:T(8,128)(2,1)} %broadcast_in_dim.24), calls=%async_computation | async-start | bytes 131072 | tf_op jit(solution)/shard_map/all_to_all | solution.py:23
  17.3 12.7 %all-to-all-done = bf16[16,14,128]{2,1,0:T(8,128)(2,1)S(1)} async-done(((bf16[16,14,128]{2,1,0:T(8,128)(2,1)}), bf16[16,14,128]{2,1,0:T(8,128)(2,1)S(1)}, u32[]{:S(2)}, u32[]{:S(2)}) %all-to-all-start) | async-done | bytes 57376 | tf_op jit(solution)/shard_map/all_to_all | solution.py:23
  30.0 0.8 broadcast_in_dim.25
  30.9 7.5 %all-to-all-start.1 = ((bf16[8,16,14,128]{3,1,2,0:T(8,128)(2,1)}), bf16[8,16,14,128]{3,1,2,0:T(8,128)(2,1)S(1)}, u32[]{:S(2)}, u32[]{:S(2)}) async-start(bf16[8,16,14,128]{3,1,2,0:T(8,128)(2,1)} %broadcast_in_dim.25), calls=%async_computation.1 | async-start | bytes 917504 | tf_op jit(solution)/shard_map/all_to_all | solution.py:23
  38.4 0.0 copy-done.2
  38.4 2.5 %all-gather = bf16[112,3584]{1,0:T(8,128)(2,1)} all-gather(bf16[56,3584]{1,0:T(8,128)(2,1)S(1)} %copy-done.2), channel_id=2, replica_groups=mesh['rows'=2,'hidden_0'=2,'hidden_1'=4,'latents_0'=16,'latents_1'=2] {'..., dimensions={0}, use_global_device_ids=true | all-gather | bytes 1204224 | tf_op jit(solution)/shard_map/all_gather | solution.py:35
  40.9 0.0 copy-done.8
  40.9 0.1 dynamic_slice.22
  41.0 0.0 copy-done.6
  41.0 0.1 dynamic_slice.23
  41.1 0.0 copy-done.3
  41.1 0.0 copy-done.4
  41.1 0.9 pad_maximum_fusion
  42.0 3.9 %all-to-all-done.1 = bf16[8,16,14,128]{3,1,2,0:T(8,128)(2,1)S(1)} async-done(((bf16[8,16,14,128]{3,1,2,0:T(8,128)(2,1)}), bf16[8,16,14,128]{3,1,2,0:T(8,128)(2,1)S(1)}, u32[]{:S(2)}, u32[]{:S(2)}) %all-to-all-start.1) | async-done | bytes 458784 | tf_op jit(solution)/shard_map/all_to_all | solution.py:23
  45.9 2.5 %all-gather.1 = bf16[16,16,14,128]{3,1,2,0:T(8,128)(2,1)S(1)} all-gather(bf16[8,16,14,128]{3,1,2,0:T(8,128)(2,1)S(1)} %all-to-all-done.1), channel_id=3, replica_groups=mesh['rows'=2,'hidden_0'=2,'hidden_1'=4,'latents_0'=16,'latents_1'=2] {'..., dimensions={0}, use_global_device_ids=true | all-gather | bytes 1376256 | tf_op jit(solution)/shard_map/all_gather | solution.py:35
  48.4 0.3 copy.24
  48.7 0.3 reshape.82
  48.9 0.0 copy-start.1
  48.9 1.6 fusion.28
  50.6 1.8 all-gather.2
  52.4 0.0 copy-done.1
  52.4 0.4 convolution_convert_fusion
  52.9 14.2 %all_to_all.55 = bf16[8,224,128]{2,1,0:T(8,128)(2,1)S(1)} all-to-all(bf16[8,224,128]{2,1,0:T(8,128)(2,1)S(1)} %dynamic-slice_bitcast_fusion), channel_id=1, replica_groups=mesh['rows'=2,'hidden_0'=2,'hidden_1'=4,'latents_0'=16,'latents_1'=2] {'..., dimensions={0} | all-to-all | bytes 917504 | tf_op jit(solution)/shard_map/all_to_all | solution.py:23
  67.1 0.1 reduce_sum.65
  67.1 0.0 copy-start.7
  67.2 0.1 copy.25
  67.3 15.8 %all_to_all.56 = bf16[16,8,224]{2,1,0:T(8,128)(2,1)S(1)} all-to-all(bf16[16,8,224]{2,1,0:T(8,128)(2,1)S(1)} %bitcast.69), channel_id=1, replica_groups=mesh['rows'=2,'hidden_0'=2,'hidden_1'=4,'latents_0'=16,'latents_1'=2] {'..., dimensions={0} | all-to-all | bytes 114688 | tf_op jit(solution)/shard_map/all_to_all | solution.py:23
  83.1 18.5 %all_to_all.57 = bf16[32,8,224]{2,1,0:T(8,128)(2,1)S(1)} all-to-all(bf16[32,8,224]{2,1,0:T(8,128)(2,1)S(1)} %broadcast_in_dim.26), channel_id=1, replica_groups=mesh['rows'=2,'hidden_0'=2,'hidden_1'=4,'latents_0'=16,'latents_1'=2] {'..., dimensions={0} | all-to-all | bytes 229376 | tf_op jit(solution)/shard_map/all_to_all | solution.py:23
  101.5 0.1 copy.26
  101.7 2.0 all_gather.40
  103.6 0.2 fusion.7
  103.8 0.3 convolution_convert_fusion.6
  104.1 0.3 convolution_convert_fusion.7
  104.4 0.0 copy-done.7
  104.4 0.5 convolution_convert_fusion.4
  104.9 0.0 copy-start.5
  104.9 15.1 %all_to_all.58 = bf16[8,32,1024]{2,1,0:T(8,128)(2,1)S(1)} all-to-all(bf16[8,32,1024]{2,1,0:T(8,128)(2,1)S(1)} %bitcast.61), channel_id=1, replica_groups=mesh['rows'=2,'hidden_0'=2,'hidden_1'=4,'latents_0'=16,'latents_1'=2] {'..., dimensions={0} | all-to-all | bytes 1048576 | tf_op jit(solution)/shard_map/all_to_all | solution.py:23
  120.0 0.1 convert_reduce_fusion.1
  120.1 0.0 copy-done.5
  120.1 0.1 fusion.2
  120.2 0.1 broadcast_in_dim.27
  120.3 13.7 %all_to_all.59 = bf16[8,32,1024]{2,1,0:T(8,128)(2,1)S(1)} all-to-all(bf16[8,32,1024]{2,1,0:T(8,128)(2,1)S(1)} %broadcast_in_dim.27), channel_id=1, replica_groups=mesh['rows'=2,'hidden_0'=2,'hidden_1'=4,'latents_0'=16,'latents_1'=2] {'..., dimensions={0} | all-to-all | bytes 1048576 | tf_op jit(solution)/shard_map/all_to_all | solution.py:23
  134.0 0.0 copy-done
  134.0 0.4 fusion
  134.5 2.1 %all-gather.3 = bf16[896,256]{1,0:T(8,128)(2,1)S(1)} all-gather(bf16[448,256]{1,0:T(8,128)(2,1)S(1)} %fusion), channel_id=5, replica_groups=mesh['rows'=2,'hidden_0'=2,'hidden_1'=4,'latents_0'=16,'latents_1'=2] {'..., dimensions={0}, use_global_device_ids=true | all-gather | bytes 688128 | tf_op jit(solution)/shard_map/all_gather | solution.py:35
  136.6 0.1 copy.27
  136.8 20.4 %all_to_all.60 = bf16[32,8,224]{2,1,0:T(8,128)(2,1)S(1)} all-to-all(bf16[32,8,224]{2,1,0:T(8,128)(2,1)S(1)} %bitcast.64), channel_id=1, replica_groups=mesh['rows'=2,'hidden_0'=2,'hidden_1'=4,'latents_0'=16,'latents_1'=2] {'..., dimensions={0} | all-to-all | bytes 229376 | tf_op jit(solution)/shard_map/all_to_all | solution.py:23
  157.2 19.2 %all_to_all.61 = bf16[32,8,224]{2,1,0:T(8,128)(2,1)S(1)} all-to-all(bf16[32,8,224]{2,1,0:T(8,128)(2,1)S(1)} %broadcast_in_dim.28), channel_id=1, replica_groups=mesh['rows'=2,'hidden_0'=2,'hidden_1'=4,'latents_0'=16,'latents_1'=2] {'..., dimensions={0} | all-to-all | bytes 229376 | tf_op jit(solution)/shard_map/all_to_all | solution.py:23
  176.4 0.1 copy.30
  176.5 2.0 all_gather.44
  178.5 0.5 convolution_convert_fusion.3
  178.9 14.6 %all_to_all.62 = bf16[8,32,1024]{2,1,0:T(8,128)(2,1)S(1)} all-to-all(bf16[8,32,1024]{2,1,0:T(8,128)(2,1)S(1)} %bitcast.62), channel_id=1, replica_groups=mesh['rows'=2,'hidden_0'=2,'hidden_1'=4,'latents_0'=16,'latents_1'=2] {'..., dimensions={0} | all-to-all | bytes 1048576 | tf_op jit(solution)/shard_map/all_to_all | solution.py:23
  193.5 0.1 convert_reduce_fusion
  193.6 0.1 multiply_convert_fusion
  193.7 0.9 broadcast_in_dim.29
  194.5 5.5 %all-to-all-start.10 = ((bf16[8,32,1024]{2,1,0:T(8,128)(2,1)}), bf16[8,32,1024]{2,1,0:T(8,128)(2,1)S(1)}, u32[]{:S(2)}, u32[]{:S(2)}) async-start(bf16[8,32,1024]{2,1,0:T(8,128)(2,1)} %broadcast_in_dim.29), calls=%async_computation.10 | async-start | bytes 1048576 | tf_op jit(solution)/shard_map/all_to_all | solution.py:23
  200.1 1.8 all_gather.43
  201.9 0.7 reshape.91
  202.6 1.3 convolution_convert_fusion.1
  203.9 5.6 %all-to-all-done.10 = bf16[8,32,1024]{2,1,0:T(8,128)(2,1)S(1)} async-done(((bf16[8,32,1024]{2,1,0:T(8,128)(2,1)}), bf16[8,32,1024]{2,1,0:T(8,128)(2,1)S(1)}, u32[]{:S(2)}, u32[]{:S(2)}) %all-to-all-start.10) | async-done | bytes 524320 | tf_op jit(solution)/shard_map/all_to_all | solution.py:23
  209.5 1.3 convolution_convert_fusion.2
  (18 shorter events, 0.3 us)
Async XLA Ops:
  0.6 133.4 %copy-start = (bf16[1024,448]{0,1:T(8,128)(2,1)S(1)}, bf16[1024,448]{0,1:T(8,128)(2,1)}, u32[]{:S(2)}) copy-start(bf16[1024,448]{0,1:T(8,128)(2,1)} %param.14) | copy-start | bytes 2752516
  0.6 37.8 %copy-start.2 = (bf16[56,3584]{1,0:T(8,128)(2,1)S(1)}, bf16[56,3584]{1,0:T(8,128)(2,1)}, u32[]{:S(2)}) copy-start(bf16[56,3584]{1,0:T(8,128)(2,1)} %param.12) | copy-start | bytes 1204228
  2.1 27.9 %all-to-all-start = ((bf16[16,14,128]{2,1,0:T(8,128)(2,1)}), bf16[16,14,128]{2,1,0:T(8,128)(2,1)S(1)}, u32[]{:S(2)}, u32[]{:S(2)}) async-start(bf16[16,14,128]{2,1,0:T(8,128)(2,1)} %broadcast_in_dim.24), calls=%async_computation | async-start | bytes 131072 | tf_op jit(solution)/shard_map/all_to_all | solution.py:23
  30.9 10.1 %copy-start.8 = (s32[256]{0:T(256)S(1)}, s32[256]{0:T(256)}, u32[]{:S(2)}) copy-start(s32[256]{0:T(256)} %param.17) | copy-start | bytes 3076
  30.9 10.1 %copy-start.6 = (f32[448]{0:T(512)S(1)}, f32[448]{0:T(512)}, u32[]{:S(2)}) copy-start(f32[448]{0:T(512)} %param.16) | copy-start | bytes 5380
  30.9 10.2 %copy-start.3 = (bf16[3584,56]{0,1:T(8,128)(2,1)S(1)}, bf16[3584,56]{0,1:T(8,128)(2,1)}, u32[]{:S(2)}) copy-start(bf16[3584,56]{0,1:T(8,128)(2,1)} %param.11) | copy-start | bytes 1204228
  30.9 10.2 %copy-start.4 = (bf16[3584,56]{0,1:T(8,128)(2,1)S(1)}, bf16[3584,56]{0,1:T(8,128)(2,1)}, u32[]{:S(2)}) copy-start(bf16[3584,56]{0,1:T(8,128)(2,1)} %param.10) | copy-start | bytes 1204228
  30.9 15.1 %all-to-all-start.1 = ((bf16[8,16,14,128]{3,1,2,0:T(8,128)(2,1)}), bf16[8,16,14,128]{3,1,2,0:T(8,128)(2,1)S(1)}, u32[]{:S(2)}, u32[]{:S(2)}) async-start(bf16[8,16,14,128]{3,1,2,0:T(8,128)(2,1)} %broadcast_in_dim.25), calls=%async_computation.1 | async-start | bytes 917504 | tf_op jit(solution)/shard_map/all_to_all | solution.py:23
  48.9 3.5 %copy-start.1 = (bf16[112,3584]{1,0:T(8,128)(2,1)S(1)}, bf16[112,3584]{1,0:T(8,128)(2,1)}, u32[]{:S(2)}) copy-start(bf16[112,3584]{1,0:T(8,128)(2,1)} %all-gather) | copy-start | bytes 2408452
  67.1 37.3 %copy-start.7 = (bf16[448,1024]{1,0:T(8,128)(2,1)S(1)}, bf16[448,1024]{1,0:T(8,128)(2,1)}, u32[]{:S(2)}) copy-start(bf16[448,1024]{1,0:T(8,128)(2,1)} %param.13) | copy-start | bytes 2752516
  104.9 15.2 %copy-start.5 = (f32[1024]{0:T(1024)S(1)}, f32[1024]{0:T(1024)}, u32[]{:S(2)}) copy-start(f32[1024]{0:T(1024)} %param.15) | copy-start | bytes 12292
  194.5 15.0 %all-to-all-start.10 = ((bf16[8,32,1024]{2,1,0:T(8,128)(2,1)}), bf16[8,32,1024]{2,1,0:T(8,128)(2,1)S(1)}, u32[]{:S(2)}, u32[]{:S(2)}) async-start(bf16[8,32,1024]{2,1,0:T(8,128)(2,1)} %broadcast_in_dim.29), calls=%async_computation.10 | async-start | bytes 1048576 | tf_op jit(solution)/shard_map/all_to_all | solution.py:23

commit v9 on v8

--- a/solution.py
+++ b/solution.py
@@ -3,6 +3,8 @@
 import jax
 import jax.numpy as jnp
 from jax import lax
+from jax.experimental import pallas as pl
+from jax.experimental.pallas import tpu as pltpu
 from jax.sharding import Mesh
 from jax.sharding import PartitionSpec as P
 
@@ -47,6 +49,30 @@
     return lax.dynamic_index_in_dim(x, index, dim, keepdims=False)
 
 
+def gated_kernel(gate_ref, up_ref, x_ref, hidden_ref):
+    gate_act = jnp.dot(gate_ref[...], x_ref[...], preferred_element_type=F32)
+    up_act = jnp.dot(up_ref[...], x_ref[...], preferred_element_type=F32)
+    hidden_ref[...] = (jax.nn.gelu(gate_act, approximate=True) * up_act).astype(BF16)
+
+
+def gated(gate, up, x):
+    units, width = gate.shape
+    count = x.shape[1]
+    whole = pl.BlockSpec(memory_space=pltpu.VMEM)
+    return pl.pallas_call(
+        gated_kernel,
+        in_specs=[whole] * 3,
+        out_specs=whole,
+        out_shape=jax.ShapeDtypeStruct((units, count), BF16),
+        compiler_params=pltpu.CompilerParams(vmem_limit_bytes=16 * 2**20),
+        cost_estimate=pl.CostEstimate(
+            flops=4 * units * width * count,
+            bytes_accessed=2 * width * (2 * units + count),
+            transcendentals=units * count,
+        ),
+    )(gate, up, x)
+
+
 def shards(
     inputs, gate_weight, up_weight, down_weight, encoder, decoder, enc_bias, dec_bias, shuffle_order
 ):
@@ -65,18 +91,16 @@
         copies_of(few, HIDDEN), gate_weight, up_weight, down_weight, shuffle_order, dec_bias
     )
     more = exchange(copies, HIDDEN)
-    weights = jnp.concatenate([gate_own.T, up_own.T], axis=0)
     down_pair = both_cores(down_own).reshape(2 * units, -1)
     count = tokens // n_rows_z
     order_own = lax.dynamic_slice_in_dim(order, lax.axis_index(ROWS_Z) * count, count, 0)
     bias_mine = lax.dynamic_slice_in_dim(out_bias, core * half, half, 0)
-    more, weights, down_pair, order_own, bias_mine = tied(
-        more, weights, down_pair, order_own, bias_mine
+    more, gate_own, up_own, down_pair, order_own, bias_mine = tied(
+        more, gate_own, up_own, down_pair, order_own, bias_mine
     )
     every = both_cores(more)
     gathered = every.transpose(1, 2, 0, 3, 4).reshape(-1, inputs.shape[0])
-    acts = jnp.dot(weights, gathered, preferred_element_type=F32)
-    hidden = (jax.nn.gelu(acts[:units], approximate=True) * acts[units:]).astype(BF16)
+    hidden = gated(gate_own.T, up_own.T, gathered)
     hidden_pair = both_cores(hidden).reshape(2 * units, -1)
     mine = lax.dot_general(
         down_pair, hidden_pair, (((0,), (0,)), ((), ())), preferred_element_type=F32

time: 214 us -> 214 us (level)
  blocking collectives: 146 us -> 173 us
  starting transfers between devices: 28.3 us -> 12.9 us
  waiting for transfers between devices: 22.2 us -> 10.6 us
    all_to_all x8 -> x9, blocking collectives: 131 us -> 159 us  [exchange(): return lax.all_to_all(blocks, axes, 0, 0, tiled=True)]
    all_to_all x3 -> x2, starting transfers between devices: 28.3 us -> 12.9 us  [exchange(): return lax.all_to_all(blocks, axes, 0, 0, tiled=True)]
    all_to_all x3 -> x2, waiting for transfers between devices: 22.2 us -> 10.6 us  [exchange(): return lax.all_to_all(blocks, axes, 0, 0, tiled=True)]
  transfers between devices with their start and end apart: 3 -> 2, of which waited for: 3 -> 2; matrix products, arithmetic and copies ran while one was open for 1% -> 1% of each run, Pallas kernels for 0% -> 0%
where the time goes in v9:
time: 214 us; the launch traced here: 211 us
  blocking collectives  173 us (81%)
  starting transfers between devices  12.9 us (6%)
  waiting for transfers between devices  10.6 us (5%)
  local copies, waits for them, and re-layouts  6.62 us (3%)
  matrix products  5.24 us (2%)
    all_to_all x9, blocking collectives, exchange(): return lax.all_to_all(blocks, axes, 0, 0, tiled=True)  159 us
    all_gather x7, blocking collectives, both_cores(): return lax.all_gather(x, C, axis=0, tiled=False)  14.5 us
    all_to_all x2, starting transfers between devices, exchange(): return lax.all_to_all(blocks, axes, 0, 0, tiled=True)  12.9 us
    all_to_all x2, waiting for transfers between devices, exchange(): return lax.all_to_all(blocks, axes, 0, 0, tiled=True)  10.6 us
  transfers between devices with their start and end apart: 2, of which 2 were waited for; matrix products, arithmetic and copies ran while one was open for 1% of the time, Pallas kernels for 0%

profile of v9, /device:TPU:6, one launch (start us, length us, event | category | flops | bytes accessed | tf_op | source)
XLA Modules:
  0.0 210.5 jit_solution(9647414373872075647)
XLA Ops:
  0.6 0.0 copy-start
  0.6 0.0 copy-start.7
  0.7 0.0 copy-start.5
  0.7 0.0 copy-start.3
  0.7 0.8 broadcast_in_dim.24
  1.5 27.7 %all_to_all.55 = bf16[16,14,128]{2,1,0:T(8,128)(2,1)S(1)} all-to-all(bf16[16,14,128]{2,1,0:T(8,128)(2,1)S(1)} %broadcast_in_dim.24), channel_id=1, replica_groups=mesh['rows'=2,'hidden_0'=2,'hidden_1'=4,'latents_0'=16,'latents_1'=2] {'..., dimensions={0} | all-to-all | bytes 114688 | tf_op jit(solution)/shard_map/all_to_all | solution.py:25
  29.2 0.8 broadcast_in_dim.25
  30.0 7.4 %all-to-all-start.1 = ((bf16[8,16,14,128]{3,1,2,0:T(8,128)(2,1)}), bf16[8,16,14,128]{3,1,2,0:T(8,128)(2,1)S(1)}, u32[]{:S(2)}, u32[]{:S(2)}) async-start(bf16[8,16,14,128]{3,1,2,0:T(8,128)(2,1)} %broadcast_in_dim.25), calls=%async_computation.1 | async-start | bytes 917504 | tf_op jit(solution)/shard_map/all_to_all | solution.py:25
  37.4 0.0 copy-done.7
  37.5 0.1 dynamic_slice.22
  37.5 0.0 copy-done.5
  37.5 0.1 dynamic_slice.23
  37.6 0.0 copy-done.3
  37.6 2.4 %all-gather = bf16[112,3584]{1,0:T(8,128)(2,1)S(1)} all-gather(bf16[56,3584]{1,0:T(8,128)(2,1)S(1)} %copy-done.3), channel_id=2, replica_groups=mesh['rows'=2,'hidden_0'=2,'hidden_1'=4,'latents_0'=16,'latents_1'=2] {'..., dimensions={0}, use_global_device_ids=true | all-gather | bytes 1204224 | tf_op jit(solution)/shard_map/all_gather | solution.py:37
  40.0 5.0 %all-to-all-done.1 = bf16[8,16,14,128]{3,1,2,0:T(8,128)(2,1)S(1)} async-done(((bf16[8,16,14,128]{3,1,2,0:T(8,128)(2,1)}), bf16[8,16,14,128]{3,1,2,0:T(8,128)(2,1)S(1)}, u32[]{:S(2)}, u32[]{:S(2)}) %all-to-all-start.1) | async-done | bytes 458784 | tf_op jit(solution)/shard_map/all_to_all | solution.py:25
  45.0 2.5 %all-gather.1 = bf16[16,16,14,128]{3,1,2,0:T(8,128)(2,1)S(1)} all-gather(bf16[8,16,14,128]{3,1,2,0:T(8,128)(2,1)S(1)} %all-to-all-done.1), channel_id=3, replica_groups=mesh['rows'=2,'hidden_0'=2,'hidden_1'=4,'latents_0'=16,'latents_1'=2] {'..., dimensions={0}, use_global_device_ids=true | all-gather | bytes 1376256 | tf_op jit(solution)/shard_map/all_gather | solution.py:37
  47.4 1.3 copy.25
  48.7 0.0 copy-start.1
  48.7 0.0 copy-start.2
  48.7 1.4 reshape.82.x_ref
  50.1 0.0 copy-done.1
  50.1 0.0 copy-done.2
  50.2 0.4 shard_map.112
  50.6 1.8 all-gather.2
  52.4 0.4 convolution_convert_fusion
  52.9 14.2 %all_to_all.56 = bf16[8,224,128]{2,1,0:T(8,128)(2,1)S(1)} all-to-all(bf16[8,224,128]{2,1,0:T(8,128)(2,1)S(1)} %dynamic-slice_bitcast_fusion), channel_id=1, replica_groups=mesh['rows'=2,'hidden_0'=2,'hidden_1'=4,'latents_0'=16,'latents_1'=2] {'..., dimensions={0} | all-to-all | bytes 917504 | tf_op jit(solution)/shard_map/all_to_all | solution.py:25
  67.1 0.1 reduce_sum.65
  67.2 0.0 copy-start.6
  67.2 0.1 copy.26
  67.3 15.8 %all_to_all.57 = bf16[16,8,224]{2,1,0:T(8,128)(2,1)S(1)} all-to-all(bf16[16,8,224]{2,1,0:T(8,128)(2,1)S(1)} %bitcast.67), channel_id=1, replica_groups=mesh['rows'=2,'hidden_0'=2,'hidden_1'=4,'latents_0'=16,'latents_1'=2] {'..., dimensions={0} | all-to-all | bytes 114688 | tf_op jit(solution)/shard_map/all_to_all | solution.py:25
  83.1 18.5 %all_to_all.58 = bf16[32,8,224]{2,1,0:T(8,128)(2,1)S(1)} all-to-all(bf16[32,8,224]{2,1,0:T(8,128)(2,1)S(1)} %broadcast_in_dim.26), channel_id=1, replica_groups=mesh['rows'=2,'hidden_0'=2,'hidden_1'=4,'latents_0'=16,'latents_1'=2] {'..., dimensions={0} | all-to-all | bytes 229376 | tf_op jit(solution)/shard_map/all_to_all | solution.py:25
  101.6 0.1 copy.27
  101.7 2.0 all_gather.40
  103.6 0.2 fusion.7
  103.8 0.3 convolution_convert_fusion.6
  104.1 0.3 convolution_convert_fusion.7
  104.4 0.0 copy-done.6
  104.4 0.5 convolution_convert_fusion.4
  104.9 0.0 copy-start.4
  104.9 15.1 %all_to_all.59 = bf16[8,32,1024]{2,1,0:T(8,128)(2,1)S(1)} all-to-all(bf16[8,32,1024]{2,1,0:T(8,128)(2,1)S(1)} %bitcast.61), channel_id=1, replica_groups=mesh['rows'=2,'hidden_0'=2,'hidden_1'=4,'latents_0'=16,'latents_1'=2] {'..., dimensions={0} | all-to-all | bytes 1048576 | tf_op jit(solution)/shard_map/all_to_all | solution.py:25
  120.0 0.1 convert_reduce_fusion.1
  120.1 0.0 copy-done.4
  120.1 0.1 fusion.2
  120.2 0.1 broadcast_in_dim.27
  120.3 13.4 %all_to_all.60 = bf16[8,32,1024]{2,1,0:T(8,128)(2,1)S(1)} all-to-all(bf16[8,32,1024]{2,1,0:T(8,128)(2,1)S(1)} %broadcast_in_dim.27), channel_id=1, replica_groups=mesh['rows'=2,'hidden_0'=2,'hidden_1'=4,'latents_0'=16,'latents_1'=2] {'..., dimensions={0} | all-to-all | bytes 1048576 | tf_op jit(solution)/shard_map/all_to_all | solution.py:25
  133.7 0.0 copy-done
  133.7 0.4 fusion
  134.1 2.1 %all-gather.3 = bf16[896,256]{1,0:T(8,128)(2,1)S(1)} all-gather(bf16[448,256]{1,0:T(8,128)(2,1)S(1)} %fusion), channel_id=5, replica_groups=mesh['rows'=2,'hidden_0'=2,'hidden_1'=4,'latents_0'=16,'latents_1'=2] {'..., dimensions={0}, use_global_device_ids=true | all-gather | bytes 688128 | tf_op jit(solution)/shard_map/all_gather | solution.py:37
  136.3 0.1 copy.28
  136.4 20.4 %all_to_all.61 = bf16[32,8,224]{2,1,0:T(8,128)(2,1)S(1)} all-to-all(bf16[32,8,224]{2,1,0:T(8,128)(2,1)S(1)} %bitcast.64), channel_id=1, replica_groups=mesh['rows'=2,'hidden_0'=2,'hidden_1'=4,'latents_0'=16,'latents_1'=2] {'..., dimensions={0} | all-to-all | bytes 229376 | tf_op jit(solution)/shard_map/all_to_all | solution.py:25
  156.9 19.2 %all_to_all.62 = bf16[32,8,224]{2,1,0:T(8,128)(2,1)S(1)} all-to-all(bf16[32,8,224]{2,1,0:T(8,128)(2,1)S(1)} %broadcast_in_dim.28), channel_id=1, replica_groups=mesh['rows'=2,'hidden_0'=2,'hidden_1'=4,'latents_0'=16,'latents_1'=2] {'..., dimensions={0} | all-to-all | bytes 229376 | tf_op jit(solution)/shard_map/all_to_all | solution.py:25
  176.1 0.1 copy.31
  176.2 2.0 all_gather.44
  178.2 0.5 convolution_convert_fusion.3
  178.6 14.6 %all_to_all.63 = bf16[8,32,1024]{2,1,0:T(8,128)(2,1)S(1)} all-to-all(bf16[8,32,1024]{2,1,0:T(8,128)(2,1)S(1)} %bitcast.62), channel_id=1, replica_groups=mesh['rows'=2,'hidden_0'=2,'hidden_1'=4,'latents_0'=16,'latents_1'=2] {'..., dimensions={0} | all-to-all | bytes 1048576 | tf_op jit(solution)/shard_map/all_to_all | solution.py:25
  193.2 0.1 convert_reduce_fusion
  193.3 0.1 multiply_convert_fusion
  193.4 0.9 broadcast_in_dim.29
  194.2 5.5 %all-to-all-start.10 = ((bf16[8,32,1024]{2,1,0:T(8,128)(2,1)}), bf16[8,32,1024]{2,1,0:T(8,128)(2,1)S(1)}, u32[]{:S(2)}, u32[]{:S(2)}) async-start(bf16[8,32,1024]{2,1,0:T(8,128)(2,1)} %broadcast_in_dim.29), calls=%async_computation.10 | async-start | bytes 1048576 | tf_op jit(solution)/shard_map/all_to_all | solution.py:25
  199.8 1.8 all_gather.43
  201.6 0.7 reshape.91
  202.3 1.3 convolution_convert_fusion.1
  203.6 5.6 %all-to-all-done.10 = bf16[8,32,1024]{2,1,0:T(8,128)(2,1)S(1)} async-done(((bf16[8,32,1024]{2,1,0:T(8,128)(2,1)}), bf16[8,32,1024]{2,1,0:T(8,128)(2,1)S(1)}, u32[]{:S(2)}, u32[]{:S(2)}) %all-to-all-start.10) | async-done | bytes 524320 | tf_op jit(solution)/shard_map/all_to_all | solution.py:25
  209.2 1.3 convolution_convert_fusion.2
  (13 shorter events, 0.2 us)
Async XLA Ops:
  0.6 133.1 %copy-start = (bf16[1024,448]{0,1:T(8,128)(2,1)S(1)}, bf16[1024,448]{0,1:T(8,128)(2,1)}, u32[]{:S(2)}) copy-start(bf16[1024,448]{0,1:T(8,128)(2,1)} %param.14) | copy-start | bytes 2752516
  0.6 36.8 %copy-start.7 = (s32[256]{0:T(256)S(1)}, s32[256]{0:T(256)}, u32[]{:S(2)}) copy-start(s32[256]{0:T(256)} %param.17) | copy-start | bytes 3076
  0.7 36.9 %copy-start.5 = (f32[448]{0:T(512)S(1)}, f32[448]{0:T(512)}, u32[]{:S(2)}) copy-start(f32[448]{0:T(512)} %param.16) | copy-start | bytes 5380
  0.7 36.9 %copy-start.3 = (bf16[56,3584]{1,0:T(8,128)(2,1)S(1)}, bf16[56,3584]{1,0:T(8,128)(2,1)}, u32[]{:S(2)}) copy-start(bf16[56,3584]{1,0:T(8,128)(2,1)} %param.12) | copy-start | bytes 1204228
  30.0 14.9 %all-to-all-start.1 = ((bf16[8,16,14,128]{3,1,2,0:T(8,128)(2,1)}), bf16[8,16,14,128]{3,1,2,0:T(8,128)(2,1)S(1)}, u32[]{:S(2)}, u32[]{:S(2)}) async-start(bf16[8,16,14,128]{3,1,2,0:T(8,128)(2,1)} %broadcast_in_dim.25), calls=%async_computation.1 | async-start | bytes 917504 | tf_op jit(solution)/shard_map/all_to_all | solution.py:25
  48.7 1.5 copy-start.1
  48.7 1.5 copy-start.2
  67.2 37.3 %copy-start.6 = (bf16[448,1024]{1,0:T(8,128)(2,1)S(1)}, bf16[448,1024]{1,0:T(8,128)(2,1)}, u32[]{:S(2)}) copy-start(bf16[448,1024]{1,0:T(8,128)(2,1)} %param.13) | copy-start | bytes 2752516
  104.9 15.2 %copy-start.4 = (f32[1024]{0:T(1024)S(1)}, f32[1024]{0:T(1024)}, u32[]{:S(2)}) copy-start(f32[1024]{0:T(1024)} %param.15) | copy-start | bytes 12292
  194.2 15.0 %all-to-all-start.10 = ((bf16[8,32,1024]{2,1,0:T(8,128)(2,1)}), bf16[8,32,1024]{2,1,0:T(8,128)(2,1)S(1)}, u32[]{:S(2)}, u32[]{:S(2)}) async-start(bf16[8,32,1024]{2,1,0:T(8,128)(2,1)} %broadcast_in_dim.29), calls=%async_computation.10 | async-start | bytes 1048576 | tf_op jit(solution)/shard_map/all_to_all | solution.py:25

commit v10 on v8

--- a/solution.py
+++ b/solution.py
@@ -3,6 +3,8 @@
 import jax
 import jax.numpy as jnp
 from jax import lax
+from jax.experimental import pallas as pl
+from jax.experimental.pallas import tpu as pltpu
 from jax.sharding import Mesh
 from jax.sharding import PartitionSpec as P
 
@@ -47,6 +49,37 @@
     return lax.dynamic_index_in_dim(x, index, dim, keepdims=False)
 
 
+def gate_kernel(gate_ref, x_ref, gate_act_ref):
+    gate_act_ref[...] = jnp.dot(gate_ref[...], x_ref[...], preferred_element_type=F32)
+
+
+def up_kernel(up_ref, x_ref, gate_act_ref, hidden_ref):
+    up_act = jnp.dot(up_ref[...], x_ref[...], preferred_element_type=F32)
+    hidden_ref[...] = (jax.nn.gelu(gate_act_ref[...], approximate=True) * up_act).astype(BF16)
+
+
+def in_vmem(kernel, out_type, weight, x, *rest):
+    units, width = weight.shape
+    count = x.shape[1]
+    whole = pl.BlockSpec(memory_space=pltpu.VMEM)
+    return pl.pallas_call(
+        kernel,
+        in_specs=[whole] * (2 + len(rest)),
+        out_specs=whole,
+        out_shape=jax.ShapeDtypeStruct((units, count), out_type),
+        compiler_params=pltpu.CompilerParams(vmem_limit_bytes=16 * 2**20),
+        cost_estimate=pl.CostEstimate(
+            flops=2 * units * width * count,
+            bytes_accessed=2 * width * (units + count),
+            transcendentals=units * count,
+        ),
+    )(weight, x, *rest)
+
+
+def gated(gate, up, x):
+    return in_vmem(up_kernel, BF16, up, x, in_vmem(gate_kernel, F32, gate, x))
+
+
 def shards(
     inputs, gate_weight, up_weight, down_weight, encoder, decoder, enc_bias, dec_bias, shuffle_order
 ):
@@ -65,18 +98,16 @@
         copies_of(few, HIDDEN), gate_weight, up_weight, down_weight, shuffle_order, dec_bias
     )
     more = exchange(copies, HIDDEN)
-    weights = jnp.concatenate([gate_own.T, up_own.T], axis=0)
     down_pair = both_cores(down_own).reshape(2 * units, -1)
     count = tokens // n_rows_z
     order_own = lax.dynamic_slice_in_dim(order, lax.axis_index(ROWS_Z) * count, count, 0)
     bias_mine = lax.dynamic_slice_in_dim(out_bias, core * half, half, 0)
-    more, weights, down_pair, order_own, bias_mine = tied(
-        more, weights, down_pair, order_own, bias_mine
+    more, gate_own, up_own, down_pair, order_own, bias_mine = tied(
+        more, gate_own, up_own, down_pair, order_own, bias_mine
     )
     every = both_cores(more)
     gathered = every.transpose(1, 2, 0, 3, 4).reshape(-1, inputs.shape[0])
-    acts = jnp.dot(weights, gathered, preferred_element_type=F32)
-    hidden = (jax.nn.gelu(acts[:units], approximate=True) * acts[units:]).astype(BF16)
+    hidden = gated(gate_own.T, up_own.T, gathered)
     hidden_pair = both_cores(hidden).reshape(2 * units, -1)
     mine = lax.dot_general(
         down_pair, hidden_pair, (((0,), (0,)), ((), ())), preferred_element_type=F32

time: 214 us -> 213 us (level)
  blocking collectives: 146 us -> 174 us
  starting transfers between devices: 28.3 us -> 12.9 us
  waiting for transfers between devices: 22.2 us -> 10.4 us
    all_to_all x8 -> x9, blocking collectives: 131 us -> 159 us  [exchange(): return lax.all_to_all(blocks, axes, 0, 0, tiled=True)]
    all_to_all x3 -> x2, starting transfers between devices: 28.3 us -> 12.9 us  [exchange(): return lax.all_to_all(blocks, axes, 0, 0, tiled=True)]
    all_to_all x3 -> x2, waiting for transfers between devices: 22.2 us -> 10.4 us  [exchange(): return lax.all_to_all(blocks, axes, 0, 0, tiled=True)]
  transfers between devices with their start and end apart: 3 -> 2, of which waited for: 3 -> 2; matrix products, arithmetic and copies ran while one was open for 1% -> 1% of each run, Pallas kernels for 0% -> 0%
where the time goes in v10:
time: 213 us; the launch traced here: 210 us
  blocking collectives  174 us (82%)
  starting transfers between devices  12.9 us (6%)
  waiting for transfers between devices  10.4 us (5%)
  matrix products  5.24 us (2%)
  local copies, waits for them, and re-layouts  5.19 us (2%)
    all_to_all x9, blocking collectives, exchange(): return lax.all_to_all(blocks, axes, 0, 0, tiled=True)  159 us
    all_gather x7, blocking collectives, both_cores(): return lax.all_gather(x, C, axis=0, tiled=False)  14.6 us
    all_to_all x2, starting transfers between devices, exchange(): return lax.all_to_all(blocks, axes, 0, 0, tiled=True)  12.9 us
    all_to_all x2, waiting for transfers between devices, exchange(): return lax.all_to_all(blocks, axes, 0, 0, tiled=True)  10.4 us
  transfers between devices with their start and end apart: 2, of which 2 were waited for; matrix products, arithmetic and copies ran while one was open for 1% of the time, Pallas kernels for 0%

profile of v10, /device:TPU:6, one launch (start us, length us, event | category | flops | bytes accessed | tf_op | source)
XLA Modules:
  0.0 209.6 jit_solution(11466852955516819220)
XLA Ops:
  0.6 0.0 copy-start
  0.6 0.0 copy-start.8
  0.7 0.0 copy-start.6
  0.7 0.0 copy-start.4
  0.7 0.8 broadcast_in_dim.24
  1.5 27.7 %all_to_all.55 = bf16[16,14,128]{2,1,0:T(8,128)(2,1)S(1)} all-to-all(bf16[16,14,128]{2,1,0:T(8,128)(2,1)S(1)} %broadcast_in_dim.24), channel_id=1, replica_groups=mesh['rows'=2,'hidden_0'=2,'hidden_1'=4,'latents_0'=16,'latents_1'=2] {'..., dimensions={0} | all-to-all | bytes 114688 | tf_op jit(solution)/shard_map/all_to_all | solution.py:25
  29.2 0.8 broadcast_in_dim.25
  30.0 7.4 %all-to-all-start.1 = ((bf16[8,16,14,128]{3,1,2,0:T(8,128)(2,1)}), bf16[8,16,14,128]{3,1,2,0:T(8,128)(2,1)S(1)}, u32[]{:S(2)}, u32[]{:S(2)}) async-start(bf16[8,16,14,128]{3,1,2,0:T(8,128)(2,1)} %broadcast_in_dim.25), calls=%async_computation.1 | async-start | bytes 917504 | tf_op jit(solution)/shard_map/all_to_all | solution.py:25
  37.4 0.0 copy-done.8
  37.5 0.1 dynamic_slice.22
  37.5 0.0 copy-done.6
  37.5 0.1 dynamic_slice.23
  37.6 0.0 copy-done.4
  37.6 2.5 %all-gather = bf16[112,3584]{1,0:T(8,128)(2,1)} all-gather(bf16[56,3584]{1,0:T(8,128)(2,1)S(1)} %copy-done.4), channel_id=2, replica_groups=mesh['rows'=2,'hidden_0'=2,'hidden_1'=4,'latents_0'=16,'latents_1'=2] {'..., dimensions={0}, use_global_device_ids=true | all-gather | bytes 1204224 | tf_op jit(solution)/shard_map/all_gather | solution.py:37
  40.1 4.9 %all-to-all-done.1 = bf16[8,16,14,128]{3,1,2,0:T(8,128)(2,1)S(1)} async-done(((bf16[8,16,14,128]{3,1,2,0:T(8,128)(2,1)}), bf16[8,16,14,128]{3,1,2,0:T(8,128)(2,1)S(1)}, u32[]{:S(2)}, u32[]{:S(2)}) %all-to-all-start.1) | async-done | bytes 458784 | tf_op jit(solution)/shard_map/all_to_all | solution.py:25
  45.0 2.5 %all-gather.1 = bf16[16,16,14,128]{3,1,2,0:T(8,128)(2,1)S(1)} all-gather(bf16[8,16,14,128]{3,1,2,0:T(8,128)(2,1)S(1)} %all-to-all-done.1), channel_id=3, replica_groups=mesh['rows'=2,'hidden_0'=2,'hidden_1'=4,'latents_0'=16,'latents_1'=2] {'..., dimensions={0}, use_global_device_ids=true | all-gather | bytes 1376256 | tf_op jit(solution)/shard_map/all_gather | solution.py:37
  47.4 0.3 copy.25
  47.7 0.0 copy-start.1
  47.7 0.3 reshape.82.x_ref
  48.0 0.0 copy-start.2
  48.0 0.7 copy-done.1
  48.7 0.3 shard_map.112.gate_act_ref
  49.0 0.0 copy-done.2
  49.0 0.3 shard_map.113
  49.3 1.8 all-gather.2
  51.1 0.0 copy-done.3
  51.1 0.4 convolution_convert_fusion
  51.6 14.2 %all_to_all.56 = bf16[8,224,128]{2,1,0:T(8,128)(2,1)S(1)} all-to-all(bf16[8,224,128]{2,1,0:T(8,128)(2,1)S(1)} %dynamic-slice_bitcast_fusion), channel_id=1, replica_groups=mesh['rows'=2,'hidden_0'=2,'hidden_1'=4,'latents_0'=16,'latents_1'=2] {'..., dimensions={0} | all-to-all | bytes 917504 | tf_op jit(solution)/shard_map/all_to_all | solution.py:25
  65.8 0.1 reduce_sum.65
  65.9 0.0 copy-start.7
  65.9 0.1 copy.26
  66.0 15.8 %all_to_all.57 = bf16[16,8,224]{2,1,0:T(8,128)(2,1)S(1)} all-to-all(bf16[16,8,224]{2,1,0:T(8,128)(2,1)S(1)} %bitcast.67), channel_id=1, replica_groups=mesh['rows'=2,'hidden_0'=2,'hidden_1'=4,'latents_0'=16,'latents_1'=2] {'..., dimensions={0} | all-to-all | bytes 114688 | tf_op jit(solution)/shard_map/all_to_all | solution.py:25
  81.8 18.5 %all_to_all.58 = bf16[32,8,224]{2,1,0:T(8,128)(2,1)S(1)} all-to-all(bf16[32,8,224]{2,1,0:T(8,128)(2,1)S(1)} %broadcast_in_dim.26), channel_id=1, replica_groups=mesh['rows'=2,'hidden_0'=2,'hidden_1'=4,'latents_0'=16,'latents_1'=2] {'..., dimensions={0} | all-to-all | bytes 229376 | tf_op jit(solution)/shard_map/all_to_all | solution.py:25
  100.3 0.1 copy.27
  100.4 2.0 all_gather.40
  102.4 0.2 fusion.7
  102.5 0.3 convolution_convert_fusion.6
  102.8 0.3 convolution_convert_fusion.7
  103.1 0.0 copy-done.7
  103.1 0.5 convolution_convert_fusion.4
  103.6 0.0 copy-start.5
  103.6 15.1 %all_to_all.59 = bf16[8,32,1024]{2,1,0:T(8,128)(2,1)S(1)} all-to-all(bf16[8,32,1024]{2,1,0:T(8,128)(2,1)S(1)} %bitcast.61), channel_id=1, replica_groups=mesh['rows'=2,'hidden_0'=2,'hidden_1'=4,'latents_0'=16,'latents_1'=2] {'..., dimensions={0} | all-to-all | bytes 1048576 | tf_op jit(solution)/shard_map/all_to_all | solution.py:25
  118.8 0.1 convert_reduce_fusion.1
  118.8 0.1 fusion.2
  118.9 0.1 broadcast_in_dim.27
  119.0 13.7 %all_to_all.60 = bf16[8,32,1024]{2,1,0:T(8,128)(2,1)S(1)} all-to-all(bf16[8,32,1024]{2,1,0:T(8,128)(2,1)S(1)} %broadcast_in_dim.27), channel_id=1, replica_groups=mesh['rows'=2,'hidden_0'=2,'hidden_1'=4,'latents_0'=16,'latents_1'=2] {'..., dimensions={0} | all-to-all | bytes 1048576 | tf_op jit(solution)/shard_map/all_to_all | solution.py:25
  132.7 0.4 fusion
  133.2 2.1 %all-gather.3 = bf16[896,256]{1,0:T(8,128)(2,1)S(1)} all-gather(bf16[448,256]{1,0:T(8,128)(2,1)S(1)} %fusion), channel_id=5, replica_groups=mesh['rows'=2,'hidden_0'=2,'hidden_1'=4,'latents_0'=16,'latents_1'=2] {'..., dimensions={0}, use_global_device_ids=true | all-gather | bytes 688128 | tf_op jit(solution)/shard_map/all_gather | solution.py:37
  135.4 0.1 copy.28
  135.5 20.4 %all_to_all.61 = bf16[32,8,224]{2,1,0:T(8,128)(2,1)S(1)} all-to-all(bf16[32,8,224]{2,1,0:T(8,128)(2,1)S(1)} %bitcast.64), channel_id=1, replica_groups=mesh['rows'=2,'hidden_0'=2,'hidden_1'=4,'latents_0'=16,'latents_1'=2] {'..., dimensions={0} | all-to-all | bytes 229376 | tf_op jit(solution)/shard_map/all_to_all | solution.py:25
  155.9 19.2 %all_to_all.62 = bf16[32,8,224]{2,1,0:T(8,128)(2,1)S(1)} all-to-all(bf16[32,8,224]{2,1,0:T(8,128)(2,1)S(1)} %broadcast_in_dim.28), channel_id=1, replica_groups=mesh['rows'=2,'hidden_0'=2,'hidden_1'=4,'latents_0'=16,'latents_1'=2] {'..., dimensions={0} | all-to-all | bytes 229376 | tf_op jit(solution)/shard_map/all_to_all | solution.py:25
  175.1 0.1 copy.31
  175.2 2.0 all_gather.44
  177.2 0.5 convolution_convert_fusion.3
  177.7 14.6 %all_to_all.63 = bf16[8,32,1024]{2,1,0:T(8,128)(2,1)S(1)} all-to-all(bf16[8,32,1024]{2,1,0:T(8,128)(2,1)S(1)} %bitcast.62), channel_id=1, replica_groups=mesh['rows'=2,'hidden_0'=2,'hidden_1'=4,'latents_0'=16,'latents_1'=2] {'..., dimensions={0} | all-to-all | bytes 1048576 | tf_op jit(solution)/shard_map/all_to_all | solution.py:25
  192.3 0.1 convert_reduce_fusion
  192.3 0.1 multiply_convert_fusion
  192.4 0.9 broadcast_in_dim.29
  193.3 5.5 %all-to-all-start.10 = ((bf16[8,32,1024]{2,1,0:T(8,128)(2,1)}), bf16[8,32,1024]{2,1,0:T(8,128)(2,1)S(1)}, u32[]{:S(2)}, u32[]{:S(2)}) async-start(bf16[8,32,1024]{2,1,0:T(8,128)(2,1)} %broadcast_in_dim.29), calls=%async_computation.10 | async-start | bytes 1048576 | tf_op jit(solution)/shard_map/all_to_all | solution.py:25
  198.8 1.8 all_gather.43
  200.6 0.7 reshape.91
  201.3 1.3 convolution_convert_fusion.1
  202.6 5.6 %all-to-all-done.10 = bf16[8,32,1024]{2,1,0:T(8,128)(2,1)S(1)} async-done(((bf16[8,32,1024]{2,1,0:T(8,128)(2,1)}), bf16[8,32,1024]{2,1,0:T(8,128)(2,1)S(1)}, u32[]{:S(2)}, u32[]{:S(2)}) %all-to-all-start.10) | async-done | bytes 524320 | tf_op jit(solution)/shard_map/all_to_all | solution.py:25
  208.2 1.3 convolution_convert_fusion.2
  (16 shorter events, 0.2 us)
Async XLA Ops:
  0.6 132.1 %copy-start = (bf16[1024,448]{0,1:T(8,128)(2,1)S(1)}, bf16[1024,448]{0,1:T(8,128)(2,1)}, u32[]{:S(2)}) copy-start(bf16[1024,448]{0,1:T(8,128)(2,1)} %param.14) | copy-start | bytes 2752516
  0.6 36.8 %copy-start.8 = (s32[256]{0:T(256)S(1)}, s32[256]{0:T(256)}, u32[]{:S(2)}) copy-start(s32[256]{0:T(256)} %param.17) | copy-start | bytes 3076
  0.7 36.9 %copy-start.6 = (f32[448]{0:T(512)S(1)}, f32[448]{0:T(512)}, u32[]{:S(2)}) copy-start(f32[448]{0:T(512)} %param.16) | copy-start | bytes 5380
  0.7 36.9 %copy-start.4 = (bf16[56,3584]{1,0:T(8,128)(2,1)S(1)}, bf16[56,3584]{1,0:T(8,128)(2,1)}, u32[]{:S(2)}) copy-start(bf16[56,3584]{1,0:T(8,128)(2,1)} %param.12) | copy-start | bytes 1204228
  30.0 14.9 %all-to-all-start.1 = ((bf16[8,16,14,128]{3,1,2,0:T(8,128)(2,1)}), bf16[8,16,14,128]{3,1,2,0:T(8,128)(2,1)S(1)}, u32[]{:S(2)}, u32[]{:S(2)}) async-start(bf16[8,16,14,128]{3,1,2,0:T(8,128)(2,1)} %broadcast_in_dim.25), calls=%async_computation.1 | async-start | bytes 917504 | tf_op jit(solution)/shard_map/all_to_all | solution.py:25
  47.7 1.0 copy-start.1
  48.0 1.0 copy-start.2
  48.7 2.4 %copy-start.3 = (bf16[112,3584]{1,0:T(8,128)(2,1)S(1)}, bf16[112,3584]{1,0:T(8,128)(2,1)}, u32[]{:S(2)}) copy-start(bf16[112,3584]{1,0:T(8,128)(2,1)} %all-gather) | copy-start | bytes 2408452
  65.9 37.3 %copy-start.7 = (bf16[448,1024]{1,0:T(8,128)(2,1)S(1)}, bf16[448,1024]{1,0:T(8,128)(2,1)}, u32[]{:S(2)}) copy-start(bf16[448,1024]{1,0:T(8,128)(2,1)} %param.13) | copy-start | bytes 2752516
  103.6 15.2 %copy-start.5 = (f32[1024]{0:T(1024)S(1)}, f32[1024]{0:T(1024)}, u32[]{:S(2)}) copy-start(f32[1024]{0:T(1024)} %param.15) | copy-start | bytes 12292
  193.3 15.0 %all-to-all-start.10 = ((bf16[8,32,1024]{2,1,0:T(8,128)(2,1)}), bf16[8,32,1024]{2,1,0:T(8,128)(2,1)S(1)}, u32[]{:S(2)}, u32[]{:S(2)}) async-start(bf16[8,32,1024]{2,1,0:T(8,128)(2,1)} %broadcast_in_dim.29), calls=%async_computation.10 | async-start | bytes 1048576 | tf_op jit(solution)/shard_map/all_to_all | solution.py:25

commit v11 on v10

--- a/solution.py
+++ b/solution.py
@@ -10,6 +10,7 @@
 
 R, Y, X, Z, C = "rows", "hidden_0", "hidden_1", "latents_0", "latents_1"
 HIDDEN = (Y, X)
+HIDDEN_X_FIRST = (X, Y)
 LATENTS = (Z, C)
 HIDDEN_LATENTS = (Y, X, Z, C)
 ROWS_LATENTS = (R, Z, C)
@@ -130,9 +131,9 @@
         axis=1,
     )
     pre_local = jnp.dot(shuffled, encoder, preferred_element_type=F32).astype(BF16)
-    pre_act = total(exchange(pre_local.reshape(n_hidden, -1, latents), HIDDEN)) + enc_bias[None, :]
+    pre_act = total(exchange(pre_local.reshape(n_hidden, -1, latents), HIDDEN_X_FIRST)) + enc_bias[None, :]
     latent_own = (smooth_scale * jax.nn.softplus(pre_act / smooth_scale)).astype(BF16)
-    latent_act = sent_to_all(latent_own, HIDDEN).reshape(tokens, latents)
+    latent_act = sent_to_all(latent_own, HIDDEN_X_FIRST).reshape(tokens, latents)
     recon_local = lax.dot_general(
         decoder, latent_act, (((0,), (1,)), ((), ())), preferred_element_type=F32
     ).astype(BF16)
@@ -146,14 +147,14 @@
     back_local = lax.dot_general(
         d_err, decoder, (((1,), (1,)), ((), ())), preferred_element_type=F32
     ).astype(BF16)
-    d_latent = total(exchange(back_local.reshape(n_hidden, -1, latents), HIDDEN))
+    d_latent = total(exchange(back_local.reshape(n_hidden, -1, latents), HIDDEN_X_FIRST))
     grad_dec = lax.dot_general(
         latent_act, d_err, (((0,), (0,)), ((), ())), preferred_element_type=F32
     ).astype(BF16)
     d_pre_own = (
         (d_latent + sparsity_weight * scale) * jax.nn.sigmoid(pre_act / smooth_scale)
     ).astype(BF16)
-    d_pre = sent_to_all(d_pre_own, HIDDEN).reshape(tokens, latents)
+    d_pre = sent_to_all(d_pre_own, HIDDEN_X_FIRST).reshape(tokens, latents)
     grad_enc = lax.dot_general(
         shuffled, d_pre, (((0,), (0,)), ((), ())), preferred_element_type=F32
     ).astype(BF16)

time: 213 us -> 209 us (0.981); the launches traced: 210 us -> 208 us
  no operation moved by 1% of the time
where the time goes in v11:
time: 209 us; the launch traced here: 208 us
  blocking collectives  173 us (83%)
  starting transfers between devices  13.1 us (6%)
  waiting for transfers between devices  9.21 us (4%)
  matrix products  5.23 us (3%)
  local copies, waits for them, and re-layouts  5.19 us (2%)
    all_to_all x9, blocking collectives, exchange(): return lax.all_to_all(blocks, axes, 0, 0, tiled=True)  158 us
    all_gather x7, blocking collectives, both_cores(): return lax.all_gather(x, C, axis=0, tiled=False)  14.6 us
    all_to_all x2, starting transfers between devices, exchange(): return lax.all_to_all(blocks, axes, 0, 0, tiled=True)  13.1 us
    all_to_all x2, waiting for transfers between devices, exchange(): return lax.all_to_all(blocks, axes, 0, 0, tiled=True)  9.21 us
  transfers between devices with their start and end apart: 2, of which 2 were waited for; matrix products, arithmetic and copies ran while one was open for 1% of the time, Pallas kernels for 0%

profile of v11, /device:TPU:6, one launch (start us, length us, event | category | flops | bytes accessed | tf_op | source)
XLA Modules:
  0.0 207.7 jit_solution(5121071203003409560)
XLA Ops:
  0.6 0.0 copy-start
  0.6 0.0 copy-start.8
  0.7 0.0 copy-start.6
  0.7 0.0 copy-start.4
  0.7 0.8 broadcast_in_dim.24
  1.5 27.7 %all_to_all.55 = bf16[16,14,128]{2,1,0:T(8,128)(2,1)S(1)} all-to-all(bf16[16,14,128]{2,1,0:T(8,128)(2,1)S(1)} %broadcast_in_dim.24), channel_id=1, replica_groups=mesh['rows'=2,'hidden_0'=2,'hidden_1'=4,'latents_0'=16,'latents_1'=2] {'..., dimensions={0} | all-to-all | bytes 114688 | tf_op jit(solution)/shard_map/all_to_all | solution.py:26
  29.2 0.8 broadcast_in_dim.25
  30.0 7.4 %all-to-all-start.1 = ((bf16[8,16,14,128]{3,1,2,0:T(8,128)(2,1)}), bf16[8,16,14,128]{3,1,2,0:T(8,128)(2,1)S(1)}, u32[]{:S(2)}, u32[]{:S(2)}) async-start(bf16[8,16,14,128]{3,1,2,0:T(8,128)(2,1)} %broadcast_in_dim.25), calls=%async_computation.1 | async-start | bytes 917504 | tf_op jit(solution)/shard_map/all_to_all | solution.py:26
  37.4 0.0 copy-done.8
  37.5 0.1 dynamic_slice.22
  37.5 0.0 copy-done.6
  37.5 0.1 dynamic_slice.23
  37.6 0.0 copy-done.4
  37.6 2.5 %all-gather = bf16[112,3584]{1,0:T(8,128)(2,1)} all-gather(bf16[56,3584]{1,0:T(8,128)(2,1)S(1)} %copy-done.4), channel_id=2, replica_groups=mesh['rows'=2,'hidden_0'=2,'hidden_1'=4,'latents_0'=16,'latents_1'=2] {'..., dimensions={0}, use_global_device_ids=true | all-gather | bytes 1204224 | tf_op jit(solution)/shard_map/all_gather | solution.py:38
  40.1 4.9 %all-to-all-done.1 = bf16[8,16,14,128]{3,1,2,0:T(8,128)(2,1)S(1)} async-done(((bf16[8,16,14,128]{3,1,2,0:T(8,128)(2,1)}), bf16[8,16,14,128]{3,1,2,0:T(8,128)(2,1)S(1)}, u32[]{:S(2)}, u32[]{:S(2)}) %all-to-all-start.1) | async-done | bytes 458784 | tf_op jit(solution)/shard_map/all_to_all | solution.py:26
  45.0 2.5 %all-gather.1 = bf16[16,16,14,128]{3,1,2,0:T(8,128)(2,1)S(1)} all-gather(bf16[8,16,14,128]{3,1,2,0:T(8,128)(2,1)S(1)} %all-to-all-done.1), channel_id=3, replica_groups=mesh['rows'=2,'hidden_0'=2,'hidden_1'=4,'latents_0'=16,'latents_1'=2] {'..., dimensions={0}, use_global_device_ids=true | all-gather | bytes 1376256 | tf_op jit(solution)/shard_map/all_gather | solution.py:38
  47.4 0.3 copy.25
  47.7 0.0 copy-start.1
  47.7 0.3 reshape.82.x_ref
  48.0 0.0 copy-start.2
  48.0 0.7 copy-done.1
  48.7 0.3 shard_map.112.gate_act_ref
  49.0 0.0 copy-done.2
  49.0 0.3 shard_map.113
  49.3 1.8 all-gather.2
  51.1 0.0 copy-done.3
  51.1 0.4 convolution_convert_fusion
  51.6 14.2 %all_to_all.56 = bf16[8,224,128]{2,1,0:T(8,128)(2,1)S(1)} all-to-all(bf16[8,224,128]{2,1,0:T(8,128)(2,1)S(1)} %dynamic-slice_bitcast_fusion), channel_id=1, replica_groups=mesh['rows'=2,'hidden_0'=2,'hidden_1'=4,'latents_0'=16,'latents_1'=2] {'..., dimensions={0} | all-to-all | bytes 917504 | tf_op jit(solution)/shard_map/all_to_all | solution.py:26
  65.8 0.1 reduce_sum.65
  65.9 0.0 copy-start.7
  65.9 0.1 copy.26
  66.0 15.8 %all_to_all.57 = bf16[16,8,224]{2,1,0:T(8,128)(2,1)S(1)} all-to-all(bf16[16,8,224]{2,1,0:T(8,128)(2,1)S(1)} %bitcast.67), channel_id=1, replica_groups=mesh['rows'=2,'hidden_0'=2,'hidden_1'=4,'latents_0'=16,'latents_1'=2] {'..., dimensions={0} | all-to-all | bytes 114688 | tf_op jit(solution)/shard_map/all_to_all | solution.py:26
  81.8 18.5 %all_to_all.58 = bf16[32,8,224]{2,1,0:T(8,128)(2,1)S(1)} all-to-all(bf16[32,8,224]{2,1,0:T(8,128)(2,1)S(1)} %broadcast_in_dim.26), channel_id=1, replica_groups=mesh['rows'=2,'hidden_0'=2,'hidden_1'=4,'latents_0'=16,'latents_1'=2] {'..., dimensions={0} | all-to-all | bytes 229376 | tf_op jit(solution)/shard_map/all_to_all | solution.py:26
  100.3 0.1 copy.27
  100.4 2.0 all_gather.40
  102.4 0.2 fusion.7
  102.5 0.3 convolution_convert_fusion.6
  102.8 0.3 convolution_convert_fusion.7
  103.1 0.0 copy-done.7
  103.1 0.5 convolution_convert_fusion.4
  103.6 0.0 copy-start.5
  103.6 14.7 %all_to_all.59 = bf16[8,32,1024]{2,1,0:T(8,128)(2,1)S(1)} all-to-all(bf16[8,32,1024]{2,1,0:T(8,128)(2,1)S(1)} %bitcast.61), channel_id=1, replica_groups=mesh['rows'=2,'hidden_0'=2,'hidden_1'=4,'latents_0'=16,'latents_1'=2] {'..., dimensions={0} | all-to-all | bytes 1048576 | tf_op jit(solution)/shard_map/all_to_all | solution.py:26
  118.3 0.1 convert_reduce_fusion.1
  118.4 0.1 fusion.2
  118.5 0.1 broadcast_in_dim.27
  118.6 13.7 %all_to_all.60 = bf16[8,32,1024]{2,1,0:T(8,128)(2,1)S(1)} all-to-all(bf16[8,32,1024]{2,1,0:T(8,128)(2,1)S(1)} %broadcast_in_dim.27), channel_id=1, replica_groups=mesh['rows'=2,'hidden_0'=2,'hidden_1'=4,'latents_0'=16,'latents_1'=2] {'..., dimensions={0} | all-to-all | bytes 1048576 | tf_op jit(solution)/shard_map/all_to_all | solution.py:26
  132.3 0.4 fusion
  132.7 2.1 %all-gather.3 = bf16[896,256]{1,0:T(8,128)(2,1)S(1)} all-gather(bf16[448,256]{1,0:T(8,128)(2,1)S(1)} %fusion), channel_id=5, replica_groups=mesh['rows'=2,'hidden_0'=2,'hidden_1'=4,'latents_0'=16,'latents_1'=2] {'..., dimensions={0}, use_global_device_ids=true | all-gather | bytes 688128 | tf_op jit(solution)/shard_map/all_gather | solution.py:38
  134.9 0.1 copy.28
  135.0 20.4 %all_to_all.61 = bf16[32,8,224]{2,1,0:T(8,128)(2,1)S(1)} all-to-all(bf16[32,8,224]{2,1,0:T(8,128)(2,1)S(1)} %bitcast.64), channel_id=1, replica_groups=mesh['rows'=2,'hidden_0'=2,'hidden_1'=4,'latents_0'=16,'latents_1'=2] {'..., dimensions={0} | all-to-all | bytes 229376 | tf_op jit(solution)/shard_map/all_to_all | solution.py:26
  155.5 19.2 %all_to_all.62 = bf16[32,8,224]{2,1,0:T(8,128)(2,1)S(1)} all-to-all(bf16[32,8,224]{2,1,0:T(8,128)(2,1)S(1)} %broadcast_in_dim.28), channel_id=1, replica_groups=mesh['rows'=2,'hidden_0'=2,'hidden_1'=4,'latents_0'=16,'latents_1'=2] {'..., dimensions={0} | all-to-all | bytes 229376 | tf_op jit(solution)/shard_map/all_to_all | solution.py:26
  174.6 0.1 copy.31
  174.7 2.0 all_gather.44
  176.7 0.5 convolution_convert_fusion.3
  177.2 14.3 %all_to_all.63 = bf16[8,32,1024]{2,1,0:T(8,128)(2,1)S(1)} all-to-all(bf16[8,32,1024]{2,1,0:T(8,128)(2,1)S(1)} %bitcast.62), channel_id=1, replica_groups=mesh['rows'=2,'hidden_0'=2,'hidden_1'=4,'latents_0'=16,'latents_1'=2] {'..., dimensions={0} | all-to-all | bytes 1048576 | tf_op jit(solution)/shard_map/all_to_all | solution.py:26
  191.5 0.1 convert_reduce_fusion
  191.6 0.1 multiply_convert_fusion
  191.7 0.9 broadcast_in_dim.29
  192.5 5.7 %all-to-all-start.10 = ((bf16[8,32,1024]{2,1,0:T(8,128)(2,1)}), bf16[8,32,1024]{2,1,0:T(8,128)(2,1)S(1)}, u32[]{:S(2)}, u32[]{:S(2)}) async-start(bf16[8,32,1024]{2,1,0:T(8,128)(2,1)} %broadcast_in_dim.29), calls=%async_computation.10 | async-start | bytes 1048576 | tf_op jit(solution)/shard_map/all_to_all | solution.py:26
  198.2 1.8 all_gather.43
  200.0 0.7 reshape.91
  200.7 1.3 convolution_convert_fusion.1
  202.0 4.4 %all-to-all-done.10 = bf16[8,32,1024]{2,1,0:T(8,128)(2,1)S(1)} async-done(((bf16[8,32,1024]{2,1,0:T(8,128)(2,1)}), bf16[8,32,1024]{2,1,0:T(8,128)(2,1)S(1)}, u32[]{:S(2)}, u32[]{:S(2)}) %all-to-all-start.10) | async-done | bytes 524320 | tf_op jit(solution)/shard_map/all_to_all | solution.py:26
  206.4 1.3 convolution_convert_fusion.2
  (16 shorter events, 0.2 us)
Async XLA Ops:
  0.6 131.6 %copy-start = (bf16[1024,448]{0,1:T(8,128)(2,1)S(1)}, bf16[1024,448]{0,1:T(8,128)(2,1)}, u32[]{:S(2)}) copy-start(bf16[1024,448]{0,1:T(8,128)(2,1)} %param.14) | copy-start | bytes 2752516
  0.6 36.8 %copy-start.8 = (s32[256]{0:T(256)S(1)}, s32[256]{0:T(256)}, u32[]{:S(2)}) copy-start(s32[256]{0:T(256)} %param.17) | copy-start | bytes 3076
  0.7 36.9 %copy-start.6 = (f32[448]{0:T(512)S(1)}, f32[448]{0:T(512)}, u32[]{:S(2)}) copy-start(f32[448]{0:T(512)} %param.16) | copy-start | bytes 5380
  0.7 36.9 %copy-start.4 = (bf16[56,3584]{1,0:T(8,128)(2,1)S(1)}, bf16[56,3584]{1,0:T(8,128)(2,1)}, u32[]{:S(2)}) copy-start(bf16[56,3584]{1,0:T(8,128)(2,1)} %param.12) | copy-start | bytes 1204228
  30.0 14.9 %all-to-all-start.1 = ((bf16[8,16,14,128]{3,1,2,0:T(8,128)(2,1)}), bf16[8,16,14,128]{3,1,2,0:T(8,128)(2,1)S(1)}, u32[]{:S(2)}, u32[]{:S(2)}) async-start(bf16[8,16,14,128]{3,1,2,0:T(8,128)(2,1)} %broadcast_in_dim.25), calls=%async_computation.1 | async-start | bytes 917504 | tf_op jit(solution)/shard_map/all_to_all | solution.py:26
  47.7 1.0 copy-start.1
  48.0 1.0 copy-start.2
  48.7 2.4 %copy-start.3 = (bf16[112,3584]{1,0:T(8,128)(2,1)S(1)}, bf16[112,3584]{1,0:T(8,128)(2,1)}, u32[]{:S(2)}) copy-start(bf16[112,3584]{1,0:T(8,128)(2,1)} %all-gather) | copy-start | bytes 2408452
  65.9 37.3 %copy-start.7 = (bf16[448,1024]{1,0:T(8,128)(2,1)S(1)}, bf16[448,1024]{1,0:T(8,128)(2,1)}, u32[]{:S(2)}) copy-start(bf16[448,1024]{1,0:T(8,128)(2,1)} %param.13) | copy-start | bytes 2752516
  103.6 14.8 %copy-start.5 = (f32[1024]{0:T(1024)S(1)}, f32[1024]{0:T(1024)}, u32[]{:S(2)}) copy-start(f32[1024]{0:T(1024)} %param.15) | copy-start | bytes 12292
  192.5 13.8 %all-to-all-start.10 = ((bf16[8,32,1024]{2,1,0:T(8,128)(2,1)}), bf16[8,32,1024]{2,1,0:T(8,128)(2,1)S(1)}, u32[]{:S(2)}, u32[]{:S(2)}) async-start(bf16[8,32,1024]{2,1,0:T(8,128)(2,1)} %broadcast_in_dim.29), calls=%async_computation.10 | async-start | bytes 1048576 | tf_op jit(solution)/shard_map/all_to_all | solution.py:26

commit v12 on v11

--- a/solution.py
+++ b/solution.py
@@ -8,13 +8,16 @@
 from jax.sharding import Mesh
 from jax.sharding import PartitionSpec as P
 
-R, Y, X, Z, C = "rows", "hidden_0", "hidden_1", "latents_0", "latents_1"
+R, Y, X, C = "rows", "hidden_0", "hidden_1", "core"
+Z_FAR, Z_NEAR = "latents_0", "latents_1"
+Z = (Z_FAR, Z_NEAR)
 HIDDEN = (Y, X)
 HIDDEN_X_FIRST = (X, Y)
-LATENTS = (Z, C)
-HIDDEN_LATENTS = (Y, X, Z, C)
-ROWS_LATENTS = (R, Z, C)
-ROWS_Z = (R, Z)
+LATENTS = (Z_FAR, Z_NEAR, C)
+HIDDEN_LATENTS = HIDDEN + LATENTS
+ROWS_LATENTS = (R,) + LATENTS
+ROWS_Z = (R,) + Z
+NEAR_FIRST = (Z_NEAR, R, Z_FAR)
 
 smooth_scale = 0.1
 sparsity_weight = 0.5
@@ -40,6 +43,11 @@
 
 def tied(*arrays):
     return lax.optimization_barrier(arrays)
+
+
+def near_first(x, count):
+    far, near = lax.axis_size(Z_FAR), lax.axis_size(Z_NEAR)
+    return x.reshape(-1, far, near, count).transpose(2, 0, 1, 3).reshape(-1)
 
 
 def total(blocks):
@@ -96,36 +104,42 @@
 
     few = sent_to_all(inputs.T, Z)
     copies, gate_own, up_own, down_own, order, out_bias = tied(
-        copies_of(few, HIDDEN), gate_weight, up_weight, down_weight, shuffle_order, dec_bias
-    )
-    more = exchange(copies, HIDDEN)
+        copies_of(few, HIDDEN_X_FIRST), gate_weight, up_weight, down_weight, shuffle_order, dec_bias
+    )
+    more = exchange(copies, HIDDEN_X_FIRST)
     down_pair = both_cores(down_own).reshape(2 * units, -1)
     count = tokens // n_rows_z
     order_own = lax.dynamic_slice_in_dim(order, lax.axis_index(ROWS_Z) * count, count, 0)
+    order = near_first(order, count)
     bias_mine = lax.dynamic_slice_in_dim(out_bias, core * half, half, 0)
-    more, gate_own, up_own, down_pair, order_own, bias_mine = tied(
-        more, gate_own, up_own, down_pair, order_own, bias_mine
+    more, gate_own, up_own, down_pair, order, order_own, bias_mine = tied(
+        more, gate_own, up_own, down_pair, order, order_own, bias_mine
     )
     every = both_cores(more)
-    gathered = every.transpose(1, 2, 0, 3, 4).reshape(-1, inputs.shape[0])
+    n_x = lax.axis_size(X)
+    blocks = every.reshape(2, n_x, n_hidden // n_x, *every.shape[2:])
+    gathered = blocks.transpose(2, 1, 3, 0, 4, 5).reshape(-1, inputs.shape[0])
     hidden = gated(gate_own.T, up_own.T, gathered)
     hidden_pair = both_cores(hidden).reshape(2 * units, -1)
     mine = lax.dot_general(
         down_pair, hidden_pair, (((0,), (0,)), ((), ())), preferred_element_type=F32
     ).astype(BF16)
-    mine = own(mine.reshape(n_hidden, 2, half, -1), core, 1)
-
-    summed = total(exchange(mine, HIDDEN)).T.astype(BF16)
+    mine = own(mine.reshape(-1, n_x, 2, half, inputs.shape[0]), core, 2)
+    mine = mine.transpose(1, 0, 2, 3).reshape(n_hidden, half, -1)
+
+    summed = total(exchange(mine, HIDDEN_X_FIRST)).T.astype(BF16)
     rows_own = total(exchange(summed.reshape(n_z, -1, half), Z)).astype(BF16)
-    mlp_out = both_cores(sent_to_all(rows_own, ROWS_Z).reshape(tokens, half))
+    mlp_out = both_cores(sent_to_all(rows_own, NEAR_FIRST).reshape(tokens, half))
+
+    held = near_first(jnp.arange(tokens), count)
 
     def picked(order):
-        return (order[:, None] == jnp.arange(tokens)[None, :]).astype(BF16)
+        return (order[:, None] == held[None, :]).astype(BF16)
 
     scale = 1.0 / math.sqrt(tokens)
     target = jnp.dot(picked(order_own), own(mlp_out, core, 0), preferred_element_type=F32)
     mlp_out, target = tied(mlp_out, target)
-    pick = picked(shuffle_order)
+    pick = picked(order)
     shuffled = jnp.concatenate(
         [jnp.dot(pick, mlp_out[c], preferred_element_type=F32).astype(BF16) for c in range(2)],
         axis=1,
@@ -139,9 +153,9 @@
     ).astype(BF16)
     recon_pair = both_cores(recon_local).reshape(2, 2, half, tokens)
     recon_mine = total(own(recon_pair, core, 1)).T.astype(BF16).reshape(n_rows_z, -1, half)
-    recon = total(exchange(recon_mine, ROWS_Z)) + bias_mine[None, :]
+    recon = total(exchange(recon_mine, NEAR_FIRST)) + bias_mine[None, :]
     err_own = (scale * (recon - target)).astype(BF16)
-    err_pair = both_cores(sent_to_all(err_own, ROWS_Z).reshape(tokens, half))
+    err_pair = both_cores(sent_to_all(err_own, NEAR_FIRST).reshape(tokens, half))
     d_err = jnp.concatenate([err_pair[0], err_pair[1]], axis=1)
 
     back_local = lax.dot_general(
@@ -165,8 +179,8 @@
 
 def solution(mesh):
     finer = Mesh(
-        mesh.devices.reshape(mesh.shape["rows"], 2, 4, 16, 2),
-        (R, Y, X, Z, C),
+        mesh.devices.reshape(mesh.shape["rows"], 2, 4, 8, 2, 2),
+        (R, Y, X, Z_FAR, Z_NEAR, C),
     )
     return jax.shard_map(
         shards,

time: 209 us -> 208 us (level)
  blocking collectives: 173 us -> 153 us
  waiting for transfers between devices: 9.21 us -> 23.2 us
  starting transfers between devices: 13.1 us -> 16.9 us
    all_to_all x9 -> x8, blocking collectives: 158 us -> 138 us  [exchange(): return lax.all_to_all(blocks, axes, 0, 0, tiled=True)]
    all_to_all x2 -> x3, waiting for transfers between devices: 9.21 us -> 23.2 us  [exchange(): return lax.all_to_all(blocks, axes, 0, 0, tiled=True)]
    all_to_all x2 -> x3, starting transfers between devices: 13.1 us -> 16.9 us  [exchange(): return lax.all_to_all(blocks, axes, 0, 0, tiled=True)]
  transfers between devices with their start and end apart: 2 -> 3, of which waited for: 2 -> 3; matrix products, arithmetic and copies ran while one was open for 1% -> 1% of each run, Pallas kernels for 0% -> 0%
where the time goes in v12:
time: 208 us; the launch traced here: 206 us
  blocking collectives  153 us (74%)
  waiting for transfers between devices  23.2 us (11%)
  starting transfers between devices  16.9 us (8%)
  local copies, waits for them, and re-layouts  6.15 us (3%)
  matrix products  5.22 us (3%)
    all_to_all x8, blocking collectives, exchange(): return lax.all_to_all(blocks, axes, 0, 0, tiled=True)  138 us
    all_to_all x3, waiting for transfers between devices, exchange(): return lax.all_to_all(blocks, axes, 0, 0, tiled=True)  23.2 us
    all_to_all x3, starting transfers between devices, exchange(): return lax.all_to_all(blocks, axes, 0, 0, tiled=True)  16.9 us
    all_gather x7, blocking collectives, both_cores(): return lax.all_gather(x, C, axis=0, tiled=False)  14.6 us
  transfers between devices with their start and end apart: 3, of which 3 were waited for; matrix products, arithmetic and copies ran while one was open for 1% of the time, Pallas kernels for 0%

profile of v12, /device:TPU:6, one launch (start us, length us, event | category | flops | bytes accessed | tf_op | source)
XLA Modules:
  0.0 206.2 jit_solution(2261203581792872808)
XLA Ops:
  0.6 0.0 copy-start
  0.6 0.0 copy-start.4
  0.7 0.0 copy-start.7
  0.7 0.0 copy-start.6
  0.7 0.8 broadcast_in_dim.22
  1.5 27.7 %all_to_all.55 = bf16[16,14,128]{2,1,0:T(8,128)(2,1)S(1)} all-to-all(bf16[16,14,128]{2,1,0:T(8,128)(2,1)S(1)} %broadcast_in_dim.22), channel_id=1, replica_groups=mesh['rows'=2,'hidden_0'=2,'hidden_1'=4,'latents_0'=8,'latents_1'=2,'cor..., dimensions={0} | all-to-all | bytes 114688 | tf_op jit(solution)/shard_map/all_to_all | solution.py:29
  29.2 0.8 broadcast_in_dim.23
  30.0 7.4 %all-to-all-start.1 = ((bf16[8,16,14,128]{3,1,2,0:T(8,128)(2,1)}), bf16[8,16,14,128]{3,1,2,0:T(8,128)(2,1)S(1)}, u32[]{:S(2)}, u32[]{:S(2)}) async-start(bf16[8,16,14,128]{3,1,2,0:T(8,128)(2,1)} %broadcast_in_dim.23), calls=%async_computation.1 | async-start | bytes 917504 | tf_op jit(solution)/shard_map/all_to_all | solution.py:29
  37.5 0.1 reshape.168
  37.6 0.1 dynamic_slice.22
  37.6 0.1 reshape.169
  37.7 0.1 dynamic_slice.23
  37.8 2.5 %all-gather = bf16[112,3584]{1,0:T(8,128)(2,1)} all-gather(bf16[56,3584]{1,0:T(8,128)(2,1)S(1)} %copy-done.4), channel_id=2, replica_groups=mesh['rows'=2,'hidden_0'=2,'hidden_1'=4,'latents_0'=8,'latents_1'=2,'cor..., dimensions={0}, use_global_device_ids=true | all-gather | bytes 1204224 | tf_op jit(solution)/shard_map/all_gather | solution.py:41
  40.3 4.6 %all-to-all-done.1 = bf16[8,16,14,128]{3,1,2,0:T(8,128)(2,1)S(1)} async-done(((bf16[8,16,14,128]{3,1,2,0:T(8,128)(2,1)}), bf16[8,16,14,128]{3,1,2,0:T(8,128)(2,1)S(1)}, u32[]{:S(2)}, u32[]{:S(2)}) %all-to-all-start.1) | async-done | bytes 458784 | tf_op jit(solution)/shard_map/all_to_all | solution.py:29
  45.0 2.5 %all-gather.1 = bf16[16,16,14,128]{3,1,2,0:T(8,128)(2,1)S(1)} all-gather(bf16[8,16,14,128]{3,1,2,0:T(8,128)(2,1)S(1)} %all-to-all-done.1), channel_id=3, replica_groups=mesh['rows'=2,'hidden_0'=2,'hidden_1'=4,'latents_0'=8,'latents_1'=2,'cor..., dimensions={0}, use_global_device_ids=true | all-gather | bytes 1376256 | tf_op jit(solution)/shard_map/all_gather | solution.py:41
  47.4 0.3 copy.31
  47.7 0.0 copy-start.1
  47.7 0.3 reshape.181.x_ref
  48.0 0.0 copy-start.2
  48.0 0.7 copy-done.1
  48.7 0.3 shard_map.112.gate_act_ref
  49.0 0.0 copy-done.2
  49.0 0.3 shard_map.113
  49.3 1.8 all-gather.2
  51.1 0.4 convolution_convert_fusion
  51.6 13.7 %all_to_all.56 = bf16[8,224,128]{2,1,0:T(8,128)(2,1)S(1)} all-to-all(bf16[8,224,128]{2,1,0:T(8,128)(2,1)S(1)} %bitcast.68), channel_id=1, replica_groups=mesh['rows'=2,'hidden_0'=2,'hidden_1'=4,'latents_0'=8,'latents_1'=2,'cor..., dimensions={0} | all-to-all | bytes 917504 | tf_op jit(solution)/shard_map/all_to_all | solution.py:29
  65.4 0.1 reduce_sum.65
  65.4 0.0 copy-start.8
  65.4 0.1 copy.33
  65.5 15.9 %all_to_all.57 = bf16[16,8,224]{2,1,0:T(8,128)(2,1)S(1)} all-to-all(bf16[16,8,224]{2,1,0:T(8,128)(2,1)S(1)} %bitcast.76), channel_id=1, replica_groups=mesh['rows'=2,'hidden_0'=2,'hidden_1'=4,'latents_0'=8,'latents_1'=2,'cor..., dimensions={0} | all-to-all | bytes 114688 | tf_op jit(solution)/shard_map/all_to_all | solution.py:29
  81.4 0.7 broadcast_in_dim.24
  82.1 3.9 %all-to-all-start.4 = ((bf16[32,8,224]{2,1,0:T(8,128)(2,1)}), bf16[32,8,224]{2,1,0:T(8,128)(2,1)S(1)}, u32[]{:S(2)}, u32[]{:S(2)}) async-start(bf16[32,8,224]{2,1,0:T(8,128)(2,1)} %broadcast_in_dim.24), calls=%async_computation.4 | async-start | bytes 262144 | tf_op jit(solution)/shard_map/all_to_all | solution.py:29
  86.0 0.1 reshape.179
  86.1 14.2 %all-to-all-done.4 = bf16[32,8,224]{2,1,0:T(8,128)(2,1)S(1)} async-done(((bf16[32,8,224]{2,1,0:T(8,128)(2,1)}), bf16[32,8,224]{2,1,0:T(8,128)(2,1)S(1)}, u32[]{:S(2)}, u32[]{:S(2)}) %all-to-all-start.4) | async-done | bytes 114720 | tf_op jit(solution)/shard_map/all_to_all | solution.py:29
  100.3 0.1 copy.34
  100.4 2.0 all_gather.40
  102.3 0.2 fusion.11
  102.5 0.3 convolution_convert_fusion.7
  102.8 0.3 convolution_convert_fusion.6
  103.1 0.5 convolution_convert_fusion.4
  103.6 0.0 copy-start.5
  103.6 14.3 %all_to_all.58 = bf16[8,32,1024]{2,1,0:T(8,128)(2,1)S(1)} all-to-all(bf16[8,32,1024]{2,1,0:T(8,128)(2,1)S(1)} %bitcast.70), channel_id=1, replica_groups=mesh['rows'=2,'hidden_0'=2,'hidden_1'=4,'latents_0'=8,'latents_1'=2,'cor..., dimensions={0} | all-to-all | bytes 1048576 | tf_op jit(solution)/shard_map/all_to_all | solution.py:29
  117.9 0.1 convert_reduce_fusion.1
  118.0 0.1 fusion.4
  118.1 0.1 broadcast_in_dim.25
  118.1 13.7 %all_to_all.59 = bf16[8,32,1024]{2,1,0:T(8,128)(2,1)S(1)} all-to-all(bf16[8,32,1024]{2,1,0:T(8,128)(2,1)S(1)} %broadcast_in_dim.25), channel_id=1, replica_groups=mesh['rows'=2,'hidden_0'=2,'hidden_1'=4,'latents_0'=8,'latents_1'=2,'cor..., dimensions={0} | all-to-all | bytes 1048576 | tf_op jit(solution)/shard_map/all_to_all | solution.py:29
  131.9 0.4 fusion
  132.3 2.1 %all-gather.3 = bf16[896,256]{1,0:T(8,128)(2,1)S(1)} all-gather(bf16[448,256]{1,0:T(8,128)(2,1)S(1)} %fusion), channel_id=5, replica_groups=mesh['rows'=2,'hidden_0'=2,'hidden_1'=4,'latents_0'=8,'latents_1'=2,'cor..., dimensions={0}, use_global_device_ids=true | all-gather | bytes 688128 | tf_op jit(solution)/shard_map/all_gather | solution.py:41
  134.5 0.1 copy.35
  134.6 19.1 %all_to_all.60 = bf16[32,8,224]{2,1,0:T(8,128)(2,1)S(1)} all-to-all(bf16[32,8,224]{2,1,0:T(8,128)(2,1)S(1)} %bitcast.73), channel_id=1, replica_groups=mesh['rows'=2,'hidden_0'=2,'hidden_1'=4,'latents_0'=8,'latents_1'=2,'cor..., dimensions={0} | all-to-all | bytes 229376 | tf_op jit(solution)/shard_map/all_to_all | solution.py:29
  153.8 19.0 %all_to_all.61 = bf16[32,8,224]{2,1,0:T(8,128)(2,1)S(1)} all-to-all(bf16[32,8,224]{2,1,0:T(8,128)(2,1)S(1)} %broadcast_in_dim.26), channel_id=1, replica_groups=mesh['rows'=2,'hidden_0'=2,'hidden_1'=4,'latents_0'=8,'latents_1'=2,'cor..., dimensions={0} | all-to-all | bytes 229376 | tf_op jit(solution)/shard_map/all_to_all | solution.py:29
  172.7 0.1 copy.38
  172.8 2.0 all_gather.44
  174.8 0.5 convolution_convert_fusion.3
  175.3 14.7 %all_to_all.62 = bf16[8,32,1024]{2,1,0:T(8,128)(2,1)S(1)} all-to-all(bf16[8,32,1024]{2,1,0:T(8,128)(2,1)S(1)} %bitcast.71), channel_id=1, replica_groups=mesh['rows'=2,'hidden_0'=2,'hidden_1'=4,'latents_0'=8,'latents_1'=2,'cor..., dimensions={0} | all-to-all | bytes 1048576 | tf_op jit(solution)/shard_map/all_to_all | solution.py:29
  190.0 0.1 convert_reduce_fusion
  190.1 0.1 multiply_convert_fusion
  190.1 0.9 broadcast_in_dim.27
  191.0 5.7 %all-to-all-start.10 = ((bf16[8,32,1024]{2,1,0:T(8,128)(2,1)}), bf16[8,32,1024]{2,1,0:T(8,128)(2,1)S(1)}, u32[]{:S(2)}, u32[]{:S(2)}) async-start(bf16[8,32,1024]{2,1,0:T(8,128)(2,1)} %broadcast_in_dim.27), calls=%async_computation.10 | async-start | bytes 1048576 | tf_op jit(solution)/shard_map/all_to_all | solution.py:29
  196.7 1.8 all_gather.43
  198.5 0.7 reshape.191
  199.2 1.3 convolution_convert_fusion.1
  200.5 4.4 %all-to-all-done.10 = bf16[8,32,1024]{2,1,0:T(8,128)(2,1)S(1)} async-done(((bf16[8,32,1024]{2,1,0:T(8,128)(2,1)}), bf16[8,32,1024]{2,1,0:T(8,128)(2,1)S(1)}, u32[]{:S(2)}, u32[]{:S(2)}) %all-to-all-start.10) | async-done | bytes 524320 | tf_op jit(solution)/shard_map/all_to_all | solution.py:29
  204.8 1.3 convolution_convert_fusion.2
  (23 shorter events, 0.3 us)
Async XLA Ops:
  0.6 131.2 %copy-start = (bf16[1024,448]{0,1:T(8,128)(2,1)S(1)}, bf16[1024,448]{0,1:T(8,128)(2,1)}, u32[]{:S(2)}) copy-start(bf16[1024,448]{0,1:T(8,128)(2,1)} %param.14) | copy-start | bytes 2752516
  0.6 37.2 %copy-start.4 = (bf16[56,3584]{1,0:T(8,128)(2,1)S(1)}, bf16[56,3584]{1,0:T(8,128)(2,1)}, u32[]{:S(2)}) copy-start(bf16[56,3584]{1,0:T(8,128)(2,1)} %param.12) | copy-start | bytes 1204228
  0.7 37.1 %copy-start.7 = (f32[448]{0:T(512)S(1)}, f32[448]{0:T(512)}, u32[]{:S(2)}) copy-start(f32[448]{0:T(512)} %param.16) | copy-start | bytes 5380
  0.7 36.8 %copy-start.6 = (s32[256]{0:T(256)S(1)}, s32[256]{0:T(256)}, u32[]{:S(2)}) copy-start(s32[256]{0:T(256)} %param.17) | copy-start | bytes 3076
  30.0 14.9 %all-to-all-start.1 = ((bf16[8,16,14,128]{3,1,2,0:T(8,128)(2,1)}), bf16[8,16,14,128]{3,1,2,0:T(8,128)(2,1)S(1)}, u32[]{:S(2)}, u32[]{:S(2)}) async-start(bf16[8,16,14,128]{3,1,2,0:T(8,128)(2,1)} %broadcast_in_dim.23), calls=%async_computation.1 | async-start | bytes 917504 | tf_op jit(solution)/shard_map/all_to_all | solution.py:29
  47.7 1.0 copy-start.1
  48.0 1.0 copy-start.2
  48.7 2.4 %copy-start.3 = (bf16[112,3584]{1,0:T(8,128)(2,1)S(1)}, bf16[112,3584]{1,0:T(8,128)(2,1)}, u32[]{:S(2)}) copy-start(bf16[112,3584]{1,0:T(8,128)(2,1)} %all-gather) | copy-start | bytes 2408452
  65.4 37.7 %copy-start.8 = (bf16[448,1024]{1,0:T(8,128)(2,1)S(1)}, bf16[448,1024]{1,0:T(8,128)(2,1)}, u32[]{:S(2)}) copy-start(bf16[448,1024]{1,0:T(8,128)(2,1)} %param.13) | copy-start | bytes 2752516
  82.1 18.1 %all-to-all-start.4 = ((bf16[32,8,224]{2,1,0:T(8,128)(2,1)}), bf16[32,8,224]{2,1,0:T(8,128)(2,1)S(1)}, u32[]{:S(2)}, u32[]{:S(2)}) async-start(bf16[32,8,224]{2,1,0:T(8,128)(2,1)} %broadcast_in_dim.24), calls=%async_computation.4 | async-start | bytes 262144 | tf_op jit(solution)/shard_map/all_to_all | solution.py:29
  103.6 14.4 %copy-start.5 = (f32[1024]{0:T(1024)S(1)}, f32[1024]{0:T(1024)}, u32[]{:S(2)}) copy-start(f32[1024]{0:T(1024)} %param.15) | copy-start | bytes 12292
  191.0 13.8 %all-to-all-start.10 = ((bf16[8,32,1024]{2,1,0:T(8,128)(2,1)}), bf16[8,32,1024]{2,1,0:T(8,128)(2,1)S(1)}, u32[]{:S(2)}, u32[]{:S(2)}) async-start(bf16[8,32,1024]{2,1,0:T(8,128)(2,1)} %broadcast_in_dim.27), calls=%async_computation.10 | async-start | bytes 1048576 | tf_op jit(solution)/shard_map/all_to_all | solution.py:29

commit v13 on v12

--- a/solution.py
+++ b/solution.py
@@ -11,6 +11,7 @@
 R, Y, X, C = "rows", "hidden_0", "hidden_1", "core"
 Z_FAR, Z_NEAR = "latents_0", "latents_1"
 Z = (Z_FAR, Z_NEAR)
+Z_NEAR_FIRST = (Z_NEAR, Z_FAR)
 HIDDEN = (Y, X)
 HIDDEN_X_FIRST = (X, Y)
 LATENTS = (Z_FAR, Z_NEAR, C)
@@ -95,6 +96,7 @@
     tokens = shuffle_order.shape[0]
     n_hidden = lax.axis_size(HIDDEN)
     n_z = lax.axis_size(Z)
+    n_far = lax.axis_size(Z_FAR)
     n_rows_z = lax.axis_size(ROWS_Z)
     core = lax.axis_index(C)
     width = decoder.shape[1]
@@ -102,7 +104,8 @@
     latents = encoder.shape[1]
     units = gate_weight.shape[1]
 
-    few = sent_to_all(inputs.T, Z)
+    few = sent_to_all(inputs.T, Z_NEAR_FIRST)
+    few = few.reshape(-1, n_far, *few.shape[1:]).swapaxes(0, 1).reshape(few.shape)
     copies, gate_own, up_own, down_own, order, out_bias = tied(
         copies_of(few, HIDDEN_X_FIRST), gate_weight, up_weight, down_weight, shuffle_order, dec_bias
     )
@@ -128,10 +131,10 @@
     mine = mine.transpose(1, 0, 2, 3).reshape(n_hidden, half, -1)
 
     summed = total(exchange(mine, HIDDEN_X_FIRST)).T.astype(BF16)
-    rows_own = total(exchange(summed.reshape(n_z, -1, half), Z)).astype(BF16)
+    rows_own = total(exchange(summed.reshape(n_z, -1, half), Z_NEAR_FIRST)).astype(BF16)
     mlp_out = both_cores(sent_to_all(rows_own, NEAR_FIRST).reshape(tokens, half))
 
-    held = near_first(jnp.arange(tokens), count)
+    held = jnp.arange(tokens).reshape(2, -1, n_far * count).swapaxes(0, 1).reshape(-1)
 
     def picked(order):
         return (order[:, None] == held[None, :]).astype(BF16)

time: 208 us -> 208 us (level)
  no operation moved by 1% of the time
where the time goes in v13:
time: 208 us; the launch traced here: 206 us
  blocking collectives  153 us (74%)
  waiting for transfers between devices  23.2 us (11%)
  starting transfers between devices  16.9 us (8%)
  local copies, waits for them, and re-layouts  6.19 us (3%)
  matrix products  5.23 us (3%)
    all_to_all x8, blocking collectives, exchange(): return lax.all_to_all(blocks, axes, 0, 0, tiled=True)  138 us
    all_to_all x3, waiting for transfers between devices, exchange(): return lax.all_to_all(blocks, axes, 0, 0, tiled=True)  23.2 us
    all_to_all x3, starting transfers between devices, exchange(): return lax.all_to_all(blocks, axes, 0, 0, tiled=True)  16.9 us
    all_gather x7, blocking collectives, both_cores(): return lax.all_gather(x, C, axis=0, tiled=False)  14.6 us
  transfers between devices with their start and end apart: 3, of which 3 were waited for; matrix products, arithmetic and copies ran while one was open for 1% of the time, Pallas kernels for 0%

profile of v13, /device:TPU:6, one launch (start us, length us, event | category | flops | bytes accessed | tf_op | source)
XLA Modules:
  0.0 206.4 jit_solution(8291313193579198172)
XLA Ops:
  0.6 0.0 copy-start
  0.6 0.0 copy-start.4
  0.7 0.8 broadcast_in_dim.22
  1.5 27.9 %all_to_all.55 = bf16[16,14,128]{2,1,0:T(8,128)(2,1)S(1)} all-to-all(bf16[16,14,128]{2,1,0:T(8,128)(2,1)S(1)} %broadcast_in_dim.22), channel_id=1, replica_groups=mesh['rows'=2,'hidden_0'=2,'hidden_1'=4,'latents_0'=8,'latents_1'=2,'cor..., dimensions={0} | all-to-all | bytes 114688 | tf_op jit(solution)/shard_map/all_to_all | solution.py:30
  29.3 0.1 copy.32
  29.4 0.8 broadcast_in_dim.23
  30.2 7.4 %all-to-all-start.1 = ((bf16[8,16,14,128]{3,1,2,0:T(8,128)(2,1)}), bf16[8,16,14,128]{3,1,2,0:T(8,128)(2,1)S(1)}, u32[]{:S(2)}, u32[]{:S(2)}) async-start(bf16[8,16,14,128]{3,1,2,0:T(8,128)(2,1)} %broadcast_in_dim.23), calls=%async_computation.1 | async-start | bytes 917504 | tf_op jit(solution)/shard_map/all_to_all | solution.py:30
  37.6 0.1 reshape.155
  37.7 0.1 dynamic_slice.22
  37.8 0.1 reshape.156
  37.9 0.1 dynamic_slice.23
  38.0 2.5 %all-gather = bf16[112,3584]{1,0:T(8,128)(2,1)} all-gather(bf16[56,3584]{1,0:T(8,128)(2,1)S(1)} %copy-done.4), channel_id=2, replica_groups=mesh['rows'=2,'hidden_0'=2,'hidden_1'=4,'latents_0'=8,'latents_1'=2,'cor..., dimensions={0}, use_global_device_ids=true | all-gather | bytes 1204224 | tf_op jit(solution)/shard_map/all_gather | solution.py:42
  40.5 4.6 %all-to-all-done.1 = bf16[8,16,14,128]{3,1,2,0:T(8,128)(2,1)S(1)} async-done(((bf16[8,16,14,128]{3,1,2,0:T(8,128)(2,1)}), bf16[8,16,14,128]{3,1,2,0:T(8,128)(2,1)S(1)}, u32[]{:S(2)}, u32[]{:S(2)}) %all-to-all-start.1) | async-done | bytes 458784 | tf_op jit(solution)/shard_map/all_to_all | solution.py:30
  45.1 2.5 %all-gather.1 = bf16[16,16,14,128]{3,1,2,0:T(8,128)(2,1)S(1)} all-gather(bf16[8,16,14,128]{3,1,2,0:T(8,128)(2,1)S(1)} %all-to-all-done.1), channel_id=3, replica_groups=mesh['rows'=2,'hidden_0'=2,'hidden_1'=4,'latents_0'=8,'latents_1'=2,'cor..., dimensions={0}, use_global_device_ids=true | all-gather | bytes 1376256 | tf_op jit(solution)/shard_map/all_gather | solution.py:42
  47.6 0.3 copy.34
  47.9 0.0 copy-start.1
  47.9 0.3 reshape.165.x_ref
  48.2 0.0 copy-start.2
  48.2 0.7 copy-done.1
  48.9 0.3 shard_map.112.gate_act_ref
  49.2 0.0 copy-done.2
  49.2 0.3 shard_map.113
  49.5 1.8 all-gather.2
  51.3 0.4 convolution_convert_fusion
  51.8 13.7 %all_to_all.56 = bf16[8,224,128]{2,1,0:T(8,128)(2,1)S(1)} all-to-all(bf16[8,224,128]{2,1,0:T(8,128)(2,1)S(1)} %bitcast.70), channel_id=1, replica_groups=mesh['rows'=2,'hidden_0'=2,'hidden_1'=4,'latents_0'=8,'latents_1'=2,'cor..., dimensions={0} | all-to-all | bytes 917504 | tf_op jit(solution)/shard_map/all_to_all | solution.py:30
  65.6 0.1 reduce_sum.65
  65.6 0.0 copy-start.8
  65.6 0.1 copy.36
  65.7 15.8 %all_to_all.57 = bf16[16,8,224]{2,1,0:T(8,128)(2,1)S(1)} all-to-all(bf16[16,8,224]{2,1,0:T(8,128)(2,1)S(1)} %bitcast.79), channel_id=1, replica_groups=mesh['rows'=2,'hidden_0'=2,'hidden_1'=4,'latents_0'=8,'latents_1'=2,'cor..., dimensions={0} | all-to-all | bytes 114688 | tf_op jit(solution)/shard_map/all_to_all | solution.py:30
  81.6 0.7 broadcast_in_dim.24
  82.3 3.9 %all-to-all-start.4 = ((bf16[32,8,224]{2,1,0:T(8,128)(2,1)}), bf16[32,8,224]{2,1,0:T(8,128)(2,1)S(1)}, u32[]{:S(2)}, u32[]{:S(2)}) async-start(bf16[32,8,224]{2,1,0:T(8,128)(2,1)} %broadcast_in_dim.24), calls=%async_computation.4 | async-start | bytes 262144 | tf_op jit(solution)/shard_map/all_to_all | solution.py:30
  86.1 0.1 reshape.163
  86.2 14.2 %all-to-all-done.4 = bf16[32,8,224]{2,1,0:T(8,128)(2,1)S(1)} async-done(((bf16[32,8,224]{2,1,0:T(8,128)(2,1)}), bf16[32,8,224]{2,1,0:T(8,128)(2,1)S(1)}, u32[]{:S(2)}, u32[]{:S(2)}) %all-to-all-start.4) | async-done | bytes 114720 | tf_op jit(solution)/shard_map/all_to_all | solution.py:30
  100.4 0.1 copy.37
  100.5 2.0 all_gather.40
  102.5 0.2 fusion.11
  102.6 0.3 convolution_convert_fusion.7
  103.0 0.3 convolution_convert_fusion.6
  103.3 0.0 copy-done.8
  103.3 0.5 convolution_convert_fusion.4
  103.7 0.0 copy-start.5
  103.7 14.2 %all_to_all.58 = bf16[8,32,1024]{2,1,0:T(8,128)(2,1)S(1)} all-to-all(bf16[8,32,1024]{2,1,0:T(8,128)(2,1)S(1)} %bitcast.72), channel_id=1, replica_groups=mesh['rows'=2,'hidden_0'=2,'hidden_1'=4,'latents_0'=8,'latents_1'=2,'cor..., dimensions={0} | all-to-all | bytes 1048576 | tf_op jit(solution)/shard_map/all_to_all | solution.py:30
  118.0 0.1 convert_reduce_fusion.1
  118.1 0.1 fusion.4
  118.2 0.1 broadcast_in_dim.25
  118.2 13.7 %all_to_all.59 = bf16[8,32,1024]{2,1,0:T(8,128)(2,1)S(1)} all-to-all(bf16[8,32,1024]{2,1,0:T(8,128)(2,1)S(1)} %broadcast_in_dim.25), channel_id=1, replica_groups=mesh['rows'=2,'hidden_0'=2,'hidden_1'=4,'latents_0'=8,'latents_1'=2,'cor..., dimensions={0} | all-to-all | bytes 1048576 | tf_op jit(solution)/shard_map/all_to_all | solution.py:30
  131.9 0.4 fusion
  132.4 2.1 %all-gather.3 = bf16[896,256]{1,0:T(8,128)(2,1)S(1)} all-gather(bf16[448,256]{1,0:T(8,128)(2,1)S(1)} %fusion), channel_id=5, replica_groups=mesh['rows'=2,'hidden_0'=2,'hidden_1'=4,'latents_0'=8,'latents_1'=2,'cor..., dimensions={0}, use_global_device_ids=true | all-gather | bytes 688128 | tf_op jit(solution)/shard_map/all_gather | solution.py:42
  134.6 0.1 copy.38
  134.7 19.2 %all_to_all.60 = bf16[32,8,224]{2,1,0:T(8,128)(2,1)S(1)} all-to-all(bf16[32,8,224]{2,1,0:T(8,128)(2,1)S(1)} %bitcast.75), channel_id=1, replica_groups=mesh['rows'=2,'hidden_0'=2,'hidden_1'=4,'latents_0'=8,'latents_1'=2,'cor..., dimensions={0} | all-to-all | bytes 229376 | tf_op jit(solution)/shard_map/all_to_all | solution.py:30
  153.9 19.0 %all_to_all.61 = bf16[32,8,224]{2,1,0:T(8,128)(2,1)S(1)} all-to-all(bf16[32,8,224]{2,1,0:T(8,128)(2,1)S(1)} %broadcast_in_dim.26), channel_id=1, replica_groups=mesh['rows'=2,'hidden_0'=2,'hidden_1'=4,'latents_0'=8,'latents_1'=2,'cor..., dimensions={0} | all-to-all | bytes 229376 | tf_op jit(solution)/shard_map/all_to_all | solution.py:30
  172.9 0.1 copy.41
  173.0 2.0 all_gather.44
  175.0 0.5 convolution_convert_fusion.3
  175.4 14.8 %all_to_all.62 = bf16[8,32,1024]{2,1,0:T(8,128)(2,1)S(1)} all-to-all(bf16[8,32,1024]{2,1,0:T(8,128)(2,1)S(1)} %bitcast.73), channel_id=1, replica_groups=mesh['rows'=2,'hidden_0'=2,'hidden_1'=4,'latents_0'=8,'latents_1'=2,'cor..., dimensions={0} | all-to-all | bytes 1048576 | tf_op jit(solution)/shard_map/all_to_all | solution.py:30
  190.3 0.1 convert_reduce_fusion
  190.4 0.1 multiply_convert_fusion
  190.4 0.9 broadcast_in_dim.27
  191.3 5.7 %all-to-all-start.10 = ((bf16[8,32,1024]{2,1,0:T(8,128)(2,1)}), bf16[8,32,1024]{2,1,0:T(8,128)(2,1)S(1)}, u32[]{:S(2)}, u32[]{:S(2)}) async-start(bf16[8,32,1024]{2,1,0:T(8,128)(2,1)} %broadcast_in_dim.27), calls=%async_computation.10 | async-start | bytes 1048576 | tf_op jit(solution)/shard_map/all_to_all | solution.py:30
  196.9 1.8 all_gather.43
  198.8 0.7 reshape.175
  199.4 1.3 convolution_convert_fusion.1
  200.8 4.4 %all-to-all-done.10 = bf16[8,32,1024]{2,1,0:T(8,128)(2,1)S(1)} async-done(((bf16[8,32,1024]{2,1,0:T(8,128)(2,1)}), bf16[8,32,1024]{2,1,0:T(8,128)(2,1)S(1)}, u32[]{:S(2)}, u32[]{:S(2)}) %all-to-all-start.10) | async-done | bytes 524320 | tf_op jit(solution)/shard_map/all_to_all | solution.py:30
  205.1 1.3 convolution_convert_fusion.2
  (23 shorter events, 0.3 us)
Async XLA Ops:
  0.6 131.3 %copy-start = (bf16[1024,448]{0,1:T(8,128)(2,1)S(1)}, bf16[1024,448]{0,1:T(8,128)(2,1)}, u32[]{:S(2)}) copy-start(bf16[1024,448]{0,1:T(8,128)(2,1)} %param.14) | copy-start | bytes 2752516
  0.6 37.4 %copy-start.4 = (bf16[56,3584]{1,0:T(8,128)(2,1)S(1)}, bf16[56,3584]{1,0:T(8,128)(2,1)}, u32[]{:S(2)}) copy-start(bf16[56,3584]{1,0:T(8,128)(2,1)} %param.12) | copy-start | bytes 1204228
  0.7 37.3 %copy-start.7 = (f32[448]{0:T(512)S(1)}, f32[448]{0:T(512)}, u32[]{:S(2)}) copy-start(f32[448]{0:T(512)} %param.16) | copy-start | bytes 5380
  0.7 37.0 %copy-start.6 = (s32[256]{0:T(256)S(1)}, s32[256]{0:T(256)}, u32[]{:S(2)}) copy-start(s32[256]{0:T(256)} %param.17) | copy-start | bytes 3076
  30.2 14.9 %all-to-all-start.1 = ((bf16[8,16,14,128]{3,1,2,0:T(8,128)(2,1)}), bf16[8,16,14,128]{3,1,2,0:T(8,128)(2,1)S(1)}, u32[]{:S(2)}, u32[]{:S(2)}) async-start(bf16[8,16,14,128]{3,1,2,0:T(8,128)(2,1)} %broadcast_in_dim.23), calls=%async_computation.1 | async-start | bytes 917504 | tf_op jit(solution)/shard_map/all_to_all | solution.py:30
  47.9 1.0 copy-start.1
  48.2 1.0 copy-start.2
  48.9 2.4 %copy-start.3 = (bf16[112,3584]{1,0:T(8,128)(2,1)S(1)}, bf16[112,3584]{1,0:T(8,128)(2,1)}, u32[]{:S(2)}) copy-start(bf16[112,3584]{1,0:T(8,128)(2,1)} %all-gather) | copy-start | bytes 2408452
  65.6 37.6 %copy-start.8 = (bf16[448,1024]{1,0:T(8,128)(2,1)S(1)}, bf16[448,1024]{1,0:T(8,128)(2,1)}, u32[]{:S(2)}) copy-start(bf16[448,1024]{1,0:T(8,128)(2,1)} %param.13) | copy-start | bytes 2752516
  82.3 18.1 %all-to-all-start.4 = ((bf16[32,8,224]{2,1,0:T(8,128)(2,1)}), bf16[32,8,224]{2,1,0:T(8,128)(2,1)S(1)}, u32[]{:S(2)}, u32[]{:S(2)}) async-start(bf16[32,8,224]{2,1,0:T(8,128)(2,1)} %broadcast_in_dim.24), calls=%async_computation.4 | async-start | bytes 262144 | tf_op jit(solution)/shard_map/all_to_all | solution.py:30
  103.7 14.3 %copy-start.5 = (f32[1024]{0:T(1024)S(1)}, f32[1024]{0:T(1024)}, u32[]{:S(2)}) copy-start(f32[1024]{0:T(1024)} %param.15) | copy-start | bytes 12292
  191.3 13.8 %all-to-all-start.10 = ((bf16[8,32,1024]{2,1,0:T(8,128)(2,1)}), bf16[8,32,1024]{2,1,0:T(8,128)(2,1)S(1)}, u32[]{:S(2)}, u32[]{:S(2)}) async-start(bf16[8,32,1024]{2,1,0:T(8,128)(2,1)} %broadcast_in_dim.27), calls=%async_computation.10 | async-start | bytes 1048576 | tf_op jit(solution)/shard_map/all_to_all | solution.py:30
